TPU v7x, 32 devices: a whole 2x2x4 slice. The times are simulated.
32 devices in a mesh: dp: 8 (over z, x), tensor: 4 (over y, core).
Axes of the slice: x: 2, y: 2, z: 4, core: 2. Of those that a mesh axis runs over, the one named last changes fastest.
Arguments:
- inputs: bfloat16 [16384, 1024], P(('dp', 'tensor')), may hold values from -6 to 6
- cotangent: bfloat16 [16384, 1024], P(('dp', 'tensor')), may hold values from -6 to 6
- lengths: int32 [8, 8], P('dp'), may hold values from 1 to 2041, as said below
- adapter_index: int32 [8], P('dp'), may hold values from 0 to 7
- w_qkv: bfloat16 [3, 1024, 1024], P(None, 'dp', 'tensor'), may hold values from -0.1875 to 0.1875
- w_out: bfloat16 [1024, 1024], P('tensor', 'dp'), may hold values from -4 to 4
- w_fc1: bfloat16 [1024, 4096], P('dp', 'tensor'), may hold values from -0.1875 to 0.1875
- w_fc2: bfloat16 [4096, 1024], P('tensor', 'dp'), may hold values from -0.09375 to 0.09375
- ln1_gain: bfloat16 [1024], P('dp'), may hold values from 0.5 to 1.5
- ln1_bias: bfloat16 [1024], P('dp'), may hold values from -2.5 to 2.5
- ln2_gain: bfloat16 [1024], P('dp'), may hold values from 0.5 to 1.5
- ln2_bias: bfloat16 [1024], P('dp'), may hold values from -2.5 to 2.5
- down_qkv: bfloat16 [3, 8, 1024, 16], P(None, None, 'dp'), may hold values from -0.1875 to 0.1875
- up_qkv: bfloat16 [3, 8, 16, 1024], P(None, None, 'dp', 'tensor'), may hold values from -0.75 to 0.75
- down_out: bfloat16 [8, 1024, 16], P(None, 'tensor', 'dp'), may hold values from -0.1875 to 0.1875
- up_out: bfloat16 [8, 16, 1024], P(None, None, 'dp'), may hold values from -0.75 to 0.75
- down_fc1: bfloat16 [8, 1024, 16], P(None, 'dp'), may hold values from -0.1875 to 0.1875
- up_fc1: bfloat16 [8, 16, 4096], P(None, 'dp', 'tensor'), may hold values from -0.75 to 0.75
- down_fc2: bfloat16 [8, 4096, 16], P(None, 'tensor', 'dp'), may hold values from -0.09375 to 0.09375
- up_fc2: bfloat16 [8, 16, 1024], P(None, None, 'dp'), may hold values from -0.75 to 0.75
Outputs:
- output: bfloat16 [16384, 1024], P(('dp', 'tensor'))
- grad_input: float32 [16384, 1024], P(('dp', 'tensor'))
- grad_down_qkv: float32 [3, 8, 1024, 16], P(None, None, ('dp', 'tensor'))
- grad_up_qkv: float32 [3, 8, 16, 1024], P(None, None, 'dp', 'tensor')
- grad_down_out: float32 [8, 1024, 16], P(None, 'tensor', 'dp')
- grad_up_out: float32 [8, 16, 1024], P(None, None, ('dp', 'tensor'))
- grad_down_fc1: float32 [8, 1024, 16], P(None, ('dp', 'tensor'))
- grad_up_fc1: float32 [8, 16, 4096], P(None, 'dp', 'tensor')
- grad_down_fc2: float32 [8, 4096, 16], P(None, 'tensor', 'dp')
- grad_up_fc2: float32 [8, 16, 1024], P(None, None, ('dp', 'tensor'))
Inputs may be any that keep to these rules, and one draw needn't show every extreme that they name: Each row holds 8 document lengths that sum to 2048.
All inputs are finite; a program needn't handle non-finite values.
Results may differ from a plain program's by a relative error of at most 0.022.
Values may be sent and summed in bfloat16 or wider, within the bound.
No kernel may reach another device: no remote copies, remote signals or barrier semaphores. Data moves between devices by JAX's collectives and lax.ppermute only.
A program may use at most 192 MiB of HBM per device.

v0:
```python
import jax
import jax.numpy as jnp
from jax import lax
from jax.sharding import PartitionSpec as P

HD = 64


NEG = -1000000000.0
EPS = 1e-05


def matmul(left, right):
    return jnp.dot(left, right, preferred_element_type=jnp.float32)


def norm_rows(values, gain, shift):
    center = values - jnp.mean(values, axis=-1, keepdims=True)
    variance = jnp.mean(center * center, axis=-1, keepdims=True)
    return center * lax.rsqrt(variance + EPS) * gain + shift


def segment_ids(doc_lengths, total):
    ends = jnp.cumsum(doc_lengths)
    places = jnp.arange(total, dtype=jnp.int32)
    return jnp.sum((places[:, None] >= ends[None, :]).astype(jnp.int32), axis=1)


def choose(set_onehot, table, axis):
    return jnp.tensordot(set_onehot, table, axes=([0], [axis]))


def spread_set(set_onehot, grad_sel, axis):
    shape = [1] * (grad_sel.ndim + 1)
    shape[axis] = set_onehot.shape[0]
    return jnp.expand_dims(grad_sel, axis) * set_onehot.astype(jnp.float32).reshape(shape)


def project_qkv(rows_all, small_all, weight, sel_up):
    main = jnp.einsum("td,jdc->jtc", rows_all, weight, preferred_element_type=jnp.float32)
    extra = jnp.einsum("tjr,jrc->jtc", small_all, sel_up, preferred_element_type=jnp.float32)
    return (main + extra).astype(jnp.bfloat16)


def gelu_exact(values):
    return jax.nn.gelu(values, approximate=False)


def feed_forward(rows_all, small_all, weight, sel_up):
    pre_gelu = matmul(rows_all, weight) + matmul(small_all, sel_up)
    return (pre_gelu, gelu_exact(pre_gelu).astype(jnp.bfloat16))


def split_heads(qkv):
    length = qkv.shape[1]
    heads = qkv.shape[2] // HD
    return (
        qkv[0].reshape(length, heads, HD),
        qkv[1].reshape(length, heads, HD),
        qkv[2].reshape(length, heads, HD),
    )


def block_scores(query_block, key_rows, query_segs, segments):
    scores = jnp.einsum(
        "qhd,khd->hqk", query_block, key_rows, preferred_element_type=jnp.float32
    ) * HD ** (-0.5)
    return jnp.where((query_segs[:, None] == segments[None, :])[None], scores, NEG)


def attend_forward(qkv, segments, block_rows):
    queries, key_rows, value_rows = split_heads(qkv)
    length, heads = (queries.shape[0], queries.shape[1])

    def advance(running, offset):
        query_block = lax.dynamic_slice_in_dim(queries, offset, block_rows, 0)
        query_segs = lax.dynamic_slice_in_dim(segments, offset, block_rows, 0)
        scores = block_scores(query_block, key_rows, query_segs, segments)
        row_max = jnp.max(scores, axis=-1, keepdims=True)
        exp_scores = jnp.exp(scores - row_max)
        row_total = jnp.sum(exp_scores, axis=-1, keepdims=True)
        prob_low = (exp_scores / row_total).astype(jnp.bfloat16)
        mixed = jnp.einsum("hqk,khd->qhd", prob_low, value_rows, preferred_element_type=jnp.float32)
        return (running, (mixed.astype(jnp.bfloat16), (row_max + jnp.log(row_total))[..., 0]))

    offsets = jnp.arange(length // block_rows, dtype=jnp.int32) * block_rows
    _, (mixed, log_total) = lax.scan(advance, jnp.zeros((), jnp.float32), offsets)
    return (mixed.reshape(length, heads * HD), log_total)


def attend_backward(qkv, log_total, grad_att, segments, block_rows):
    queries, key_rows, value_rows = split_heads(qkv)
    length, heads = (queries.shape[0], queries.shape[1])
    grad_rows = grad_att.reshape(length, heads, HD)
    scale = HD ** (-0.5)

    def advance(running, pieces):
        key_grad, value_grad = running
        offset, block_log = pieces
        query_block = lax.dynamic_slice_in_dim(queries, offset, block_rows, 0)
        grad_block = lax.dynamic_slice_in_dim(grad_rows, offset, block_rows, 0)
        query_segs = lax.dynamic_slice_in_dim(segments, offset, block_rows, 0)
        scores = block_scores(query_block, key_rows, query_segs, segments)
        attn_prob = jnp.exp(scores - block_log[:, :, None])
        prob_low = attn_prob.astype(jnp.bfloat16)
        prob_grad = jnp.einsum(
            "qhd,khd->hqk", grad_block, value_rows, preferred_element_type=jnp.float32
        )
        row_dot = jnp.sum(attn_prob * prob_grad, axis=-1, keepdims=True)
        score_grad = (attn_prob * (prob_grad - row_dot)).astype(jnp.bfloat16)
        query_grad = (
            jnp.einsum("hqk,khd->qhd", score_grad, key_rows, preferred_element_type=jnp.float32)
            * scale
        )
        key_grad = (
            key_grad
            + jnp.einsum(
                "hqk,qhd->khd", score_grad, query_block, preferred_element_type=jnp.float32
            )
            * scale
        )
        value_grad = value_grad + jnp.einsum(
            "hqk,qhd->khd", prob_low, grad_block, preferred_element_type=jnp.float32
        )
        return ((key_grad, value_grad), query_grad.astype(jnp.bfloat16))

    offsets = jnp.arange(length // block_rows, dtype=jnp.int32) * block_rows
    zeros = jnp.zeros((length, heads, HD), jnp.float32)
    (key_grad, value_grad), query_grad = lax.scan(advance, (zeros, zeros), (offsets, log_total))
    width = heads * HD
    return jnp.stack(
        [
            query_grad.reshape(length, width),
            key_grad.reshape(length, width).astype(jnp.bfloat16),
            value_grad.reshape(length, width).astype(jnp.bfloat16),
        ]
    )


def shards(
    inputs,
    cotangent,
    lengths,
    adapter_index,
    w_qkv,
    w_out,
    w_fc1,
    w_fc2,
    ln1_gain,
    ln1_bias,
    ln2_gain,
    ln2_bias,
    down_qkv,
    up_qkv,
    down_out,
    up_out,
    down_fc1,
    up_fc1,
    down_fc2,
    up_fc2,
):
    (
        w_qkv,
        w_out,
        w_fc1,
        w_fc2,
        ln1_gain,
        ln1_bias,
        ln2_gain,
        ln2_bias,
        down_qkv,
        up_qkv,
        down_out,
        up_out,
        down_fc1,
        up_fc1,
        down_fc2,
        up_fc2,
    ) = (
        lax.all_gather(w_qkv, "dp", axis=1, tiled=True),
        lax.all_gather(w_out, "dp", axis=1, tiled=True),
        lax.all_gather(w_fc1, "dp", axis=0, tiled=True),
        lax.all_gather(w_fc2, "dp", axis=1, tiled=True),
        lax.all_gather(ln1_gain, "dp", axis=0, tiled=True),
        lax.all_gather(ln1_bias, "dp", axis=0, tiled=True),
        lax.all_gather(ln2_gain, "dp", axis=0, tiled=True),
        lax.all_gather(ln2_bias, "dp", axis=0, tiled=True),
        lax.all_gather(down_qkv, "dp", axis=2, tiled=True),
        lax.all_gather(up_qkv, "dp", axis=2, tiled=True),
        lax.all_gather(down_out, "dp", axis=2, tiled=True),
        lax.all_gather(up_out, "dp", axis=2, tiled=True),
        lax.all_gather(down_fc1, "dp", axis=1, tiled=True),
        lax.all_gather(up_fc1, "dp", axis=1, tiled=True),
        lax.all_gather(down_fc2, "dp", axis=2, tiled=True),
        lax.all_gather(up_fc2, "dp", axis=2, tiled=True),
    )
    set_onehot = (jnp.arange(down_qkv.shape[1], dtype=jnp.int32) == adapter_index[0]).astype(
        jnp.bfloat16
    )
    sel_down_qkv = choose(set_onehot, down_qkv, 1)
    sel_up_qkv = choose(set_onehot, up_qkv, 1)
    sel_down_out = choose(set_onehot, down_out, 0)
    sel_up_out = choose(set_onehot, up_out, 0)
    sel_down_fc1 = choose(set_onehot, down_fc1, 0)
    sel_up_fc1 = choose(set_onehot, up_fc1, 0)
    sel_down_fc2 = choose(set_onehot, down_fc2, 0)
    sel_up_fc2 = choose(set_onehot, up_fc2, 0)
    gain_first = ln1_gain.astype(jnp.float32)
    shift_first = ln1_bias.astype(jnp.float32)
    gain_second = ln2_gain.astype(jnp.float32)
    shift_second = ln2_bias.astype(jnp.float32)
    length = inputs.shape[0] * lax.axis_size("tensor")
    block_rows = min(512, length)
    segments = segment_ids(lengths[0], length)
    u_in_shard = jnp.einsum(
        "td,jdr->tjr", inputs, sel_down_qkv, preferred_element_type=jnp.float32
    ).astype(jnp.bfloat16)
    rows_all, u_in_all = (
        lax.all_gather(inputs, "tensor", axis=0, tiled=True),
        lax.all_gather(u_in_shard, "tensor", axis=0, tiled=True),
    )
    qkv = project_qkv(rows_all, u_in_all, w_qkv, sel_up_qkv)
    att, log_total = attend_forward(qkv, segments, block_rows)
    branch_part = matmul(att, w_out)
    u_out_part = matmul(att, sel_down_out)
    branch_sum, u_out_sum = (
        lax.psum_scatter(
            branch_part.astype(jnp.bfloat16), "tensor", scatter_dimension=0, tiled=True
        ).astype(jnp.float32),
        lax.psum_scatter(
            u_out_part.astype(jnp.bfloat16), "tensor", scatter_dimension=0, tiled=True
        ).astype(jnp.float32),
    )
    u_out = u_out_sum.astype(jnp.bfloat16)
    first_sum = inputs.astype(jnp.float32) + branch_sum + matmul(u_out, sel_up_out)
    normed = norm_rows(first_sum, gain_first, shift_first)
    normed_low = normed.astype(jnp.bfloat16)
    u_fc1_shard = matmul(normed_low, sel_down_fc1).astype(jnp.bfloat16)
    normed_all, u_fc1_all = (
        lax.all_gather(normed_low, "tensor", axis=0, tiled=True),
        lax.all_gather(u_fc1_shard, "tensor", axis=0, tiled=True),
    )
    pre_gelu, hidden_act = feed_forward(normed_all, u_fc1_all, w_fc1, sel_up_fc1)
    ffn_part = matmul(hidden_act, w_fc2)
    u_fc2_part = matmul(hidden_act, sel_down_fc2)
    ffn_sum, u_fc2_sum = (
        lax.psum_scatter(
            ffn_part.astype(jnp.bfloat16), "tensor", scatter_dimension=0, tiled=True
        ).astype(jnp.float32),
        lax.psum_scatter(
            u_fc2_part.astype(jnp.bfloat16), "tensor", scatter_dimension=0, tiled=True
        ).astype(jnp.float32),
    )
    u_fc2 = u_fc2_sum.astype(jnp.bfloat16)
    second_sum = normed + ffn_sum + matmul(u_fc2, sel_up_fc2)
    output = norm_rows(second_sum, gain_second, shift_second).astype(jnp.bfloat16)
    _, second_back = jax.vjp(
        lambda value_in: norm_rows(value_in, gain_second, shift_second), second_sum
    )
    d_second = second_back(cotangent.astype(jnp.float32))[0]
    d_ffn = d_second.astype(jnp.bfloat16)
    d_u_fc2 = jnp.einsum("tc,rc->tr", d_ffn, sel_up_fc2, preferred_element_type=jnp.float32).astype(
        jnp.bfloat16
    )
    grad_up_fc2 = jnp.einsum("tr,tc->rc", u_fc2, d_ffn, preferred_element_type=jnp.float32)
    d_ffn_all, d_u_fc2_all = (
        lax.all_gather(d_ffn, "tensor", axis=0, tiled=True),
        lax.all_gather(d_u_fc2, "tensor", axis=0, tiled=True),
    )
    normed_again, u_fc1_all = (
        lax.all_gather(normed_low, "tensor", axis=0, tiled=True),
        lax.all_gather(u_fc1_shard, "tensor", axis=0, tiled=True),
    )
    pre_gelu, hidden_act = feed_forward(normed_again, u_fc1_all, w_fc1, sel_up_fc1)
    d_hidden = jnp.einsum(
        "tc,fc->tf", d_ffn_all, w_fc2, preferred_element_type=jnp.float32
    ) + jnp.einsum("tr,fr->tf", d_u_fc2_all, sel_down_fc2, preferred_element_type=jnp.float32)
    grad_down_fc2 = jnp.einsum(
        "tf,tr->fr", hidden_act, d_u_fc2_all, preferred_element_type=jnp.float32
    )
    _, gelu_back = jax.vjp(gelu_exact, pre_gelu)
    d_pre = gelu_back(d_hidden)[0].astype(jnp.bfloat16)
    d_normed_part = jnp.einsum("tf,df->td", d_pre, w_fc1, preferred_element_type=jnp.float32)
    d_u_fc1_part = jnp.einsum("tf,rf->tr", d_pre, sel_up_fc1, preferred_element_type=jnp.float32)
    grad_up_fc1 = jnp.einsum("tr,tf->rf", u_fc1_all, d_pre, preferred_element_type=jnp.float32)
    d_normed_sum, d_u_fc1_sum = (
        lax.psum_scatter(
            d_normed_part.astype(jnp.bfloat16), "tensor", scatter_dimension=0, tiled=True
        ).astype(jnp.float32),
        lax.psum_scatter(
            d_u_fc1_part.astype(jnp.bfloat16), "tensor", scatter_dimension=0, tiled=True
        ).astype(jnp.float32),
    )
    d_u_fc1 = d_u_fc1_sum.astype(jnp.bfloat16)
    d_normed = (
        d_second
        + d_normed_sum
        + jnp.einsum("tr,dr->td", d_u_fc1, sel_down_fc1, preferred_element_type=jnp.float32)
    )
    grad_down_fc1 = jnp.einsum("td,tr->dr", normed_low, d_u_fc1, preferred_element_type=jnp.float32)
    _, first_back = jax.vjp(
        lambda value_in: norm_rows(value_in, gain_first, shift_first), first_sum
    )
    d_first = first_back(d_normed)[0]
    d_branch = d_first.astype(jnp.bfloat16)
    d_u_out = jnp.einsum(
        "tc,rc->tr", d_branch, sel_up_out, preferred_element_type=jnp.float32
    ).astype(jnp.bfloat16)
    grad_up_out = jnp.einsum("tr,tc->rc", u_out, d_branch, preferred_element_type=jnp.float32)
    d_branch_all, d_u_out_all = (
        lax.all_gather(d_branch, "tensor", axis=0, tiled=True),
        lax.all_gather(d_u_out, "tensor", axis=0, tiled=True),
    )
    d_att = (
        jnp.einsum("tc,ec->te", d_branch_all, w_out, preferred_element_type=jnp.float32)
        + jnp.einsum("tr,er->te", d_u_out_all, sel_down_out, preferred_element_type=jnp.float32)
    ).astype(jnp.bfloat16)
    grad_down_out = jnp.einsum("te,tr->er", att, d_u_out_all, preferred_element_type=jnp.float32)
    rows_again, u_in_all = (
        lax.all_gather(inputs, "tensor", axis=0, tiled=True),
        lax.all_gather(u_in_shard, "tensor", axis=0, tiled=True),
    )
    qkv = project_qkv(rows_again, u_in_all, w_qkv, sel_up_qkv)
    d_qkv = attend_backward(qkv, log_total, d_att, segments, block_rows)
    d_rows_part = jnp.einsum("jtc,jdc->td", d_qkv, w_qkv, preferred_element_type=jnp.float32)
    d_u_in_part = jnp.einsum("jtc,jrc->tjr", d_qkv, sel_up_qkv, preferred_element_type=jnp.float32)
    grad_up_qkv = jnp.einsum("tjr,jtc->jrc", u_in_all, d_qkv, preferred_element_type=jnp.float32)
    d_rows_sum, d_u_in_sum = (
        lax.psum_scatter(
            d_rows_part.astype(jnp.bfloat16), "tensor", scatter_dimension=0, tiled=True
        ).astype(jnp.float32),
        lax.psum_scatter(
            d_u_in_part.astype(jnp.bfloat16), "tensor", scatter_dimension=0, tiled=True
        ).astype(jnp.float32),
    )
    d_u_in = d_u_in_sum.astype(jnp.bfloat16)
    grad_input = (
        d_first
        + d_rows_sum
        + jnp.einsum("tjr,jdr->td", d_u_in, sel_down_qkv, preferred_element_type=jnp.float32)
    )
    grad_down_qkv = jnp.einsum("td,tjr->jdr", inputs, d_u_in, preferred_element_type=jnp.float32)
    sum_up_qkv, sum_down_out, sum_up_fc1, sum_down_fc2 = (
        lax.psum_scatter(
            spread_set(set_onehot, grad_up_qkv, 1).astype(jnp.bfloat16),
            "dp",
            scatter_dimension=2,
            tiled=True,
        ).astype(jnp.float32),
        lax.psum_scatter(
            spread_set(set_onehot, grad_down_out, 0).astype(jnp.bfloat16),
            "dp",
            scatter_dimension=2,
            tiled=True,
        ).astype(jnp.float32),
        lax.psum_scatter(
            spread_set(set_onehot, grad_up_fc1, 0).astype(jnp.bfloat16),
            "dp",
            scatter_dimension=1,
            tiled=True,
        ).astype(jnp.float32),
        lax.psum_scatter(
            spread_set(set_onehot, grad_down_fc2, 0).astype(jnp.bfloat16),
            "dp",
            scatter_dimension=2,
            tiled=True,
        ).astype(jnp.float32),
    )
    sum_down_qkv, sum_up_out, sum_down_fc1, sum_up_fc2 = (
        lax.psum_scatter(
            spread_set(set_onehot, grad_down_qkv, 1),
            ("dp", "tensor"),
            scatter_dimension=2,
            tiled=True,
        ),
        lax.psum_scatter(
            spread_set(set_onehot, grad_up_out, 0),
            ("dp", "tensor"),
            scatter_dimension=2,
            tiled=True,
        ),
        lax.psum_scatter(
            spread_set(set_onehot, grad_down_fc1, 0),
            ("dp", "tensor"),
            scatter_dimension=1,
            tiled=True,
        ),
        lax.psum_scatter(
            spread_set(set_onehot, grad_up_fc2, 0),
            ("dp", "tensor"),
            scatter_dimension=2,
            tiled=True,
        ),
    )
    return (
        output,
        grad_input,
        sum_down_qkv,
        sum_up_qkv,
        sum_down_out,
        sum_up_out,
        sum_down_fc1,
        sum_up_fc1,
        sum_down_fc2,
        sum_up_fc2,
    )


def solution(mesh):
    in_specs = (
        P(("dp", "tensor"), None),
        P(("dp", "tensor"), None),
        P("dp", None),
        P("dp"),
        P(None, "dp", "tensor"),
        P("tensor", "dp"),
        P("dp", "tensor"),
        P("tensor", "dp"),
        P("dp"),
        P("dp"),
        P("dp"),
        P("dp"),
        P(None, None, "dp", None),
        P(None, None, "dp", "tensor"),
        P(None, "tensor", "dp"),
        P(None, None, "dp"),
        P(None, "dp", None),
        P(None, "dp", "tensor"),
        P(None, "tensor", "dp"),
        P(None, None, "dp"),
    )
    out_specs = (
        P(("dp", "tensor"), None),
        P(("dp", "tensor"), None),
        P(None, None, ("dp", "tensor"), None),
        P(None, None, "dp", "tensor"),
        P(None, "tensor", "dp"),
        P(None, None, ("dp", "tensor")),
        P(None, ("dp", "tensor"), None),
        P(None, "dp", "tensor"),
        P(None, "tensor", "dp"),
        P(None, None, ("dp", "tensor")),
    )
    return jax.shard_map(shards, mesh=mesh, in_specs=in_specs, out_specs=out_specs, check_vma=False)
```

profile of v0, /device:TPU:0, one launch (start us, length us, event | category | flops | bytes accessed | tf_op | source)
XLA Modules:
  0.0 1781.5 jit_solution(10383377220902404139)
XLA Ops:
  12.7 32.6 %all_gather.82 = bf16[8,256,16]{1,0,2:T(8,128)(2,1)S(1)} all-gather(bf16[8,256,2]{1,0,2:T(8,128)(2,1)S(1)} %copy.63), channel_id=1, replica_groups=mesh['dp'=8,'tensor'=4] {'dp'}, dimensions={2}, use_global_device_ids=true | all-gather | bytes 73728 | tf_op jit(solution)/shard_map/all_gather | solution.py:190
  46.2 32.4 %all_gather.78 = bf16[3,8,1024,16]{2,3,1,0:T(8,128)(2,1)S(1)} all-gather(bf16[3,8,128,16]{2,3,1,0:T(8,128)(2,1)} %param.36), channel_id=1, replica_groups=mesh['dp'=8,'tensor'=4] {'dp'}, dimensions={2}, use_global_device_ids=true | all-gather | bytes 884736 | tf_op jit(solution)/shard_map/all_gather | solution.py:188
  87.9 30.8 %all_gather.80 = bf16[3,8,16,256]{3,1,0,2:T(8,128)(2,1)S(1)} all-gather(bf16[3,8,2,256]{3,1,0,2:T(8,128)(2,1)S(1)} %copy.61), channel_id=1, replica_groups=mesh['dp'=8,'tensor'=4] {'dp'}, dimensions={2}, use_global_device_ids=true | all-gather | bytes 221184 | tf_op jit(solution)/shard_map/all_gather | solution.py:189
  118.8 28.7 %all_gather.81 = bf16[256,1024]{1,0:T(8,128)(2,1)} all-gather(bf16[256,128]{1,0:T(8,128)(2,1)S(1)} %copy-done.48), channel_id=1, replica_groups=mesh['dp'=8,'tensor'=4] {'dp'}, dimensions={1}, use_global_device_ids=true | all-gather | bytes 589824 | tf_op jit(solution)/shard_map/all_gather | solution.py:181
  155.9 70.5 %while.27 = (s32[]{:T(128)}, bf16[4,512,4,64]{1,3,2,0:T(8,128)(2,1)S(1)}, f32[4,4,512]{2,1,0:T(4,128)}, s32[4]{0:T(128)S(1)}, s32[2048]{0:T(1024)S(1)}, /*index=...) while((s32[]{:T(128)}, ...), condition=%wide.region_5.6_spmd, body=%wide.region_2.5_spmd.sunk | while | flops 1125251072 | bytes 57227940 | solution.py:87
  233.7 16.2 all-gather
  249.9 18.2 %all-gather.1 = bf16[8,1,128]{2,1,0:T(2,128)(2,1)S(1)} all-gather(bf16[1,1,128]{2,1,0:T(2,128)(2,1)S(1)} %bitcast.274), channel_id=1, replica_groups=mesh['dp'=8,'tensor'=4] {'dp'}, dimensions={0}, use_global_device_ids=true | all-gather | bytes 2304 | tf_op jit(solution)/shard_map/all_gather | solution.py:185
  268.0 26.6 %all_gather.83 = bf16[8,16,1024]{2,1,0:T(8,128)(2,1)S(1)} all-gather(bf16[8,16,128]{2,1,0:T(8,128)(2,1)S(1)} %copy-done.51), channel_id=1, replica_groups=mesh['dp'=8,'tensor'=4] {'dp'}, dimensions={2}, use_global_device_ids=true | all-gather | bytes 294912 | tf_op jit(solution)/shard_map/all_gather | solution.py:191
  299.8 27.2 %all_gather.88 = bf16[8,1024,16]{1,2,0:T(8,128)(2,1)S(1)} all-gather(bf16[8,128,16]{1,2,0:T(8,128)(2,1)S(1)} %copy-done.52), channel_id=1, replica_groups=mesh['dp'=8,'tensor'=4] {'dp'}, dimensions={1}, use_global_device_ids=true | all-gather | bytes 294912 | tf_op jit(solution)/shard_map/all_gather | solution.py:192
  328.1 33.3 %all_gather.90 = bf16[8,16,1024]{2,0,1:T(8,128)(2,1)} all-gather(bf16[8,2,1024]{2,0,1:T(8,128)(2,1)S(1)} %copy.64), channel_id=1, replica_groups=mesh['dp'=8,'tensor'=4] {'dp'}, dimensions={1}, use_global_device_ids=true | all-gather | bytes 294912 | tf_op jit(solution)/shard_map/all_gather | solution.py:193
  362.2 30.8 %all_gather.92 = bf16[8,1024,16]{1,0,2:T(8,128)(2,1)S(1)} all-gather(bf16[8,1024,2]{1,0,2:T(8,128)(2,1)S(1)} %copy.65), channel_id=1, replica_groups=mesh['dp'=8,'tensor'=4] {'dp'}, dimensions={2}, use_global_device_ids=true | all-gather | bytes 294912 | tf_op jit(solution)/shard_map/all_gather | solution.py:194
  409.7 21.0 %multiply_convert_fusion.1 = (bf16[2048,1024]{1,0:T(8,128)(2,1)S(1)}, f32[2048,1024]{1,0:T(8,128)}, f32[2048,1024]{1,0:T(8,128)}) fusion(f32[2048,1024]{1,0:T(8,128)S(1)} %fusion.117, bf16[2048,16]{0,1:T(8,128)(2,1)S(1)} %all_gather.89, bf16[1,16,1024]{2,0,1:T(2,128)(2,1)S(1)} %copy-done.41), kind=kOutput, calls=%fused_computation.49 | convolution fusion | flops 205520896 | bytes 29458432 | tf_op jit(solution)/shard_map/dot_general | solution.py:14
  436.7 9.4 convolution_convert_fusion.2
  446.8 17.6 all-gather.2
  464.4 16.7 all-gather.3
  481.7 26.4 %all_gather.93 = bf16[8,16,1024]{2,1,0:T(8,128)(2,1)S(1)} all-gather(bf16[8,16,128]{2,1,0:T(8,128)(2,1)S(1)} %copy-done.53), channel_id=1, replica_groups=mesh['dp'=8,'tensor'=4] {'dp'}, dimensions={2}, use_global_device_ids=true | all-gather | bytes 294912 | tf_op jit(solution)/shard_map/all_gather | solution.py:195
  522.7 24.8 %all-gather.22.cloned.1.call-done = bf16[2048,1024]{1,0:T(8,128)(2,1)} async-done(((bf16[512,1024]{1,0:T(8,128)(2,1)}), bf16[2048,1024]{1,0:T(8,128)(2,1)}) %all-gather.22.cloned.1.call-update) | async-done | bytes 4194320 | tf_op jit(solution)/shard_map/all_gather | solution.py:267
  566.5 9.4 convolution_convert_fusion.1
  576.0 10.0 reduce-scatter.35.cloned.1.call-done
  586.0 47.1 %reduce-scatter.33.cloned.1.call-done = bf16[512,1024]{1,0:T(8,128)(2,1)} async-done(((bf16[2048,1024]{1,0:T(8,128)(2,1)}), bf16[512,1024]{1,0:T(8,128)(2,1)}) %reduce-scatter.33.cloned.1.call-update) | async-done | bytes 1048592 | tf_op jit(solution)/shard_map/reduce_scatter | solution.py:287
  649.5 25.0 %all-gather.24.cloned.1.call-done = bf16[2048,1024]{1,0:T(8,128)(2,1)} async-done(((bf16[512,1024]{1,0:T(8,128)(2,1)}), bf16[2048,1024]{1,0:T(8,128)(2,1)}) %all-gather.24.cloned.1.call-update) | async-done | bytes 4194320 | tf_op jit(solution)/shard_map/all_gather | solution.py:311
  680.6 254.2 %while.28 = (s32[]{:T(128)}, f32[2048,4,64]{0,2,1:T(8,128)}, f32[2048,4,64]{0,2,1:T(8,128)}, bf16[4,512,4,64]{1,3,2,0:T(8,128)(2,1)}, s32[4]{0:T(128)S(1)}, /*in...) while((s32[]{:T(128)}, f32[2048,4,64]{0,2,1:T(8,128)}, ...), condition=%wide.region_22.23_spmd.clone, body=%wide.region_20.22_spmd.clone.sunk | while | flops 2751199232 | bytes 176495360 | solution.py:129
  683.5 9.3 fusion.210
  694.3 12.6 multiply_reduce_fusion.6
  706.8 14.9 multiply_convert_fusion.7
  731.7 11.8 fusion.212
  746.1 9.3 fusion.210
  756.8 12.6 multiply_reduce_fusion.6
  769.4 14.9 multiply_convert_fusion.7
  794.9 12.4 fusion.212
  809.8 9.3 fusion.210
  820.5 12.6 multiply_reduce_fusion.6
  833.1 14.9 multiply_convert_fusion.7
  858.6 12.4 fusion.212
  873.5 9.2 fusion.210
  884.2 12.6 multiply_reduce_fusion.6
  896.8 14.9 multiply_convert_fusion.7
  922.3 12.4 fusion.212
  989.0 9.3 reshape.271
  1005.1 29.9 %reduce-scatter.47.cloned.1.call-done = bf16[8,1024,2]{1,0,2:T(8,128)(2,1)} async-done(((bf16[8,1024,16]{1,0,2:T(8,128)(2,1)}), bf16[8,1024,2]{1,0,2:T(8,128)(2,1)}) %reduce-scatter.47.cloned.1.call-update) | async-done | bytes 32784 | tf_op jit(solution)/shard_map/reduce_scatter | solution.py:362
  1036.4 133.7 %reduce-scatter.53.cloned.1.call-done = f32[32,128]{1,0:T(8,128)} async-done(((f32[1024,128]{1,0:T(8,128)}), f32[32,128]{1,0:T(8,128)}) %reduce-scatter.53.cloned.1.call-update) | async-done | bytes 16400
  1171.7 59.8 %reduce-scatter.43.cloned.1.call-done = bf16[8,256,2]{1,0,2:T(8,128)(2,1)} async-done(((bf16[8,256,16]{1,0,2:T(8,128)(2,1)}), bf16[8,256,2]{1,0,2:T(8,128)(2,1)}) %reduce-scatter.43.cloned.1.call-update) | async-done | bytes 8208 | tf_op jit(solution)/shard_map/reduce_scatter | solution.py:350
  1232.8 62.5 %reduce-scatter.45.cloned.1.call-done = bf16[8,2,1024]{2,0,1:T(8,128)(2,1)} async-done(((bf16[8,16,1024]{2,0,1:T(8,128)(2,1)}), bf16[8,2,1024]{2,0,1:T(8,128)(2,1)}) %reduce-scatter.45.cloned.1.call-update) | async-done | bytes 32784 | tf_op jit(solution)/shard_map/reduce_scatter | solution.py:356
  1296.7 133.5 %reduce-scatter.55.cloned.1.call-done = f32[32,128]{1,0:T(8,128)} async-done(((f32[1024,128]{1,0:T(8,128)}), f32[32,128]{1,0:T(8,128)}) %reduce-scatter.55.cloned.1.call-update) | async-done | bytes 16400
  1431.8 130.2 %reduce-scatter.51.cloned.1.call-done = f32[32,128]{1,0:T(8,128)} async-done(((f32[1024,128]{1,0:T(8,128)}), f32[32,128]{1,0:T(8,128)}) %reduce-scatter.51.cloned.1.call-update) | async-done | bytes 16400
  1563.6 59.1 %reduce-scatter.41.cloned.1.call-done = bf16[3,8,2,256]{3,1,0,2:T(8,128)(2,1)} async-done(((bf16[3,8,16,256]{3,1,0,2:T(8,128)(2,1)}), bf16[3,8,2,256]{3,1,0,2:T(8,128)(2,1)}) %reduce-scatter.41.cloned.1.call-update) | async-done | bytes 24592 | tf_op jit(solution)/shard_map/reduce_scatter | solution.py:344
  1624.1 101.4 %reduce-scatter.49.cloned.1.call-done = f32[32,384]{1,0:T(8,128)} async-done(((f32[1024,384]{1,0:T(8,128)}), f32[32,384]{1,0:T(8,128)}) %reduce-scatter.49.cloned.1.call-update) | async-done | bytes 49168
  1727.3 44.4 %reduce-scatter.37.cloned.1.call-done = bf16[512,1024]{1,0:T(8,128)(2,1)} async-done(((bf16[2048,1024]{1,0:T(8,128)(2,1)}), bf16[512,1024]{1,0:T(8,128)(2,1)}) %reduce-scatter.37.cloned.1.call-update) | async-done | bytes 1048592 | tf_op jit(solution)/shard_map/reduce_scatter | solution.py:329
  (356 shorter events, 305.2 us)
Async XLA Ops:
  7.2 111.6 %copy-start.48 = (bf16[256,128]{1,0:T(8,128)(2,1)S(1)}, bf16[256,128]{1,0:T(8,128)(2,1)}, u32[]{:S(2)}) copy-start(bf16[256,128]{1,0:T(8,128)(2,1)} %param.29) | copy-start | bytes 196612
  7.2 140.5 %all-gather.12.cloned.1.call-start = ((), (), s32[]{:S(2)}) async-start(), calls=%async_computation.16 | async-start | bytes 1769472 | tf_op jit(solution)/shard_map/all_gather | solution.py:180
  9.0 138.7 %all-gather.14.cloned.1.call-start = ((), (), s32[]{:S(2)}) async-start(), calls=%async_computation.17 | async-start | bytes 5242880 | tf_op jit(solution)/shard_map/all_gather | solution.py:219
  9.8 285.2 %reduce-scatter.27.cloned.1.call-start = ((), (), s32[]{:S(2)}) async-start(), calls=%async_computation.19 | async-start | bytes 81920 | tf_op jit(solution)/shard_map/reduce_scatter | solution.py:230
  79.2 74.2 %copy-start.28 = (bf16[1,3,1024,16]{2,0,3,1:T(2,128)(2,1)}, bf16[1,3,1024,16]{2,0,3,1:T(2,128)(2,1)S(1)}, u32[]{:S(2)}) copy-start(bf16[1,3,1024,16]{2,0,3,1:T(2,128)(2,1)S(1)} %fusion.53) | copy-start | bytes 294916
  87.9 65.6 %copy-start.30 = (bf16[2048,3,16]{0,2,1:T(8,128)(2,1)}, bf16[2048,3,16]{0,2,1:T(8,128)(2,1)S(1)}, u32[]{:S(2)}) copy-start(bf16[2048,3,16]{0,2,1:T(8,128)(2,1)S(1)} %all_gather.79) | copy-start | bytes 589828
  228.6 66.4 %reduce-scatter.25.cloned.1.call-start = ((), (), s32[]{:S(2)}) async-start(), calls=%async_computation.18 | async-start | bytes 5242880 | tf_op jit(solution)/shard_map/reduce_scatter | solution.py:227
  233.0 16.9 copy-start.60
  233.0 35.0 %copy-start.51 = (bf16[8,16,128]{2,1,0:T(8,128)(2,1)S(1)}, bf16[8,16,128]{2,1,0:T(8,128)(2,1)}, u32[]{:S(2)}) copy-start(bf16[8,16,128]{2,1,0:T(8,128)(2,1)} %param.39) | copy-start | bytes 98308
  233.0 169.7 %all-gather.18.cloned.1.call-start = ((), (), s32[]{:S(2)}) async-start(), calls=%async_computation.21 | async-start | bytes 2359296 | tf_op jit(solution)/shard_map/all_gather | solution.py:182
  233.6 169.1 %all-gather.16.cloned.1.call-start = ((), (), s32[]{:S(2)}) async-start(), calls=%async_computation.20 | async-start | bytes 5242880 | tf_op jit(solution)/shard_map/all_gather | solution.py:240
  297.5 29.4 %copy-start.56 = (f32[512]{0:T(512)}, f32[512]{0:T(512)S(1)}, u32[]{:S(2)}) copy-start(f32[512]{0:T(512)S(1)} %multiply_reduce_fusion.4) | copy-start | bytes 6148
  297.5 100.0 %copy-start.49 = (f32[512]{0:T(512)}, f32[512]{0:T(512)S(1)}, u32[]{:S(2)}) copy-start(f32[512]{0:T(512)S(1)} %fusion.100) | copy-start | bytes 6148
  299.0 137.7 %all-gather.20.cloned.1.call-start = ((), (), s32[]{:S(2)}) async-start(), calls=%async_computation.22 | async-start | bytes 2359296 | tf_op jit(solution)/shard_map/all_gather | solution.py:183
  299.7 208.7 %reduce-scatter.31.cloned.1.call-start = ((), (), s32[]{:S(2)}) async-start(), calls=%async_computation.24 | async-start | bytes 81920 | tf_op jit(solution)/shard_map/reduce_scatter | solution.py:250
  409.7 23.0 %copy-start.22 = (bf16[1,1024,16]{2,1,0:T(8,128)(2,1)S(1)}, bf16[1,1024,16]{2,1,0:T(8,128)(2,1)}, u32[]{:S(2)}) copy-start(bf16[1,1024,16]{2,1,0:T(8,128)(2,1)} %copy.90) | copy-start | bytes 98308
  434.6 73.8 %reduce-scatter.29.cloned.1.call-start = ((), (), s32[]{:S(2)}) async-start(), calls=%async_computation.23 | async-start | bytes 5242880 | tf_op jit(solution)/shard_map/reduce_scatter | solution.py:247
  446.1 18.2 %copy-start.62 = (bf16[128]{0:T(256)(128)(2,1)S(1)}, bf16[128]{0:T(256)(128)(2,1)}, u32[]{:S(2)}) copy-start(bf16[128]{0:T(256)(128)(2,1)} %param.35) | copy-start | bytes 772
  446.1 35.6 %copy-start.53 = (bf16[8,16,128]{2,1,0:T(8,128)(2,1)S(1)}, bf16[8,16,128]{2,1,0:T(8,128)(2,1)}, u32[]{:S(2)}) copy-start(bf16[8,16,128]{2,1,0:T(8,128)(2,1)} %param.43) | copy-start | bytes 98308
  446.1 101.3 %all-gather.22.cloned.1.call-start = ((), (), s32[]{:S(2)}) async-start(), calls=%async_computation.25 | async-start | bytes 5242880 | tf_op jit(solution)/shard_map/all_gather | solution.py:267
  515.6 70.4 %reduce-scatter.35.cloned.1.call-start = ((), (), s32[]{:S(2)}) async-start(), calls=%async_computation.27 | async-start | bytes 81920 | tf_op jit(solution)/shard_map/reduce_scatter | solution.py:290
  554.5 10.0 copy-start.42
  566.4 66.7 %reduce-scatter.33.cloned.1.call-start = ((), (), s32[]{:S(2)}) async-start(), calls=%async_computation.26 | async-start | bytes 5242880 | tf_op jit(solution)/shard_map/reduce_scatter | solution.py:287
  575.9 60.7 %copy-start.50 = (f32[512]{0:T(512)S(1)}, f32[512]{0:T(512)}, u32[]{:S(2)}) copy-start(f32[512]{0:T(512)} %copy-done.49) | copy-start | bytes 6148
  575.9 98.5 %all-gather.24.cloned.1.call-start = ((), (), s32[]{:S(2)}) async-start(), calls=%async_computation.28 | async-start | bytes 5242880 | tf_op jit(solution)/shard_map/all_gather | solution.py:311
  639.8 340.9 %reduce-scatter.39.cloned.1.call-start = ((), (), s32[]{:S(2)}) async-start(), calls=%async_computation.30 | async-start | bytes 245760 | tf_op jit(solution)/shard_map/reduce_scatter | solution.py:332
  649.5 30.0 %copy-start.33 = (bf16[2048,16]{0,1:T(8,128)(2,1)}, bf16[2048,16]{0,1:T(8,128)(2,1)S(1)}, u32[]{:S(2)}) copy-start(bf16[2048,16]{0,1:T(8,128)(2,1)S(1)} %all_gather.99) | copy-start | bytes 196612
  649.5 31.1 %copy-start.3 = (bf16[2048,4,64]{0,2,1:T(8,128)(2,1)S(1)}, bf16[2048,4,64]{0,2,1:T(8,128)(2,1)}, u32[]{:S(2)}) copy-start(bf16[2048,4,64]{0,2,1:T(8,128)(2,1)} %copy-done.2) | copy-start | bytes 3145732
  649.5 31.1 %copy-start.18 = (s32[2048]{0:T(1024)S(1)}, s32[2048]{0:T(1024)}, u32[]{:S(2)}) copy-start(s32[2048]{0:T(1024)} %copy-done.17) | copy-start | bytes 24580
  649.5 31.1 %copy-start.64 = (s32[4]{0:T(128)S(1)}, s32[4]{0:T(128)}, u32[]{:S(2)}) copy-start(s32[4]{0:T(128)} %copy-done.63) | copy-start | bytes 52
  934.8 8.6 copy-start.1
  950.5 84.4 %reduce-scatter.47.cloned.1.call-start = ((), (), s32[]{:S(2)}) async-start(), calls=%async_computation.34 | async-start | bytes 294912 | tf_op jit(solution)/shard_map/reduce_scatter | solution.py:362
  951.9 218.3 %reduce-scatter.53.cloned.1.call-start = ((), (), s32[]{:S(2)}) async-start(), calls=%async_computation.37 | async-start | bytes 540672
  954.6 7.3 copy-start.34
  958.7 272.8 %reduce-scatter.43.cloned.1.call-start = ((), (), s32[]{:S(2)}) async-start(), calls=%async_computation.32 | async-start | bytes 73728 | tf_op jit(solution)/shard_map/reduce_scatter | solution.py:350
  963.0 332.3 %reduce-scatter.45.cloned.1.call-start = ((), (), s32[]{:S(2)}) async-start(), calls=%async_computation.33 | async-start | bytes 294912 | tf_op jit(solution)/shard_map/reduce_scatter | solution.py:356
  964.4 465.8 %reduce-scatter.55.cloned.1.call-start = ((), (), s32[]{:S(2)}) async-start(), calls=%async_computation.38 | async-start | bytes 540672
  971.2 590.9 %reduce-scatter.51.cloned.1.call-start = ((), (), s32[]{:S(2)}) async-start(), calls=%async_computation.36 | async-start | bytes 540672
  977.9 644.8 %reduce-scatter.41.cloned.1.call-start = ((), (), s32[]{:S(2)}) async-start(), calls=%async_computation.31 | async-start | bytes 221184 | tf_op jit(solution)/shard_map/reduce_scatter | solution.py:344
  980.7 744.8 %reduce-scatter.49.cloned.1.call-start = ((), (), s32[]{:S(2)}) async-start(), calls=%async_computation.35 | async-start | bytes 1622016
  989.0 9.3 copy-start.21
  989.0 9.3 copy-start.26
  989.0 9.4 copy-start.27
  998.3 773.4 %reduce-scatter.37.cloned.1.call-start = ((), (), s32[]{:S(2)}) async-start(), calls=%async_computation.29 | async-start | bytes 5242880 | tf_op jit(solution)/shard_map/reduce_scatter | solution.py:329
  1005.0 766.7 %copy-start.9 = (f32[512,1024]{1,0:T(8,128)S(1)}, f32[512,1024]{1,0:T(8,128)}, u32[]{:S(2)}) copy-start(f32[512,1024]{1,0:T(8,128)} %copy-done.8) | copy-start | bytes 6291460
  1005.0 766.7 %copy-start.29 = (bf16[1,3,1024,16]{2,0,3,1:T(2,128)(2,1)S(1)}, bf16[1,3,1024,16]{2,0,3,1:T(2,128)(2,1)}, u32[]{:S(2)}) copy-start(bf16[1,3,1024,16]{2,0,3,1:T(2,128)(2,1)} %copy-done.28) | copy-start | bytes 294916
  1005.0 766.7 %copy-start.40 = (bf16[512,3,16]{0,2,1:T(8,128)(2,1)S(1)}, bf16[512,3,16]{0,2,1:T(8,128)(2,1)}, u32[]{:S(2)}) copy-start(bf16[512,3,16]{0,2,1:T(8,128)(2,1)} %reduce-scatter.39.cloned.1.call-done) | copy-start | bytes 147460
  1005.0 766.7 %copy-start.55 = (f32[512]{0:T(512)S(1)}, f32[512]{0:T(512)}, u32[]{:S(2)}) copy-start(f32[512]{0:T(512)} %copy-done.54) | copy-start | bytes 6148
  (43 other events, 196.4 us)
Sparse Core Ops, SparseCore 0:
  10.6 49.8 all-gather.11
  62.0 40.9 all-gather.13
  228.7 17.2 reduce-scatter.26
  248.5 44.5 reduce-scatter.24
  295.0 53.6 all-gather.17
  350.2 33.3 all-gather.15
  385.6 51.0 all-gather.19
  439.7 17.6 reduce-scatter.30
  460.0 44.5 reduce-scatter.28
  515.7 31.7 all-gather.21
  566.5 19.4 reduce-scatter.34
  588.6 44.5 reduce-scatter.32
  639.9 34.4 all-gather.23
  950.6 19.7 reduce-scatter.38
  973.6 61.2 reduce-scatter.46
  1037.0 133.0 reduce-scatter.52
  1174.3 57.1 reduce-scatter.42
  1235.0 60.2 reduce-scatter.44
  1297.6 132.5 reduce-scatter.54
  1432.3 129.6 reduce-scatter.50
  1565.6 57.0 reduce-scatter.40
  1629.4 96.0 reduce-scatter.48
  1728.2 43.5 reduce-scatter.36
where the time goes:
time: 1790 us; the launch traced here: 1780 us
  waiting for transfers between devices  866 us (48%)
  blocking collectives  360 us (20%)
  matrix products  337 us (19%)
  other arithmetic  99 us (6%)
  local copies, waits for them, and re-layouts  86 us (5%)
    unnamed x27, waiting for transfers between devices  501 us
    reduce_scatter x1, waiting for transfers between devices, shards(): lax.psum_scatter(spread_set(set_onehot, grad_up_fc1, 0).astype(jnp.bfloat...  62.5 us
    unnamed x154, local copies, waits for them, and re-layouts  60.7 us
    reduce_scatter x1, waiting for transfers between devices, shards(): lax.psum_scatter(spread_set(set_onehot, grad_down_out, 0).astype(jnp.bflo...  59.8 us
    convert_element_type x4, other arithmetic, advance(): score_grad = (attn_prob * (prob_grad - row_dot)).astype(jnp.bfloat16)  59.7 us
    reduce_scatter x1, waiting for transfers between devices, shards(): lax.psum_scatter(spread_set(set_onehot, grad_up_qkv, 1).astype(jnp.bfloat...  59.1 us
    dot_general x8, matrix products, block_scores(): jnp.einsum('qhd,khd->hqk', query_block, key_rows, preferred_element_type=...  55.6 us
    dot_general x4, matrix products, advance(): jnp.einsum('qhd,khd->hqk', grad_block, value_rows, preferred_element_type...  50.3 us
  transfers between devices with their start and end apart: 23, of which 14 were waited for; matrix products, arithmetic and copies ran while one was open for 8% of the time, Pallas kernels for 0%

commit v1 on v0

v1 whole, which is shorter than its diff:
```python
import functools

import jax
import jax.numpy as jnp
from jax import lax
from jax.experimental import pallas as pl
from jax.experimental.pallas import tpu as pltpu
from jax.sharding import PartitionSpec as P

HD = 64
EPS = 1e-05
NEG = -1000000000.0
LOG2E = 1.4426950408889634
BF = jnp.bfloat16
F32 = jnp.float32
VMEM_LIMIT = 60 * 2**20


def mm(left, right):
    return jnp.dot(left, right, preferred_element_type=F32)


def mm_nt(left, right):
    return lax.dot_general(left, right, (((1,), (1,)), ((), ())), preferred_element_type=F32)


def transpose_small(value):
    return value.astype(F32).T.astype(BF)


def segment_ids(doc_lengths, total):
    ends = jnp.cumsum(doc_lengths)
    places = jnp.arange(total, dtype=jnp.int32)
    return jnp.sum((places[:, None] >= ends[None, :]).astype(jnp.int32), axis=1)


def attend_forward_kernel(
    heads, block, chunk, q_ref, k_ref, v_ref, segq_ref, segk_ref,
    att_ref, e_ref, l_ref, keys_wide, values_t, scores,
):
    length = k_ref.shape[0]

    @pl.when(pl.program_id(0) == 0)
    def _():
        onehot = (lax.broadcasted_iota(jnp.int32, (length, 128), 1) == segk_ref[...]).astype(BF)
        ones = (lax.broadcasted_iota(jnp.int32, (16, length), 0) == 0).astype(BF)
        flipped = v_ref[...].T
        for h in range(heads):
            key = k_ref[:, h * HD : (h + 1) * HD]
            keys_wide[h, :, 0:HD] = key
            keys_wide[h, :, HD : 2 * HD] = key
            keys_wide[h, :, 2 * HD :] = onehot
            values_t[h, 0:HD, :] = flipped[h * HD : (h + 1) * HD, :]
            values_t[h, HD:, :] = ones

    flipped_q = q_ref[...].astype(F32).T * (HD ** (-0.5) * LOG2E)
    mask = jnp.where(
        lax.broadcasted_iota(jnp.int32, (128, block), 0) == segq_ref[...], 0.0, NEG
    ).astype(BF)
    mixed = []
    for h in range(heads):
        query = flipped_q[h * HD : (h + 1) * HD, :]
        high = query.astype(BF)
        low = (query - high.astype(F32)).astype(BF)
        right = jnp.concatenate([high, low, mask], axis=0)
        top = None
        for c in range(length // chunk):
            part = mm(keys_wide[h, c * chunk : (c + 1) * chunk, :], right)
            scores[h, c * chunk : (c + 1) * chunk, :] = part
            part = jnp.max(part.reshape(chunk // 8, 8, block), axis=0)
            top = part if top is None else jnp.maximum(top, part)
        top = jnp.max(top, axis=0, keepdims=True)
        total = None
        for c in range(length // chunk):
            e = jnp.exp2(scores[h, c * chunk : (c + 1) * chunk, :] - top).astype(BF)
            e_ref[h, 0, c * chunk : (c + 1) * chunk, :] = e
            part = mm(values_t[h, :, c * chunk : (c + 1) * chunk], e)
            total = part if total is None else total + part
        row_sum = total[HD : HD + 1, :]
        l_ref[h, 0] = jnp.broadcast_to(row_sum, (8, block))
        mixed.append(total[0:HD, :] / row_sum)
    att_ref[...] = jnp.concatenate(mixed, axis=0).T.astype(BF)


def attend_forward(q, k, v, segments, group, heads):
    length = q.shape[0]
    width = heads * HD
    block = min(512, length)
    chunk = min(512, length)
    count = length // block
    return pl.pallas_call(
        functools.partial(attend_forward_kernel, heads, block, chunk),
        grid=(count,),
        in_specs=[
            pl.BlockSpec((block, width), lambda i: (i, group)),
            pl.BlockSpec((length, width), lambda i: (0, group)),
            pl.BlockSpec((length, width), lambda i: (0, group)),
            pl.BlockSpec((1, block), lambda i: (0, i)),
            pl.BlockSpec((length, 1), lambda i: (0, 0)),
        ],
        out_specs=[
            pl.BlockSpec((block, width), lambda i: (i, 0)),
            pl.BlockSpec((heads, 1, length, block), lambda i: (0, i, 0, 0)),
            pl.BlockSpec((heads, 1, 8, block), lambda i: (0, i, 0, 0)),
        ],
        out_shape=[
            jax.ShapeDtypeStruct((length, width), BF),
            jax.ShapeDtypeStruct((heads, count, length, block), BF),
            jax.ShapeDtypeStruct((heads, count, 8, block), F32),
        ],
        scratch_shapes=[
            pltpu.VMEM((heads, length, 256), BF),
            pltpu.VMEM((heads, HD + 16, length), BF),
            pltpu.VMEM((heads, length, block), F32),
        ],
        compiler_params=pltpu.CompilerParams(
            vmem_limit_bytes=VMEM_LIMIT, dimension_semantics=("arbitrary",)
        ),
        cost_estimate=pl.CostEstimate(
            flops=4 * heads * length * length * 256,
            bytes_accessed=heads * length * length * 2,
            transcendentals=heads * length * length,
        ),
        name="attend_forward",
    )(q, k, v, segments[None, :], segments[:, None])


def attend_backward_kernel(
    heads, block, chunk, q_ref, k_ref, v_ref, o_ref, do_ref, e_ref, l_ref,
    dq_ref, dk_ref, dv_ref, values_wide, keys_t, dk_sum, dv_sum,
):
    length = k_ref.shape[0]
    width = heads * HD
    i = pl.program_id(0)

    @pl.when(i == 0)
    def _():
        ones = (lax.broadcasted_iota(jnp.int32, (length, 128), 1) < 2).astype(BF)
        for h in range(heads):
            value = v_ref[:, h * HD : (h + 1) * HD]
            values_wide[h, :, 0:HD] = value
            values_wide[h, :, HD : 2 * HD] = value
            values_wide[h, :, 2 * HD :] = ones
        keys_t[...] = k_ref[...].T
        dk_sum[...] = jnp.zeros_like(dk_sum)
        dv_sum[...] = jnp.zeros_like(dv_sum)

    q = q_ref[...]
    flipped_do = do_ref[...].astype(F32).T
    flipped_o = o_ref[...].astype(F32).T
    lane = lax.broadcasted_iota(jnp.int32, (block, width), 1)
    row = lax.broadcasted_iota(jnp.int32, (128, block), 0)
    grads = []
    for h in range(heads):
        own = slice(h * HD, (h + 1) * HD)
        inverse = 1.0 / l_ref[h, 0, 0:1, :]
        dot = -jnp.sum(flipped_do[own] * flipped_o[own], axis=0, keepdims=True) * inverse
        scaled = flipped_do[own] * inverse
        high = scaled.astype(BF)
        low = (scaled - high.astype(F32)).astype(BF)
        dot_high = dot.astype(BF)
        dot_low = (dot - dot_high.astype(F32)).astype(BF)
        dots = jnp.where(row == 0, dot_high, jnp.where(row == 1, dot_low, jnp.zeros_like(dot_low)))
        right = jnp.concatenate([high, low, dots], axis=0)
        do_rows = high.T
        if heads == 2:
            empty = jnp.zeros_like(do_rows)
            do_rows = jnp.concatenate([do_rows, empty] if h == 0 else [empty, do_rows], axis=1)
        query = jnp.where((lane >= h * HD) & (lane < (h + 1) * HD), q, jnp.zeros_like(q))
        total = None
        for c in range(length // chunk):
            rows = slice(c * chunk, (c + 1) * chunk)
            e = e_ref[h, 0, rows, :]
            part = mm(values_wide[h, rows, :], right)
            ds = (e.astype(F32) * part).astype(BF)
            dv_sum[rows, :] += mm(e, do_rows)
            dk_sum[rows, :] += mm(ds, query)
            part = mm(keys_t[own, rows], ds)
            total = part if total is None else total + part
        grads.append(total * HD ** (-0.5))
    dq_ref[...] = jnp.concatenate(grads, axis=0).T.astype(BF)

    @pl.when(i == pl.num_programs(0) - 1)
    def _():
        dk_ref[...] = (dk_sum[...] * HD ** (-0.5)).astype(BF)
        dv_ref[...] = dv_sum[...].astype(BF)


def attend_backward(q, k, v, att, d_att, e, row_sum, group, heads):
    length = q.shape[0]
    width = heads * HD
    block = e.shape[3]
    chunk = min(512, length)
    count = length // block
    whole = pl.BlockSpec((length, width), lambda i: (0, group))
    return pl.pallas_call(
        functools.partial(attend_backward_kernel, heads, block, chunk),
        grid=(count,),
        in_specs=[
            pl.BlockSpec((block, width), lambda i: (i, group)),
            whole,
            whole,
            pl.BlockSpec((block, width), lambda i: (i, 0)),
            pl.BlockSpec((block, width), lambda i: (i, group)),
            pl.BlockSpec((heads, 1, length, block), lambda i: (0, i, 0, 0)),
            pl.BlockSpec((heads, 1, 8, block), lambda i: (0, i, 0, 0)),
        ],
        out_specs=[
            pl.BlockSpec((block, width), lambda i: (i, 0)),
            pl.BlockSpec((length, width), lambda i: (0, 0)),
            pl.BlockSpec((length, width), lambda i: (0, 0)),
        ],
        out_shape=[jax.ShapeDtypeStruct((length, width), BF)] * 3,
        scratch_shapes=[
            pltpu.VMEM((heads, length, 256), BF),
            pltpu.VMEM((width, length), BF),
            pltpu.VMEM((length, width), F32),
            pltpu.VMEM((length, width), F32),
        ],
        compiler_params=pltpu.CompilerParams(
            vmem_limit_bytes=VMEM_LIMIT, dimension_semantics=("arbitrary",)
        ),
        cost_estimate=pl.CostEstimate(
            flops=8 * heads * length * length * 256,
            bytes_accessed=heads * length * length * 2,
            transcendentals=0,
        ),
        name="attend_backward",
    )(q, k, v, att, d_att, e, row_sum)


def normal_parts(z):
    density = jnp.exp2(z * z * (-0.5 * LOG2E))
    t = 1.0 / (1.0 + (0.3275911 * 0.5**0.5) * jnp.abs(z))
    poly = t * (
        0.254829592 * 0.5
        + t
        * (
            -0.284496736 * 0.5
            + t * (1.421413741 * 0.5 + t * (-1.453152027 * 0.5 + t * (1.061405429 * 0.5)))
        )
    )
    tail = poly * density
    return jnp.where(z < 0.0, tail, 1.0 - tail), density * 0.3989422804014327


def normalize(values):
    center = values - jnp.mean(values, axis=-1, keepdims=True)
    scale = lax.rsqrt(jnp.mean(center * center, axis=-1, keepdims=True) + EPS)
    return center * scale, scale


def normalize_back(e, normal, scale):
    return scale * (
        e
        - jnp.mean(e, axis=-1, keepdims=True)
        - normal * jnp.mean(e * normal, axis=-1, keepdims=True)
    )


def middle_kernel(
    cuts, hidden_block, perm_ref, att_ref, x_ref, cot_ref, wo_hbm, w1_hbm, w2_hbm,
    down_out, up_out, down_fc1, up_fc1, down_fc2, up_fc2, gain1, bias1, gain2, bias2,
    *rest,
):
    out_ref, dy1_ref = rest[0:2]
    d_att_refs = rest[2 : 2 + cuts]
    (
        g_up_fc2, g_down_fc2, g_up_fc1, g_down_fc1, g_up_out, g_down_out,
        wo, w1, w2, hidden, slope, normal1, normed, low_rows, total, wo_sem, w1_sem, w2_sem,
    ) = rest[2 + cuts :]
    rows, model = x_ref.shape
    units = w1.shape[1]

    def fetch(source, a, b, target, row, col, sem):
        height, width = source.shape[2:]
        return pltpu.make_async_copy(
            source.at[a, b],
            target.at[pl.ds(row * height, height), pl.ds(col * width, width)],
            sem,
        )

    outer, inner = wo_hbm.shape[:2]
    for b in range(inner):
        for a in range(outer):
            fetch(wo_hbm, a, perm_ref[b] if inner > 1 else 0, wo, b, a, wo_sem).start()
    for b in range(w1_hbm.shape[1]):
        for a in range(w1_hbm.shape[0]):
            fetch(w1_hbm, a, b, w1, a, b, w1_sem.at[b]).start()
        for a in range(w2_hbm.shape[0]):
            fetch(w2_hbm, a, b, w2, b, a, w2_sem.at[b]).start()

    pltpu.make_async_copy(wo, wo, wo_sem).wait()
    att = att_ref[...]
    u_out = mm_nt(att, down_out[...]).astype(BF)
    first = x_ref[...].astype(F32) + mm(att, wo[...]) + mm(u_out, up_out[...])
    normal, scale1 = normalize(first)
    normal1[...] = normal
    full = normal * gain1[...].astype(F32) + bias1[...].astype(F32)
    normed[...] = full
    low_rows[...] = full.astype(BF)
    u_fc1 = mm_nt(low_rows[...], down_fc1[...]).astype(BF)

    blocks = units // hidden_block
    per_cut = w1_hbm.shape[3] // hidden_block

    def before(i):
        cols = slice(i * hidden_block, (i + 1) * hidden_block)
        if i % per_cut == 0:
            part = w1_hbm.shape[3]
            b = i // per_cut
            view = w1.at[:, b * part : (b + 1) * part]
            pltpu.make_async_copy(view, view, w1_sem.at[b]).wait()
            part = w2_hbm.shape[2]
            view = w2.at[b * part : (b + 1) * part, :]
            pltpu.make_async_copy(view, view, w2_sem.at[b]).wait()
        return mm(low_rows[...], w1[:, cols]) + mm(u_fc1, up_fc1[:, cols])

    z = before(0)
    u_sum = None
    for i in range(blocks):
        cols = slice(i * hidden_block, (i + 1) * hidden_block)
        following = before(i + 1) if i + 1 < blocks else None
        phi_sum, phi = normal_parts(z)
        act = (z * phi_sum).astype(BF)
        hidden[:, cols] = act
        slope[:, cols] = phi_sum + z * phi
        part = mm(act, w2[cols, :])
        total[...] = part if i == 0 else total[...] + part
        part = mm_nt(act, down_fc2[:, cols])
        u_sum = part if u_sum is None else u_sum + part
        z = following
    u_fc2 = u_sum.astype(BF)
    second = normed[...] + total[...] + mm(u_fc2, up_fc2[...])
    normal2, scale2 = normalize(second)
    gain = gain2[...].astype(F32)
    out_ref[...] = (normal2 * gain + bias2[...].astype(F32)).astype(BF)
    d_second = normalize_back(cot_ref[...].astype(F32) * gain, normal2, scale2)
    total[...] = d_second
    d_ffn = d_second.astype(BF)
    d_u2 = mm_nt(d_ffn, up_fc2[...]).astype(BF)
    d_u2_t = transpose_small(d_u2)
    g_up_fc2[...] = mm(transpose_small(u_fc2), d_ffn).astype(BF)
    u_fc1_t = transpose_small(u_fc1)

    def before_back(i):
        cols = slice(i * hidden_block, (i + 1) * hidden_block)
        return mm_nt(d_ffn, w2[cols, :]) + mm(d_u2, down_fc2[:, cols])

    d_hidden = before_back(0)
    u_sum = None
    for i in range(blocks):
        cols = slice(i * hidden_block, (i + 1) * hidden_block)
        following = before_back(i + 1) if i + 1 < blocks else None
        d_pre = (d_hidden * slope[:, cols]).astype(BF)
        g_down_fc2[:, cols] = mm(d_u2_t, hidden[:, cols]).astype(BF)
        g_up_fc1[:, cols] = mm(u_fc1_t, d_pre).astype(BF)
        total[...] += mm_nt(d_pre, w1[:, cols])
        part = mm_nt(d_pre, up_fc1[:, cols])
        u_sum = part if u_sum is None else u_sum + part
        d_hidden = following
    d_u1 = u_sum.astype(BF)
    d_normed = total[...] + mm(d_u1, down_fc1[...])
    g_down_fc1[...] = mm(transpose_small(d_u1), low_rows[...]).astype(BF)
    d_first = normalize_back(d_normed * gain1[...].astype(F32), normal1[...], scale1)
    dy1_ref[...] = d_first
    d_a = d_first.astype(BF)
    d_uo = mm_nt(d_a, up_out[...]).astype(BF)
    g_up_out[...] = mm(transpose_small(u_out), d_a).astype(BF)
    g_down_out[...] = mm(transpose_small(d_uo), att).astype(BF)
    d_att = (mm_nt(d_a, wo[...]) + mm(d_uo, down_out[...])).astype(BF)
    width = model // cuts
    for k in range(cuts):
        d_att_refs[k][...] = d_att[:, k * width : (k + 1) * width]


def middle(perm, att, x, cot, wo, w1, w2, adapters, norms):
    rows, model = x.shape
    units = w1.shape[1] * w1.shape[3]
    rank = adapters[0].shape[0]
    cuts = perm.shape[0]
    hidden_block = min(512, w1.shape[3])
    vmem = pl.BlockSpec(memory_space=pltpu.VMEM)
    anywhere = pl.BlockSpec(memory_space=pl.ANY)
    wide = jax.ShapeDtypeStruct((rank, units), BF)
    narrow = jax.ShapeDtypeStruct((rank, model), BF)
    out_shape = (
        [jax.ShapeDtypeStruct((rows, model), BF), jax.ShapeDtypeStruct((rows, model), F32)]
        + [jax.ShapeDtypeStruct((rows, model // cuts), BF)] * cuts
        + [narrow, wide, wide, narrow, narrow, narrow]
    )
    return pl.pallas_call(
        functools.partial(middle_kernel, cuts, hidden_block),
        in_specs=[pl.BlockSpec(memory_space=pltpu.SMEM)]
        + [vmem] * 3
        + [anywhere] * 3
        + [vmem] * 10,
        out_specs=[vmem] * len(out_shape),
        out_shape=out_shape,
        scratch_shapes=[
            pltpu.VMEM((model, model), BF),
            pltpu.VMEM((model, units), BF),
            pltpu.VMEM((units, model), BF),
            pltpu.VMEM((rows, units), BF),
            pltpu.VMEM((rows, units), F32),
            pltpu.VMEM((rows, model), F32),
            pltpu.VMEM((rows, model), F32),
            pltpu.VMEM((rows, model), BF),
            pltpu.VMEM((rows, model), F32),
            pltpu.SemaphoreType.DMA,
            pltpu.SemaphoreType.DMA((w1.shape[1],)),
            pltpu.SemaphoreType.DMA((w2.shape[1],)),
        ],
        compiler_params=pltpu.CompilerParams(vmem_limit_bytes=VMEM_LIMIT),
        cost_estimate=pl.CostEstimate(
            flops=2 * rows * model * (2 * model + 4 * units),
            bytes_accessed=2 * model * (model + 2 * units),
            transcendentals=2 * rows * units,
        ),
        name="middle",
    )(perm, att, x, cot, wo, w1, w2, *adapters, *norms)


def blocks_or_whole(gathered, rows_axis):
    outer, inner, height, width = gathered.shape
    if width % 128 == 0:
        return gathered
    if rows_axis == "dp":
        whole = gathered.transpose(0, 2, 1, 3).reshape(outer * height, inner * width)
    else:
        whole = gathered.transpose(1, 2, 0, 3).reshape(inner * height, outer * width)
    return whole[None, None]


def shards(
    inputs, cotangent, lengths, adapter_index, w_qkv, w_out, w_fc1, w_fc2,
    ln1_gain, ln1_bias, ln2_gain, ln2_bias, down_qkv, up_qkv, down_out, up_out,
    down_fc1, up_fc1, down_fc2, up_fc2,
):
    n_dp = lax.axis_size("dp")
    n_t = lax.axis_size("tensor")
    every = ("dp", "tensor")
    mine = lax.axis_index("tensor")
    rows, model = inputs.shape
    length = rows * n_t
    n_set = down_qkv.shape[1]
    rank = down_qkv.shape[3]
    r_dp = rank // n_dp
    r_t = rank // n_t
    d_dp = model // n_dp
    c_t = model // n_t
    f_t = w_fc1.shape[1]
    f_all = f_t * n_t

    def swap(value, bit):
        return lax.ppermute(value, "tensor", [(i, i ^ bit) for i in range(n_t)])

    bits = []
    bit = n_t // 2
    while bit:
        bits.append(bit)
        bit //= 2
    order = [0]
    for bit in bits:
        order = order + [k ^ bit for k in order]
    perm = jnp.array(order, jnp.int32) ^ mine

    rows_all = inputs
    for bit in bits:
        rows_all = jnp.concatenate([rows_all, swap(rows_all, bit)], axis=0)
    w_qkv_all = lax.all_gather(w_qkv, "dp", axis=0)
    wo_all = lax.all_gather(w_out, every, axis=0)
    w1_all = lax.all_gather(w_fc1, every, axis=0)
    w2_all = lax.all_gather(w_fc2, every, axis=0)

    index_all = lax.all_gather(adapter_index, "dp", axis=0, tiled=True)
    onehot_all = (index_all[:, None] == jnp.arange(n_set, dtype=jnp.int32)[None, :]).astype(BF)

    def part_of_rank(value, axis):
        return lax.dynamic_slice_in_dim(value, mine * r_t, r_t, axis)

    tables = [
        part_of_rank(down_qkv.transpose(1, 0, 3, 2), 2),
        up_qkv.transpose(1, 0, 2, 3),
        down_out.transpose(0, 2, 1),
        part_of_rank(up_out, 1),
        part_of_rank(down_fc1.transpose(0, 2, 1), 1),
        up_fc1,
        down_fc2.transpose(0, 2, 1),
        part_of_rank(up_fc2, 1),
    ]
    sizes = [t.size // n_set for t in tables]
    table = jnp.concatenate([t.reshape(n_set, -1) for t in tables], axis=1)
    chosen = mm(onehot_all, table).astype(BF)
    norm_part = jnp.stack([ln1_gain, ln1_bias, ln2_gain, ln2_bias]).reshape(1, -1)
    chosen = jnp.concatenate([chosen, jnp.broadcast_to(norm_part, (n_dp, norm_part.size))], axis=1)
    sent = jnp.broadcast_to(chosen[:, None, :], (n_dp, n_t, chosen.shape[1])).reshape(n_dp * n_t, -1)
    came = lax.all_to_all(sent, every, 0, 0, tiled=True).reshape(n_dp, n_t, -1)
    pieces = []
    start = 0
    for size in sizes:
        pieces.append(came[:, :, start : start + size])
        start += size
    norms = came[:, 0, start:].reshape(n_dp, 4, d_dp).transpose(1, 0, 2).reshape(4, 1, model)

    def from_rank_parts(piece):
        return piece.reshape(n_dp, n_t, r_t, d_dp).transpose(1, 2, 0, 3).reshape(rank, model)

    def from_blocks(piece, width):
        return piece.reshape(n_dp, n_t, r_dp, width).transpose(0, 2, 1, 3).reshape(rank, n_t * width)

    sel_down_qkv = (
        pieces[0].reshape(n_dp, n_t, 3, r_t, d_dp).transpose(2, 1, 3, 0, 4).reshape(3 * rank, model)
    )
    up_mine = lax.dynamic_index_in_dim(pieces[1], mine, 1, keepdims=False)
    sel_up_qkv = up_mine.reshape(n_dp, 3, r_dp, c_t).transpose(1, 0, 2, 3).reshape(3, rank, c_t)

    def reorder(value):
        cols = value.reshape(rank, n_t, c_t)
        return jnp.concatenate(
            [lax.dynamic_index_in_dim(cols, perm[k], 1, keepdims=False) for k in range(n_t)], axis=1
        )

    where = jnp.array([order.index(k) for k in range(n_t)], jnp.int32)

    def restore(value):
        cols = value.reshape(rank, n_t, c_t)
        return jnp.concatenate(
            [
                lax.dynamic_index_in_dim(cols, where[k ^ mine], 1, keepdims=False)
                for k in range(n_t)
            ],
            axis=1,
        )

    adapters = [
        reorder(from_blocks(pieces[2], c_t)),
        from_rank_parts(pieces[3]),
        from_rank_parts(pieces[4]),
        from_blocks(pieces[5], f_t),
        from_blocks(pieces[6], f_t),
        from_rank_parts(pieces[7]),
    ]

    w_cols = w_qkv_all.transpose(1, 0, 2, 3).reshape(3, model, c_t)
    u_in = mm_nt(rows_all, sel_down_qkv).astype(BF)
    qkv = [
        (mm(rows_all, w_cols[j]) + mm(u_in[:, j * rank : (j + 1) * rank], sel_up_qkv[j])).astype(BF)
        for j in range(3)
    ]
    segments = segment_ids(lengths[0], length).reshape(n_t, rows)
    segments = jnp.concatenate(
        [lax.dynamic_index_in_dim(segments, perm[k], 0, keepdims=False) for k in range(n_t)]
    )
    heads = c_t // HD
    group_heads = 2 if heads % 2 == 0 else 1
    groups = heads // group_heads
    kept = []
    att_parts = [[] for _ in range(n_t)]
    for g in range(groups):
        att, e, row_sum = attend_forward(*qkv, segments, g, group_heads)
        kept.append((att, e, row_sum))
        for k in range(n_t):
            block = att[k * rows : (k + 1) * rows]
            att_parts[k].append(block if order[k] == 0 else swap(block, order[k]))
    att_own = jnp.concatenate([part for parts in att_parts for part in parts], axis=1)

    wo_blocks = wo_all.reshape(n_dp, n_t, c_t, d_dp)
    if d_dp % 128 == 0:
        wo_blocks = blocks_or_whole(wo_blocks, "tensor")
    else:
        wo_blocks = blocks_or_whole(jnp.take(wo_blocks, perm, axis=1), "tensor")
    w1_blocks = blocks_or_whole(w1_all.reshape(n_dp, n_t, d_dp, f_t), "dp")
    w2_blocks = blocks_or_whole(w2_all.reshape(n_dp, n_t, f_t, d_dp), "tensor")
    if w1_blocks.shape[1] != w2_blocks.shape[1]:
        w1_blocks = (
            w1_all.reshape(n_dp, n_t, d_dp, f_t)
            .transpose(0, 2, 1, 3)
            .reshape(1, 1, model, f_all)
        )
    done = middle(
        perm, att_own, inputs, cotangent, wo_blocks, w1_blocks, w2_blocks, adapters, list(norms)
    )
    output, d_first = done[0:2]
    d_att_blocks = done[2 : 2 + n_t]
    g_up_fc2, g_down_fc2, g_up_fc1, g_down_fc1, g_up_out, g_down_out = done[2 + n_t :]

    def share_cols(value):
        lead = value.size // model
        return (
            value.reshape(lead, n_dp, n_t, model // (n_dp * n_t))
            .transpose(1, 2, 0, 3)
            .reshape(n_dp * n_t, -1)
        )

    def share_blocks(value):
        width = value.shape[1] // n_t
        return (
            value.reshape(n_dp, r_dp, n_t, width).transpose(0, 2, 1, 3).reshape(n_dp * n_t, -1)
        )

    def exchange(parts):
        widths = [p.shape[1] for p in parts]
        got = lax.all_to_all(jnp.concatenate(parts, axis=1), every, 0, 0, tiled=True)
        return got, widths

    early, early_widths = exchange(
        [
            share_blocks(restore(g_down_out)),
            share_cols(g_up_out),
            share_cols(g_down_fc1),
            share_blocks(g_up_fc1),
            share_blocks(g_down_fc2),
            share_cols(g_up_fc2),
        ]
    )

    d_att_all = jnp.concatenate(
        [
            d_att_blocks[k] if order[k] == 0 else swap(d_att_blocks[k], order[k])
            for k in range(n_t)
        ],
        axis=0,
    )
    grads = [
        attend_backward(*qkv, kept[g][0], d_att_all, kept[g][1], kept[g][2], g, group_heads)
        for g in range(groups)
    ]
    d_qkv = [jnp.concatenate([grads[g][j] for g in range(groups)], axis=1) for j in range(3)]
    d_u_in = jnp.concatenate([mm_nt(d_qkv[j], sel_up_qkv[j]) for j in range(3)], axis=1).astype(BF)

    def rows_part(begin, end):
        part = mm(d_u_in[begin:end], sel_down_qkv)
        for j in range(3):
            part = part + mm_nt(d_qkv[j][begin:end], w_cols[j])
        return part

    span = length
    parts = None
    for bit in reversed(bits):
        half = span // 2
        if parts is None:
            far = swap(rows_part(half, span).astype(BF), bit)
            parts = rows_part(0, half) + far.astype(F32)
        else:
            far = swap(parts[half:].astype(BF), bit)
            parts = parts[:half] + far.astype(F32)
        span = half
    if parts is None:
        parts = rows_part(0, length)
    grad_input = d_first + parts

    tn = (((0,), (0,)), ((), ()))
    g_up_qkv = jnp.stack(
        [
            lax.dot_general(
                u_in[:, j * rank : (j + 1) * rank], d_qkv[j], tn, preferred_element_type=F32
            )
            for j in range(3)
        ]
    ).astype(BF)
    g_down_qkv = lax.dot_general(d_u_in, rows_all, tn, preferred_element_type=F32).astype(BF)
    up_share = (
        g_up_qkv.reshape(3, n_dp, r_dp, c_t).transpose(1, 0, 2, 3).reshape(n_dp, 1, -1)
    )
    up_share = jnp.broadcast_to(up_share, (n_dp, n_t, up_share.shape[2])).reshape(n_dp * n_t, -1)
    late, late_widths = exchange([share_cols(g_down_qkv), up_share])

    by_sender = jnp.broadcast_to(onehot_all[:, None, :], (n_dp, n_t, n_set)).reshape(-1, n_set)
    same_cols = (jnp.arange(n_dp * n_t, dtype=jnp.int32) % n_t == mine).astype(BF)

    def total(got, weights):
        return lax.dot_general(weights, got, tn, preferred_element_type=F32)

    early_sum = total(early, by_sender)
    pieces = []
    start = 0
    for width in early_widths:
        pieces.append(early_sum[:, start : start + width])
        start += width
    d_all = model // (n_dp * n_t)
    sum_down_out = pieces[0].reshape(n_set, r_dp, c_t).transpose(0, 2, 1)
    sum_up_out = pieces[1].reshape(n_set, rank, d_all)
    sum_down_fc1 = pieces[2].reshape(n_set, rank, d_all).transpose(0, 2, 1)
    sum_up_fc1 = pieces[3].reshape(n_set, r_dp, f_t)
    sum_down_fc2 = pieces[4].reshape(n_set, r_dp, f_t).transpose(0, 2, 1)
    sum_up_fc2 = pieces[5].reshape(n_set, rank, d_all)
    sum_down_qkv = (
        total(late[:, : late_widths[0]], by_sender)
        .reshape(n_set, 3, rank, d_all)
        .transpose(1, 0, 3, 2)
    )
    sum_up_qkv = (
        total(late[:, late_widths[0] :], by_sender * same_cols[:, None])
        .reshape(n_set, 3, r_dp, c_t)
        .transpose(1, 0, 2, 3)
    )
    return (
        output,
        grad_input,
        sum_down_qkv,
        sum_up_qkv,
        sum_down_out,
        sum_up_out,
        sum_down_fc1,
        sum_up_fc1,
        sum_down_fc2,
        sum_up_fc2,
    )


def solution(mesh):
    both = ("dp", "tensor")
    in_specs = (
        P(both, None),
        P(both, None),
        P("dp", None),
        P("dp"),
        P(None, "dp", "tensor"),
        P("tensor", "dp"),
        P("dp", "tensor"),
        P("tensor", "dp"),
        P("dp"),
        P("dp"),
        P("dp"),
        P("dp"),
        P(None, None, "dp", None),
        P(None, None, "dp", "tensor"),
        P(None, "tensor", "dp"),
        P(None, None, "dp"),
        P(None, "dp", None),
        P(None, "dp", "tensor"),
        P(None, "tensor", "dp"),
        P(None, None, "dp"),
    )
    out_specs = (
        P(both, None),
        P(both, None),
        P(None, None, both, None),
        P(None, None, "dp", "tensor"),
        P(None, "tensor", "dp"),
        P(None, None, both),
        P(None, both, None),
        P(None, "dp", "tensor"),
        P(None, "tensor", "dp"),
        P(None, None, both),
    )
    return jax.shard_map(shards, mesh=mesh, in_specs=in_specs, out_specs=out_specs, check_vma=False)
```

time: 1790 us -> 503 us (0.28)
  waiting for transfers between devices: 866 us -> 167 us
  blocking collectives: 360 us -> 13.3 us
  matrix products: 337 us -> 56.4 us
  Pallas kernels: 0 us -> 131 us
  other arithmetic: 99 us -> 18.2 us
  local copies, waits for them, and re-layouts: 86 us -> 56.3 us
  starting transfers between devices: 1.35 us -> 23.2 us
    unnamed x27 -> x4, waiting for transfers between devices: 501 us -> 2.58 us
    all_gather x17 -> x0, blocking collectives: 360 us -> none  [the longest x1 33.3 us: shards(): lax.all_gather(up_fc1, 'dp', axis=1, tiled=True)]
    reduce_scatter x12 -> x0, waiting for transfers between devices: 313 us -> none  [the longest x1 62.5 us: shards(): lax.psum_scatter(spread_set(set_onehot, grad_up_fc1, 0).astype(jnp.bfloat...]
    dot_general x68 -> x26, matrix products: 337 us -> 56.4 us  [the longest x9 28.3 us: mm(): return jnp.dot(left, right, preferred_element_type=F32)]
    pallas_call x0 -> x5, Pallas kernels: none -> 131 us  [the longest x1 45.5 us: middle(): pl.pallas_call(functools.partial(middle_kernel, cuts, hidden_block), in_s...]
    convert_element_type x17 -> x2, other arithmetic: 68.4 us -> 0.08 us  [the longest x1 0.07 us: shards(): (index_all[:, None] == jnp.arange(n_set, dtype=jnp.int32)[None, :]).astyp...]
    all_gather x7 -> x4, waiting for transfers between devices: 51.5 us -> 119 us  [the longest x1 78.9 us: shards(): w2_all = lax.all_gather(w_fc2, every, axis=0)]
    ppermute x0 -> x13, waiting for transfers between devices: none -> 45.9 us  [swap(): return lax.ppermute(value, 'tensor', [(i, i ^ bit) for i in range(n_t)])]
  transfers between devices with their start and end apart: 23 -> 20, of which waited for: 14 -> 9; matrix products, arithmetic and copies ran while one was open for 8% -> 18% of each run, Pallas kernels for 0% -> 8%
where the time goes in v1:
time: 503 us; the launch traced here: 496 us
  waiting for transfers between devices  167 us (33%)
  Pallas kernels  131 us (26%)
  matrix products  56.4 us (11%)
  local copies, waits for them, and re-layouts  56.3 us (11%)
  between operations  31.4 us (6%)
  starting transfers between devices  23.2 us (5%)
  other arithmetic  18.2 us (4%)
  blocking collectives  13.3 us (3%)
    all_gather x1, waiting for transfers between devices, shards(): w2_all = lax.all_gather(w_fc2, every, axis=0)  78.9 us
    ppermute x13, waiting for transfers between devices, swap(): return lax.ppermute(value, 'tensor', [(i, i ^ bit) for i in range(n_t)])  45.9 us
    pallas_call x1, Pallas kernels, middle(): pl.pallas_call(functools.partial(middle_kernel, cuts, hidden_block), in_s...  45.5 us
    pallas_call x2, Pallas kernels, attend_backward(): pl.pallas_call(functools.partial(attend_backward_kernel, heads, block, ch...  45.5 us
    pallas_call x2, Pallas kernels, attend_forward(): pl.pallas_call(functools.partial(attend_forward_kernel, heads, block, chu...  39.6 us
    all_gather x1, waiting for transfers between devices, shards(): w1_all = lax.all_gather(w_fc1, every, axis=0)  39.6 us
    dot_general x9, matrix products, mm(): return jnp.dot(left, right, preferred_element_type=F32)  28.3 us
    unnamed x110, local copies, waits for them, and re-layouts  23.9 us
  transfers between devices with their start and end apart: 20, of which 9 were waited for; matrix products, arithmetic and copies ran while one was open for 18% of the time, Pallas kernels for 8%

profile of v1, /device:TPU:0, one launch (start us, length us, event | category | flops | bytes accessed | tf_op | source)
XLA Modules:
  0.0 496.5 jit_solution(17634921625600151295)
XLA Ops:
  12.7 13.3 %all-reduce = s32[8]{0:T(128)S(1)} all-reduce(s32[8]{0:T(128)S(1)} %dynamic-update-slice), channel_id=1, replica_groups=mesh['dp'=8,'tensor'=4] {'dp'}, use_global_device_ids=true, to_apply=%add | all-reduce | flops 8 | bytes 64
  33.6 4.4 reduce.3
  39.0 3.2 all-to-all-start
  42.2 1.9 collective-permute-start
  58.7 1.3 copy.205.segk_ref
  63.9 10.3 %collective-permute-done = bf16[512,1024]{1,0:T(8,128)(2,1)S(1)} collective-permute-done((bf16[512,1024]{1,0:T(8,128)(2,1)S(1)}, bf16[512,1024]{1,0:T(8,128)(2,1)S(1)}, u32[]{:S(2)}, u32[]{:S(2)}) %collective-permute-start) | collective-permute-done | bytes 1048608 | tf_op jit(solution)/shard_map/ppermute | solution.py:456
  74.2 1.5 pad_maximum_fusion
  77.3 3.7 reduce
  83.9 1.5 fusion.44
  85.4 3.7 constant_dynamic-update-slice_fusion
  89.1 3.6 convolution_convert_fusion.1
  94.1 4.6 fusion.2.v_ref
  98.7 4.5 fusion.1.k_ref
  103.2 4.5 fusion.q_ref
  107.8 19.9 %attend_forward.2 = (bf16[2048,128]{1,0:T(8,128)(2,1)}, bf16[2,4,2048,512]{3,2,1,0:T(8,128)(2,1)}, f32[2,4,8,512]{3,2,1,0:T(8,128)}) custom-call(bf16[2048,256]{1,0:T(8,128)(2,1)} %fusion.q_ref, bf16[2048,256]{1,0:T(8,128)(2,1)} %fusion.1.k_ref, bf16[2048,256]{1,0:T(8,128)(2,1)} %fusion.2.v_ref, s32[1,2048]{1,0:T(1,128)} %bitcast.298, s32[2048,1]{1,0:T(8,128)} %copy.205.segk_ref), custom_call_target="tpu_custom_call" | custom-call | flops 8589934592 | bytes 16777216 | tf_op jit(solution)/shard_map/attend_forward/pallas_call | solution.py:91
  129.5 19.7 %attend_forward.3 = (bf16[2048,128]{1,0:T(8,128)(2,1)}, bf16[2,4,2048,512]{3,2,1,0:T(8,128)(2,1)}, f32[2,4,8,512]{3,2,1,0:T(8,128)}) custom-call(bf16[2048,256]{1,0:T(8,128)(2,1)} %fusion.q_ref, bf16[2048,256]{1,0:T(8,128)(2,1)} %fusion.1.k_ref, bf16[2048,256]{1,0:T(8,128)(2,1)} %fusion.2.v_ref, s32[1,2048]{1,0:T(1,128)} %bitcast.299, s32[2048,1]{1,0:T(8,128)} %copy.205.segk_ref), custom_call_target="tpu_custom_call" | custom-call | flops 8589934592 | bytes 16777216 | tf_op jit(solution)/shard_map/attend_forward/pallas_call | solution.py:91
  150.3 1.5 collective-permute-start.3
  155.2 1.5 collective-permute-start.7
  156.8 1.5 collective-permute-done.3
  158.5 4.1 collective-permute-done.6
  162.6 2.8 collective-permute-done.7
  165.5 39.6 %all-gather.13.cloned.1.call-done = bf16[4096,1024]{1,0:T(8,128)(2,1)} async-done(((bf16[128,1024]{1,0:T(8,128)(2,1)}), bf16[4096,1024]{1,0:T(8,128)(2,1)}) %all-gather.13.cloned.1.call-update) | async-done | bytes 8388624 | tf_op jit(solution)/shard_map/all_gather | solution.py:473
  205.0 78.9 %all-gather.15.cloned.1.call-done = bf16[32768,128]{1,0:T(8,128)(2,1)} async-done(((bf16[1024,128]{1,0:T(8,128)(2,1)}), bf16[32768,128]{1,0:T(8,128)(2,1)}) %all-gather.15.cloned.1.call-update) | async-done | bytes 8388624 | tf_op jit(solution)/shard_map/all_gather | solution.py:474
  283.9 45.5 %middle.1 = (bf16[512,1024]{1,0:T(8,128)(2,1)}, f32[512,1024]{1,0:T(8,128)}, bf16[512,256]{1,0:T(8,128)(2,1)}, bf16[512,256]{1,0:T(8,128)(2,1)}, bf16[512,256]{1...) custom-call(s32[4]{0:T(128)} %copy-done.25, ...), custom_call_target="tpu_custom_call" | custom-call | flops 19327352832 | bytes 18874368 | tf_op jit(solution)/shard_map/middle/pallas_call | solution.py:392
  336.0 1.5 collective-permute-start.8
  340.6 4.8 collective-permute-done.8
  345.5 4.2 collective-permute-done.10
  350.7 22.7 %attend_backward.2 = (bf16[2048,128]{1,0:T(8,128)(2,1)}, bf16[2048,128]{1,0:T(8,128)(2,1)}, bf16[2048,128]{1,0:T(8,128)(2,1)}) custom-call(bf16[2048,256]{1,0:T(8,128)(2,1)} %fusion.q_ref, bf16[2048,256]{1,0:T(8,128)(2,1)} %fusion.1.k_ref, bf16[2048,256]{1,0:T(8,128)(2,1)} %fusion.2.v_ref, bf16[2048,128]{1,0:T(8,128)(2,1)} %get-tuple-element.34.o_ref, ...), custom_call_target="tpu_custom_call" | custom-call | flops 17179869184 | bytes 16777216 | tf_op jit(solution)/shard_map/attend_backward/pallas_call | solution.py:196
  374.5 22.8 %attend_backward.3 = (bf16[2048,128]{1,0:T(8,128)(2,1)}, bf16[2048,128]{1,0:T(8,128)(2,1)}, bf16[2048,128]{1,0:T(8,128)(2,1)}) custom-call(bf16[2048,256]{1,0:T(8,128)(2,1)} %fusion.q_ref, bf16[2048,256]{1,0:T(8,128)(2,1)} %fusion.1.k_ref, bf16[2048,256]{1,0:T(8,128)(2,1)} %fusion.2.v_ref, bf16[2048,128]{1,0:T(8,128)(2,1)} %get-tuple-element.35.o_ref, ...), custom_call_target="tpu_custom_call" | custom-call | flops 17179869184 | bytes 16777216 | tf_op jit(solution)/shard_map/attend_backward/pallas_call | solution.py:196
  401.1 3.7 convolution_convert_fusion.5
  405.5 2.8 fusion.8
  408.3 2.7 fusion.6
  411.1 2.7 fusion.4
  415.8 2.0 reshape.332
  418.0 6.8 %add_convert_fusion = bf16[1024,1024]{1,0:T(8,128)(2,1)} fusion(f32[1024,1024]{1,0:T(8,128)} %fusion.4, f32[1024,1024]{1,0:T(8,128)} %fusion.6, f32[1024,1024]{1,0:T(8,128)} %fusion.8, bf16[2048,48]{0,1:T(8,128)(2,1)} %pad_maximum_fusion.1, bf16[6,8,8,128]{3,2,1,0:T(8,128)(2,1)S(1)} %bitcast.260), kind=kOutput, calls=%fused_computation.2 | convolution fusion | flops 104857600 | bytes 14876672 | tf_op jit(solution)/shard_map/dot_general | solution.py:20
  425.2 1.4 reduce.4
  426.6 1.7 reshape.375
  428.4 3.2 all-to-all-start.1
  431.6 3.9 fusion.14
  435.4 2.8 fusion.12
  438.2 2.8 fusion.10
  441.7 5.8 %all-to-all-start.2 = ((bf16[32,2,3072]{2,1,0:T(2,128)(2,1)}), bf16[32,2,3072]{2,1,0:T(2,128)(2,1)S(1)}, u32[]{:S(2)}, u32[]{:S(2)}) async-start(bf16[32,2,3072]{2,1,0:T(2,128)(2,1)} %reshape.377), calls=%async_computation.2 | async-start | bytes 786432 | tf_op jit(solution)/shard_map/all_to_all | solution.py:604
  447.5 1.6 reshape.376
  450.9 6.3 %convert_add_fusion = f32[1024,1024]{1,0:T(8,128)S(1)} fusion(bf16[1024,1024]{1,0:T(8,128)(2,1)} %collective-permute-done.11, f32[1024,1024]{1,0:T(8,128)} %fusion.10, f32[1024,1024]{1,0:T(8,128)} %fusion.12, f32[1024,1024]{1,0:T(8,128)} %fusion.14, bf16[2048,48]{0,1:T(8,128)(2,1)S(1)} %copy-done.13, bf16[6,8,8,128]{3,2,1,0:T(8,128)(2,1)S(1)} %bitcast.261), kind=kOutput, calls=%fused_computation.1 | convolution fusion | flops 105906176 | bytes 19070976 | tf_op jit(solution)/shard_map/dot_general | solution.py:20
  457.2 2.0 copy-done.2
  460.3 1.8 collective-permute-start.12
  467.7 18.2 %collective-permute-done.12 = bf16[512,1024]{1,0:T(8,128)(2,1)} collective-permute-done((bf16[512,1024]{1,0:T(8,128)(2,1)}, bf16[512,1024]{1,0:T(8,128)(2,1)}, u32[]{:S(2)}, u32[]{:S(2)}) %collective-permute-start.12) | collective-permute-done | bytes 1048608 | tf_op jit(solution)/shard_map/ppermute | solution.py:456
  485.9 3.7 fusion.3
  (248 shorter events, 56.0 us)
Async XLA Ops:
  7.2 18.9 %copy-start = (bf16[3,8,128,16]{2,3,1,0:T(8,128)(2,1)S(1)}, bf16[3,8,128,16]{2,3,1,0:T(8,128)(2,1)}, u32[]{:S(2)}) copy-start(bf16[3,8,128,16]{2,3,1,0:T(8,128)(2,1)} %param.34) | copy-start | bytes 294916
  7.2 76.7 %all-gather.9.cloned.1.call-start = ((), (), s32[]{:S(2)}) async-start(), calls=%async_computation.3 | async-start | bytes 1769472 | tf_op jit(solution)/shard_map/all_gather | solution.py:471
  7.9 157.5 %all-gather.11.cloned.1.call-start = ((), (), s32[]{:S(2)}) async-start(), calls=%async_computation.4 | async-start | bytes 2162688 | tf_op jit(solution)/shard_map/all_gather | solution.py:472
  8.7 196.4 %all-gather.13.cloned.1.call-start = ((), (), s32[]{:S(2)}) async-start(), calls=%async_computation.5 | async-start | bytes 8650752 | tf_op jit(solution)/shard_map/all_gather | solution.py:473
  9.4 274.5 %all-gather.15.cloned.1.call-start = ((), (), s32[]{:S(2)}) async-start(), calls=%async_computation.6 | async-start | bytes 8650752 | tf_op jit(solution)/shard_map/all_gather | solution.py:474
  10.6 31.6 %copy-start.11 = (bf16[512,1024]{1,0:T(8,128)(2,1)S(1)}, bf16[512,1024]{1,0:T(8,128)(2,1)}, u32[]{:S(2)}) copy-start(bf16[512,1024]{1,0:T(8,128)(2,1)} %x_ref.1) | copy-start | bytes 3145732
  10.6 33.5 %copy-start.24 = (s32[4]{0:T(128)S(1)}, s32[4]{0:T(128)}, u32[]{:S(2)}) copy-start(s32[4]{0:T(128)} %constant.66.clone) | copy-start | bytes 52
  26.1 29.7 %copy-start.26 = (s32[1,8]{1,0:T(1,128)S(1)}, s32[1,8]{1,0:T(1,128)}, u32[]{:S(2)}) copy-start(s32[1,8]{1,0:T(1,128)} %param.24) | copy-start | bytes 100
  39.0 37.8 %all-to-all-start = ((bf16[32,2,4864]{2,1,0:T(2,128)(2,1)}), bf16[32,2,4864]{2,1,0:T(2,128)(2,1)S(1)}, u32[]{:S(2)}, u32[]{:S(2)}) async-start(bf16[32,2,4864]{2,1,0:T(2,128)(2,1)} %reshape.373), calls=%async_computation | async-start | bytes 1245184 | tf_op jit(solution)/shard_map/all_to_all | solution.py:498
  42.2 32.0 %collective-permute-start = (bf16[512,1024]{1,0:T(8,128)(2,1)S(1)}, bf16[512,1024]{1,0:T(8,128)(2,1)S(1)}, u32[]{:S(2)}, u32[]{:S(2)}) collective-permute-start(bf16[512,1024]{1,0:T(8,128)(2,1)S(1)} %copy-done.11), channel_id=1, source_target_pairs={{0,2},{1,3},{2,0},{3,1},{4,6},{5,7},{6,4},{7,5},{8,10},{9,11},{10,... | collective-permute-start | bytes 3145736 | tf_op jit(solution)/shard_map/ppermute | solution.py:456
  44.2 32.6 %copy-start.25 = (s32[4]{0:T(128)}, s32[4]{0:T(128)S(1)}, u32[]{:S(2)}) copy-start(s32[4]{0:T(128)S(1)} %broadcast_xor_fusion.perm_ref) | copy-start | bytes 52
  58.7 18.0 %copy-start.21 = (s32[2048]{0:T(1024)}, s32[2048]{0:T(1024)S(1)}, u32[]{:S(2)}) copy-start(s32[2048]{0:T(1024)S(1)} %pad_add_fusion) | copy-start | bytes 24580
  75.7 9.7 %collective-permute-start.1 = (bf16[1024,1024]{1,0:T(8,128)(2,1)}, bf16[1024,1024]{1,0:T(8,128)(2,1)}, u32[]{:S(2)}, u32[]{:S(2)}) collective-permute-start(bf16[1024,1024]{1,0:T(8,128)(2,1)} %pad_maximum_fusion), channel_id=1, source_target_pairs={{0,1},{1,0},{2,3},{3,2},{4,5},{5,4},{6,7},{7,6},{8,9},{9,8},{10,11... | collective-permute-start | bytes 6291464 | tf_op jit(solution)/shard_map/ppermute | solution.py:456
  85.4 8.7 %copy-start.3 = (bf16[1,8,128,256]{3,2,0,1:T(8,128)(2,1)}, bf16[1,8,128,256]{3,2,0,1:T(8,128)(2,1)S(1)}, u32[]{:S(2)}) copy-start(bf16[1,8,128,256]{3,2,0,1:T(8,128)(2,1)S(1)} %get-tuple-element.118) | copy-start | bytes 1572868
  85.4 13.3 %copy-start.6 = (bf16[1,8,128,256]{3,2,0,1:T(8,128)(2,1)}, bf16[1,8,128,256]{3,2,0,1:T(8,128)(2,1)S(1)}, u32[]{:S(2)}) copy-start(bf16[1,8,128,256]{3,2,0,1:T(8,128)(2,1)S(1)} %get-tuple-element.119) | copy-start | bytes 1572868
  85.4 17.8 %copy-start.9 = (bf16[1,8,128,256]{3,2,0,1:T(8,128)(2,1)}, bf16[1,8,128,256]{3,2,0,1:T(8,128)(2,1)S(1)}, u32[]{:S(2)}) copy-start(bf16[1,8,128,256]{3,2,0,1:T(8,128)(2,1)S(1)} %get-tuple-element.120) | copy-start | bytes 1572868
  128.9 26.4 %collective-permute-start.2 = (bf16[512,128]{1,0:T(8,128)(2,1)S(1)}, bf16[512,128]{1,0:T(8,128)(2,1)S(1)}, u32[]{:S(2)}, u32[]{:S(2)}) collective-permute-start(bf16[512,128]{1,0:T(8,128)(2,1)S(1)} %get-tuple-element.136), channel_id=1, source_target_pairs={{0,2},{1,3},{2,0},{3,1},{4,6},{5,7},{6,4},{7,5},{8,10},{9,11},{10,... | collective-permute-start | bytes 393224 | tf_op jit(solution)/shard_map/ppermute | solution.py:456
  150.3 8.0 %collective-permute-start.3 = (bf16[512,128]{1,0:T(8,128)(2,1)S(1)}, bf16[512,128]{1,0:T(8,128)(2,1)S(1)}, u32[]{:S(2)}, u32[]{:S(2)}) collective-permute-start(bf16[512,128]{1,0:T(8,128)(2,1)S(1)} %get-tuple-element.132), channel_id=1, source_target_pairs={{0,2},{1,3},{2,0},{3,1},{4,6},{5,7},{6,4},{7,5},{8,10},{9,11},{10,... | collective-permute-start | bytes 393224 | tf_op jit(solution)/shard_map/ppermute | solution.py:456
  154.5 3.8 collective-permute-start.4
  154.5 3.9 collective-permute-start.5
  155.0 7.5 %collective-permute-start.6 = (bf16[512,128]{1,0:T(8,128)(2,1)S(1)}, bf16[512,128]{1,0:T(8,128)(2,1)S(1)}, u32[]{:S(2)}, u32[]{:S(2)}) collective-permute-start(bf16[512,128]{1,0:T(8,128)(2,1)S(1)} %get-tuple-element.134), channel_id=1, source_target_pairs={{0,3},{1,2},{2,1},{3,0},{4,7},{5,6},{6,5},{7,4},{8,11},{9,10},{10,... | collective-permute-start | bytes 393224 | tf_op jit(solution)/shard_map/ppermute | solution.py:456
  155.2 10.1 %collective-permute-start.7 = (bf16[512,128]{1,0:T(8,128)(2,1)S(1)}, bf16[512,128]{1,0:T(8,128)(2,1)S(1)}, u32[]{:S(2)}, u32[]{:S(2)}) collective-permute-start(bf16[512,128]{1,0:T(8,128)(2,1)S(1)} %get-tuple-element.130), channel_id=1, source_target_pairs={{0,3},{1,2},{2,1},{3,0},{4,7},{5,6},{6,5},{7,4},{8,11},{9,10},{10,... | collective-permute-start | bytes 393224 | tf_op jit(solution)/shard_map/ppermute | solution.py:456
  165.4 118.5 %copy-start.23 = (bf16[512,1024]{1,0:T(8,128)(2,1)}, bf16[512,1024]{1,0:T(8,128)(2,1)S(1)}, u32[]{:S(2)}) copy-start(bf16[512,1024]{1,0:T(8,128)(2,1)S(1)} %constant_dynamic-update-slice_fusion.11.att_ref) | copy-start | bytes 3145732
  329.4 8.8 %copy-start.22 = (bf16[16,1024]{1,0:T(8,128)(2,1)S(1)}, bf16[16,1024]{1,0:T(8,128)(2,1)}, u32[]{:S(2)}) copy-start(bf16[16,1024]{1,0:T(8,128)(2,1)} %get-tuple-element.57) | copy-start | bytes 98308
  336.0 9.4 %collective-permute-start.8 = (bf16[512,256]{1,0:T(8,128)(2,1)}, bf16[512,256]{1,0:T(8,128)(2,1)S(1)}, u32[]{:S(2)}, u32[]{:S(2)}) collective-permute-start(bf16[512,256]{1,0:T(8,128)(2,1)} %get-tuple-element.39), channel_id=1, source_target_pairs={{0,2},{1,3},{2,0},{3,1},{4,6},{5,7},{6,4},{7,5},{8,10},{9,11},{10,... | collective-permute-start | bytes 786440 | tf_op jit(solution)/shard_map/ppermute | solution.py:456
  337.6 7.9 %collective-permute-start.9 = (bf16[512,256]{1,0:T(8,128)(2,1)}, bf16[512,256]{1,0:T(8,128)(2,1)S(1)}, u32[]{:S(2)}, u32[]{:S(2)}) collective-permute-start(bf16[512,256]{1,0:T(8,128)(2,1)} %get-tuple-element.40), channel_id=1, source_target_pairs={{0,1},{1,0},{2,3},{3,2},{4,5},{5,4},{6,7},{7,6},{8,9},{9,8},{10,11... | collective-permute-start | bytes 786440 | tf_op jit(solution)/shard_map/ppermute | solution.py:456
  337.6 12.1 %collective-permute-start.10 = (bf16[512,256]{1,0:T(8,128)(2,1)}, bf16[512,256]{1,0:T(8,128)(2,1)S(1)}, u32[]{:S(2)}, u32[]{:S(2)}) collective-permute-start(bf16[512,256]{1,0:T(8,128)(2,1)} %get-tuple-element.41), channel_id=1, source_target_pairs={{0,3},{1,2},{2,1},{3,0},{4,7},{5,6},{6,5},{7,4},{8,11},{9,10},{10,... | collective-permute-start | bytes 786440 | tf_op jit(solution)/shard_map/ppermute | solution.py:456
  349.7 1.0 copy-start.20
  374.5 24.8 %copy-start.16 = (bf16[2048,128]{1,0:T(8,128)(2,1)S(1)}, bf16[2048,128]{1,0:T(8,128)(2,1)}, u32[]{:S(2)}) copy-start(bf16[2048,128]{1,0:T(8,128)(2,1)} %get-tuple-element.48) | copy-start | bytes 1572868
  397.3 2.1 copy-start.18
  397.3 2.8 copy-start.15
  397.3 2.9 copy-start.17
  400.3 5.2 %copy-start.10 = (bf16[1,8,128,256]{3,2,0,1:T(8,128)(2,1)S(1)}, bf16[1,8,128,256]{3,2,0,1:T(8,128)(2,1)}, u32[]{:S(2)}) copy-start(bf16[1,8,128,256]{3,2,0,1:T(8,128)(2,1)} %copy-done.9) | copy-start | bytes 1572868
  401.1 7.2 %copy-start.7 = (bf16[1,8,128,256]{3,2,0,1:T(8,128)(2,1)S(1)}, bf16[1,8,128,256]{3,2,0,1:T(8,128)(2,1)}, u32[]{:S(2)}) copy-start(bf16[1,8,128,256]{3,2,0,1:T(8,128)(2,1)} %copy-done.6) | copy-start | bytes 1572868
  405.5 5.6 %copy-start.4 = (bf16[1,8,128,256]{3,2,0,1:T(8,128)(2,1)S(1)}, bf16[1,8,128,256]{3,2,0,1:T(8,128)(2,1)}, u32[]{:S(2)}) copy-start(bf16[1,8,128,256]{3,2,0,1:T(8,128)(2,1)} %copy-done.3) | copy-start | bytes 1572868
  417.9 7.3 %copy-start.19 = (bf16[32,1536]{1,0:T(8,128)(2,1)S(1)}, bf16[32,1536]{1,0:T(8,128)(2,1)}, u32[]{:S(2)}) copy-start(bf16[32,1536]{1,0:T(8,128)(2,1)} %reshape.332) | copy-start | bytes 294916
  424.7 26.1 %collective-permute-start.11 = (bf16[1024,1024]{1,0:T(8,128)(2,1)}, bf16[1024,1024]{1,0:T(8,128)(2,1)}, u32[]{:S(2)}, u32[]{:S(2)}) collective-permute-start(bf16[1024,1024]{1,0:T(8,128)(2,1)} %add_convert_fusion), channel_id=1, source_target_pairs={{0,1},{1,0},{2,3},{3,2},{4,5},{5,4},{6,7},{7,6},{8,9},{9,8},{10,11... | collective-permute-start | bytes 6291464 | tf_op jit(solution)/shard_map/ppermute | solution.py:456
  428.4 12.7 %all-to-all-start.1 = ((bf16[32,2,1536]{2,1,0:T(2,128)(2,1)}), bf16[32,2,1536]{2,1,0:T(2,128)(2,1)S(1)}, u32[]{:S(2)}, u32[]{:S(2)}) async-start(bf16[32,2,1536]{2,1,0:T(2,128)(2,1)} %reshape.375), calls=%async_computation.1 | async-start | bytes 393216 | tf_op jit(solution)/shard_map/all_to_all | solution.py:604
  431.6 3.9 copy-start.8
  431.6 6.6 %copy-start.5 = (bf16[1,8,128,256]{3,2,0,1:T(8,128)(2,1)S(1)}, bf16[1,8,128,256]{3,2,0,1:T(8,128)(2,1)}, u32[]{:S(2)}) copy-start(bf16[1,8,128,256]{3,2,0,1:T(8,128)(2,1)} %copy-done.3) | copy-start | bytes 1572868
  438.2 12.7 %copy-start.13 = (bf16[2048,48]{0,1:T(8,128)(2,1)S(1)}, bf16[2048,48]{0,1:T(8,128)(2,1)}, u32[]{:S(2)}) copy-start(bf16[2048,48]{0,1:T(8,128)(2,1)} %pad_maximum_fusion.1) | copy-start | bytes 589828
  441.0 0.7 copy-start.14
  441.7 21.2 %all-to-all-start.2 = ((bf16[32,2,3072]{2,1,0:T(2,128)(2,1)}), bf16[32,2,3072]{2,1,0:T(2,128)(2,1)S(1)}, u32[]{:S(2)}, u32[]{:S(2)}) async-start(bf16[32,2,3072]{2,1,0:T(2,128)(2,1)} %reshape.377), calls=%async_computation.2 | async-start | bytes 786432 | tf_op jit(solution)/shard_map/all_to_all | solution.py:604
  457.1 2.0 copy-start.2
  459.1 26.8 %copy-start.12 = (f32[512,1024]{1,0:T(8,128)S(1)}, f32[512,1024]{1,0:T(8,128)}, u32[]{:S(2)}) copy-start(f32[512,1024]{1,0:T(8,128)} %get-tuple-element.37) | copy-start | bytes 6291460
  460.3 25.6 %collective-permute-start.12 = (bf16[512,1024]{1,0:T(8,128)(2,1)}, bf16[512,1024]{1,0:T(8,128)(2,1)}, u32[]{:S(2)}, u32[]{:S(2)}) collective-permute-start(bf16[512,1024]{1,0:T(8,128)(2,1)} %slice.299), channel_id=1, source_target_pairs={{0,2},{1,3},{2,0},{3,1},{4,6},{5,7},{6,4},{7,5},{8,10},{9,11},{10,... | collective-permute-start | bytes 3145736 | tf_op jit(solution)/shard_map/ppermute | solution.py:456
  463.2 26.4 %copy-start.1 = (bf16[3,8,128,16]{2,3,1,0:T(8,128)(2,1)S(1)}, bf16[3,8,128,16]{2,3,1,0:T(8,128)(2,1)}, u32[]{:S(2)}) copy-start(bf16[3,8,128,16]{2,3,1,0:T(8,128)(2,1)} %param.34) | copy-start | bytes 294916
Sparse Core Ops, SparseCore 0:
  10.2 56.3 all-gather.8
  69.5 54.6 all-gather.10
  127.1 77.9 all-gather.12
  207.8 76.1 all-gather.14

commit v2 on v1

v2 whole, which is shorter than its diff:
```python
import functools

import jax
import jax.numpy as jnp
from jax import lax
from jax.experimental import pallas as pl
from jax.experimental.pallas import tpu as pltpu
from jax.sharding import PartitionSpec as P

HD = 64
EPS = 1e-05
NEG = -1000000000.0
LOG2E = 1.4426950408889634
BF = jnp.bfloat16
F32 = jnp.float32
VMEM_LIMIT = 60 * 2**20
BRIEF = pl.CostEstimate(flops=1, bytes_accessed=1, transcendentals=0)


def mm(left, right):
    return jnp.dot(left, right, preferred_element_type=F32)


def mm_nt(left, right):
    return lax.dot_general(left, right, (((1,), (1,)), ((), ())), preferred_element_type=F32)


def transpose_small(value):
    return value.astype(F32).T.astype(BF)


def token_place(index, rows, cuts, mine):
    shift = rows.bit_length() - 1
    bits = cuts.bit_length() - 1
    block = index >> shift
    reverse = jnp.zeros_like(block)
    for i in range(bits):
        reverse = reverse | (((block >> i) & 1) << (bits - 1 - i))
    return ((reverse ^ mine) << shift) | (index & (rows - 1))


def attend_forward_kernel(
    heads, block, chunk, rows, first, kept, cut_range, lengths_ref, q_ref, k_ref, v_ref, *rest
):
    length = k_ref.shape[0]
    cuts = length // rows
    rest = rest[kept:]
    att_ref, e_ref, l_ref = rest[0:3]
    cut_refs = rest[3 : 3 + len(cut_range)]
    keys_wide, values_t, scores = rest[3 + len(cut_range) :]
    mine = lax.axis_index("tensor")
    step = pl.program_id(0) + first
    ends = [lengths_ref[0, 0]]
    for d in range(1, lengths_ref.shape[1]):
        ends.append(ends[-1] + lengths_ref[0, d])

    @pl.when(step == first)
    def _():
        lane = lax.broadcasted_iota(jnp.int32, (1, 128), 1)
        begin = jnp.zeros_like(lane)
        end = jnp.zeros_like(lane)
        for d in range(len(ends)):
            begin = jnp.where(lane == d, ends[d - 1] if d else 0, begin)
            end = jnp.where(lane == d, ends[d], end)
        place = token_place(
            lax.broadcasted_iota(jnp.int32, (length, 128), 0), rows, cuts, mine
        )
        onehot = jnp.where((place >= begin) & (place < end), 1.0, 0.0).astype(BF)
        ones = (lax.broadcasted_iota(jnp.int32, (16, length), 0) == 0).astype(BF)
        flipped = v_ref[...].T
        for h in range(heads):
            key = k_ref[:, h * HD : (h + 1) * HD]
            keys_wide[h, :, 0:HD] = key
            keys_wide[h, :, HD : 2 * HD] = key
            keys_wide[h, :, 2 * HD :] = onehot
            values_t[h, 0:HD, :] = flipped[h * HD : (h + 1) * HD, :]
            values_t[h, HD:, :] = ones

    flipped_q = q_ref[...].astype(F32).T * (HD ** (-0.5) * LOG2E)
    place = token_place(
        lax.broadcasted_iota(jnp.int32, (1, block), 1) + step * block, rows, cuts, mine
    )
    segment = jnp.zeros_like(place)
    for end in ends:
        segment = segment + (place >= end).astype(jnp.int32)
    mask = jnp.where(
        lax.broadcasted_iota(jnp.int32, (128, block), 0) == segment, 0.0, NEG
    ).astype(BF)
    mixed = []
    for h in range(heads):
        query = flipped_q[h * HD : (h + 1) * HD, :]
        high = query.astype(BF)
        low = (query - high.astype(F32)).astype(BF)
        right = jnp.concatenate([high, low, mask], axis=0)
        top = None
        for c in range(length // chunk):
            part = mm(keys_wide[h, c * chunk : (c + 1) * chunk, :], right)
            scores[h, c * chunk : (c + 1) * chunk, :] = part
            part = jnp.max(part.reshape(chunk // 8, 8, block), axis=0)
            top = part if top is None else jnp.maximum(top, part)
        top = jnp.max(top, axis=0, keepdims=True)
        total = None
        for c in range(length // chunk):
            e = jnp.exp2(scores[h, c * chunk : (c + 1) * chunk, :] - top).astype(BF)
            e_ref[h, 0, c * chunk : (c + 1) * chunk, :] = e
            part = mm(values_t[h, :, c * chunk : (c + 1) * chunk], e)
            total = part if total is None else total + part
        row_sum = total[HD : HD + 1, :]
        l_ref[h, 0] = jnp.broadcast_to(row_sum, (8, block))
        mixed.append(total[0:HD, :] / row_sum)
    att = jnp.concatenate(mixed, axis=0).T.astype(BF)
    att_ref[...] = att
    for i, k in enumerate(cut_range):

        @pl.when(step == k * rows // block)
        def _():
            begin = k * rows % block
            cut_refs[i][...] = att[begin : begin + rows, :]


def attend_forward(q, k, v, lengths, group, heads, rows, part, parts, kept):
    length = q.shape[0]
    width = heads * HD
    block = min(512, length)
    chunk = min(512, length)
    count = length // block
    steps = count // parts
    first = part * steps
    per_part = steps * block // rows
    cut_range = range(part * per_part, (part + 1) * per_part)
    own_specs = [
        pl.BlockSpec((block, width), lambda i: (i + first, 0)),
        pl.BlockSpec((heads, 1, length, block), lambda i: (0, i + first, 0, 0)),
        pl.BlockSpec((heads, 1, 8, block), lambda i: (0, i + first, 0, 0)),
    ]
    return pl.pallas_call(
        functools.partial(
            attend_forward_kernel, heads, block, chunk, rows, first, len(kept), cut_range
        ),
        grid=(steps,),
        in_specs=[
            pl.BlockSpec(memory_space=pltpu.SMEM),
            pl.BlockSpec((block, width), lambda i: (i + first, group)),
            pl.BlockSpec((length, width), lambda i: (0, group)),
            pl.BlockSpec((length, width), lambda i: (0, group)),
        ]
        + [pl.BlockSpec(memory_space=pl.ANY)] * len(kept),
        out_specs=own_specs + [pl.BlockSpec((rows, width), lambda i: (0, 0))] * per_part,
        out_shape=[
            jax.ShapeDtypeStruct((length, width), BF),
            jax.ShapeDtypeStruct((heads, count, length, block), BF),
            jax.ShapeDtypeStruct((heads, count, 8, block), F32),
        ]
        + [jax.ShapeDtypeStruct((rows, width), BF)] * per_part,
        scratch_shapes=[
            pltpu.VMEM((heads, length, 256), BF),
            pltpu.VMEM((heads, HD + 16, length), BF),
            pltpu.VMEM((heads, length, block), F32),
        ],
        input_output_aliases={4 + i: i for i in range(len(kept))},
        compiler_params=pltpu.CompilerParams(
            vmem_limit_bytes=VMEM_LIMIT, dimension_semantics=("arbitrary",)
        ),
        cost_estimate=BRIEF,
        name="attend_forward",
    )(lengths, q, k, v, *kept)


def attend_backward_kernel(
    heads, block, chunk, cuts, q_ref, k_ref, v_ref, o_ref, e_ref, l_ref, *rest
):
    cut_refs = rest[0:cuts]
    dq_ref, dk_ref, dv_ref, do_rows_ref, values_wide, keys_t, dk_sum, dv_sum = rest[cuts:]
    length = k_ref.shape[0]
    rows = length // cuts
    width = heads * HD
    i = pl.program_id(0)
    for k in range(cuts):

        @pl.when(i == k * rows // block)
        def _():
            begin = k * rows % block
            do_rows_ref[begin : begin + rows, :] = cut_refs[k][...]

    @pl.when(i == 0)
    def _():
        ones = (lax.broadcasted_iota(jnp.int32, (length, 128), 1) < 2).astype(BF)
        for h in range(heads):
            value = v_ref[:, h * HD : (h + 1) * HD]
            values_wide[h, :, 0:HD] = value
            values_wide[h, :, HD : 2 * HD] = value
            values_wide[h, :, 2 * HD :] = ones
        keys_t[...] = k_ref[...].T
        dk_sum[...] = jnp.zeros_like(dk_sum)
        dv_sum[...] = jnp.zeros_like(dv_sum)

    q = q_ref[...]
    flipped_do = do_rows_ref[...].astype(F32).T
    flipped_o = o_ref[...].astype(F32).T
    lane = lax.broadcasted_iota(jnp.int32, (block, width), 1)
    row = lax.broadcasted_iota(jnp.int32, (128, block), 0)
    grads = []
    for h in range(heads):
        own = slice(h * HD, (h + 1) * HD)
        inverse = 1.0 / l_ref[h, 0, 0:1, :]
        dot = -jnp.sum(flipped_do[own] * flipped_o[own], axis=0, keepdims=True) * inverse
        scaled = flipped_do[own] * inverse
        high = scaled.astype(BF)
        low = (scaled - high.astype(F32)).astype(BF)
        dot_high = dot.astype(BF)
        dot_low = (dot - dot_high.astype(F32)).astype(BF)
        dots = jnp.where(row == 0, dot_high, jnp.where(row == 1, dot_low, jnp.zeros_like(dot_low)))
        right = jnp.concatenate([high, low, dots], axis=0)
        do_rows = high.T
        if heads == 2:
            empty = jnp.zeros_like(do_rows)
            do_rows = jnp.concatenate([do_rows, empty] if h == 0 else [empty, do_rows], axis=1)
        query = jnp.where((lane >= h * HD) & (lane < (h + 1) * HD), q, jnp.zeros_like(q))
        total = None
        for c in range(length // chunk):
            rows = slice(c * chunk, (c + 1) * chunk)
            e = e_ref[h, 0, rows, :]
            part = mm(values_wide[h, rows, :], right)
            ds = (e.astype(F32) * part).astype(BF)
            dv_sum[rows, :] += mm(e, do_rows)
            dk_sum[rows, :] += mm(ds, query)
            part = mm(keys_t[own, rows], ds)
            total = part if total is None else total + part
        grads.append(total * HD ** (-0.5))
    dq_ref[...] = jnp.concatenate(grads, axis=0).T.astype(BF)

    @pl.when(i == pl.num_programs(0) - 1)
    def _():
        dk_ref[...] = (dk_sum[...] * HD ** (-0.5)).astype(BF)
        dv_ref[...] = dv_sum[...].astype(BF)


def attend_backward(q, k, v, att, d_att, e, row_sum, group, heads):
    length = q.shape[0]
    width = heads * HD
    block = e.shape[3]
    cuts = len(d_att)
    rows = length // cuts
    chunk = min(512, length)
    count = length // block
    whole = pl.BlockSpec((length, width), lambda i: (0, group))
    return pl.pallas_call(
        functools.partial(attend_backward_kernel, heads, block, chunk, cuts),
        grid=(count,),
        in_specs=[
            pl.BlockSpec((block, width), lambda i: (i, group)),
            whole,
            whole,
            pl.BlockSpec((block, width), lambda i: (i, 0)),
            pl.BlockSpec((heads, 1, length, block), lambda i: (0, i, 0, 0)),
            pl.BlockSpec((heads, 1, 8, block), lambda i: (0, i, 0, 0)),
        ]
        + [pl.BlockSpec((rows, width), lambda i: (0, group))] * cuts,
        out_specs=[
            pl.BlockSpec((block, width), lambda i: (i, 0)),
            pl.BlockSpec((length, width), lambda i: (0, 0)),
            pl.BlockSpec((length, width), lambda i: (0, 0)),
        ],
        out_shape=[jax.ShapeDtypeStruct((length, width), BF)] * 3,
        scratch_shapes=[
            pltpu.VMEM((block, width), BF),
            pltpu.VMEM((heads, length, 256), BF),
            pltpu.VMEM((width, length), BF),
            pltpu.VMEM((length, width), F32),
            pltpu.VMEM((length, width), F32),
        ],
        compiler_params=pltpu.CompilerParams(
            vmem_limit_bytes=VMEM_LIMIT, dimension_semantics=("arbitrary",)
        ),
        cost_estimate=BRIEF,
        name="attend_backward",
    )(q, k, v, att, e, row_sum, *d_att)


def normal_parts(z):
    density = jnp.exp2(z * z * (-0.5 * LOG2E))
    t = 1.0 / (1.0 + (0.3275911 * 0.5**0.5) * jnp.abs(z))
    poly = t * (
        0.254829592 * 0.5
        + t
        * (
            -0.284496736 * 0.5
            + t * (1.421413741 * 0.5 + t * (-1.453152027 * 0.5 + t * (1.061405429 * 0.5)))
        )
    )
    tail = poly * density
    return jnp.where(z < 0.0, tail, 1.0 - tail), density * 0.3989422804014327


def normalize(values):
    center = values - jnp.mean(values, axis=-1, keepdims=True)
    scale = lax.rsqrt(jnp.mean(center * center, axis=-1, keepdims=True) + EPS)
    return center * scale, scale


def normalize_back(e, normal, scale):
    return scale * (
        e
        - jnp.mean(e, axis=-1, keepdims=True)
        - normal * jnp.mean(e * normal, axis=-1, keepdims=True)
    )


def assemble_kernel(rank, share, sets, down_ref, up_ref):
    ranks = 3 * rank
    count, tail = sets.shape[0], sets.shape[1] - ranks
    for k in range(count):
        down_ref[:, k * 128 : (k + 1) * 128] = sets[k, 0:ranks, :]
    row = lax.broadcasted_iota(jnp.int32, (ranks, tail), 0)
    source = lax.broadcasted_iota(jnp.int32, (ranks, tail), 1)
    for j in range(3):
        for half in range(2):
            total = None
            for k in range(count):
                wanted = row < 0
                for r in range(share):
                    target = j * rank + k * share + r
                    wanted = wanted | (
                        (row == target) & (source == (j * share + r) * 2 + half)
                    )
                part = mm(jnp.where(wanted, 1.0, 0.0).astype(BF), sets[k, ranks:, :])
                total = part if total is None else total + part
            begin = (j * 2 + half) * 128
            up_ref[:, begin : begin + 128] = total.astype(BF)


def assemble(sets, rank, share):
    count = sets.shape[0]
    vmem = pl.BlockSpec(memory_space=pltpu.VMEM)
    return pl.pallas_call(
        functools.partial(assemble_kernel, rank, share),
        in_specs=[vmem],
        out_specs=[vmem] * 2,
        out_shape=[
            jax.ShapeDtypeStruct((3 * rank, count * 128), BF),
            jax.ShapeDtypeStruct((3 * rank, 6 * 128), BF),
        ],
        name="assemble",
    )(sets)


def place_rows(source, j, height, target, row, sem):
    return pltpu.make_async_copy(
        source.at[j * height : (j + 1) * height, :],
        target.at[pl.ds(row * height, height), :],
        sem,
    )


def ring_rows():
    n_dp = lax.axis_size("dp")
    mine = lax.axis_index("dp")
    found = []
    for d in (mine, mine ^ 1):
        found += [(d + n_dp - 2 * j) % n_dp for j in range(n_dp // 2)]
    return found


def project_kernel(parts, counts, height, down_ref, up_ref, *rest):
    places = ring_rows() if len(counts) > 1 else [0]
    x_hbm = rest[0:parts]
    w_hbm = rest[parts : parts + len(counts)]
    q_ref, k_ref, v_ref, u_ref, w_ref, x, x_sem, w_sem = rest[parts + len(counts) :]
    block = 0
    for i, count in enumerate(counts):
        for j in range(count):
            place_rows(w_hbm[i], j, height, w_ref, places[block], w_sem).start()
            block += 1
    copies = []
    begin = 0
    for i in range(parts):
        rows = x_hbm[i].shape[0]
        copies.append(pltpu.make_async_copy(x_hbm[i], x.at[begin : begin + rows], x_sem.at[i]))
        copies[-1].start()
        begin += rows
    pltpu.make_async_copy(w_ref, w_ref, w_sem).wait()
    begin = 0
    width = q_ref.shape[1]
    for i in range(parts):
        rows = x_hbm[i].shape[0]
        copies[i].wait()
        step = min(512, rows)
        for r in range(begin, begin + rows, step):
            here = x[r : r + step, :]
            u = mm_nt(here, down_ref[...]).astype(BF)
            u_ref[r : r + step, :] = u
            for j, out in enumerate((q_ref, k_ref, v_ref)):
                cols = slice(j * width, (j + 1) * width)
                out[r : r + step, :] = (mm(here, w_ref[:, cols]) + mm(u, up_ref[:, cols])).astype(BF)
        begin += rows


def project(height, down, up, xs, ws):
    model = xs[0].shape[1]
    length = sum(x.shape[0] for x in xs)
    width = up.shape[1] // 3
    counts = [w.shape[0] // height for w in ws]
    vmem = pl.BlockSpec(memory_space=pltpu.VMEM)
    return pl.pallas_call(
        functools.partial(project_kernel, len(xs), counts, height),
        in_specs=[vmem, vmem] + [pl.BlockSpec(memory_space=pl.ANY)] * (len(xs) + len(ws)),
        out_specs=[vmem] * 5,
        out_shape=[jax.ShapeDtypeStruct((length, width), BF)] * 3
        + [
            jax.ShapeDtypeStruct((length, down.shape[0]), BF),
            jax.ShapeDtypeStruct((model, 3 * width), BF),
        ],
        scratch_shapes=[
            pltpu.VMEM((length, model), BF),
            pltpu.SemaphoreType.DMA((len(xs),)),
            pltpu.SemaphoreType.DMA,
        ],
        compiler_params=pltpu.CompilerParams(vmem_limit_bytes=VMEM_LIMIT),
        cost_estimate=BRIEF,
        name="project",
    )(down, up, *xs, *ws)


def unproject_kernel(
    parts, groups, u_ref, w_ref, down_ref, up_ref, *rest
):
    x_refs = rest[0:parts]
    grads = rest[parts : parts + 3 * groups]
    out_ref, g_up_ref, g_down_ref = rest[parts + 3 * groups :]
    width = w_ref.shape[1] // 3
    total = None
    g_down = None
    g_up = [None] * 3
    begin = 0
    for i in range(parts):
        rows = x_refs[i].shape[0]
        here = slice(begin, begin + rows)
        values = [
            jnp.concatenate([grads[g * 3 + j][here, :] for g in range(groups)], axis=1)
            for j in range(3)
        ]
        d_u = None
        for j in range(3):
            cols = slice(j * width, (j + 1) * width)
            part = mm_nt(values[j], up_ref[:, cols])
            d_u = part if d_u is None else d_u + part
        d_u = d_u.astype(BF)
        total = mm(d_u, down_ref[...])
        for j in range(3):
            total = total + mm_nt(values[j], w_ref[:, j * width : (j + 1) * width])
        out_ref[here, :] = total.astype(out_ref.dtype)
        part = mm(transpose_small(d_u), x_refs[i][...])
        g_down = part if g_down is None else g_down + part
        u_t = transpose_small(u_ref[here, :])
        for j in range(3):
            part = mm(u_t, values[j])
            g_up[j] = part if g_up[j] is None else g_up[j] + part
        begin += rows
    g_down_ref[...] = g_down
    for j in range(3):
        g_up_ref[:, j * width : (j + 1) * width] = g_up[j]


def unproject(grads, u, w, down, up, xs, half, halves, dtype):
    length = u.shape[0]
    model = w.shape[0]
    width = w.shape[1] // 3
    rows = length // halves
    ranks = down.shape[0]
    grads = [value for group in grads for value in group]
    vmem = pl.BlockSpec(memory_space=pltpu.VMEM)
    return pl.pallas_call(
        functools.partial(unproject_kernel, len(xs), len(grads) // 3),
        grid=(1,),
        in_specs=[pl.BlockSpec((rows, ranks), lambda i: (half, 0))]
        + [vmem] * (3 + len(xs))
        + [pl.BlockSpec((rows, g.shape[1]), lambda i: (half, 0)) for g in grads],
        out_specs=[vmem] * 3,
        out_shape=[
            jax.ShapeDtypeStruct((rows, model), dtype),
            jax.ShapeDtypeStruct((ranks, 3 * width), F32),
            jax.ShapeDtypeStruct((ranks, model), F32),
        ],
        compiler_params=pltpu.CompilerParams(vmem_limit_bytes=VMEM_LIMIT),
        cost_estimate=BRIEF,
        name="unproject",
    )(u, w, down, up, *xs, *grads)


def middle_kernel(
    cuts, parts, counts, counts2, sizes, hidden_block, x_ref, cot_ref,
    down_out, up_out, down_fc1, up_fc1, down_fc2, up_fc2, gain1, bias1, gain2, bias2, *rest
):
    att_hbm = rest[0:parts]
    rest = rest[parts:]
    first_hbm = rest[0 : len(counts)]
    rest = rest[len(counts) :]
    second_hbm = rest[0 : len(counts2)]
    rest = rest[len(counts2) :]
    out_ref, dy1_ref = rest[0:2]
    d_att_refs = rest[2 : 2 + cuts]
    (
        g_up_fc2, g_down_fc2, g_up_fc1, g_down_fc1, g_up_out, g_down_out,
        att_own, wo_t, w1, w2_t, hidden, slope, normal1, normed, low_rows, total,
        att_sem, wo_sem, w1_sem, w2_sem,
    ) = rest[2 + cuts :]
    rows, model = x_ref.shape
    units = w1.shape[1]
    height, wide, narrow = sizes
    mine = lax.axis_index("tensor")
    n_t = lax.axis_size("tensor")
    order = cut_order(n_t)
    places = spread_places() if sum(counts) > 1 else [(0, 0)]
    places2 = places

    def fetch(source, j, begin, width, target, row, col, sem):
        pltpu.make_async_copy(
            source.at[j * height : (j + 1) * height, begin : begin + width],
            target.at[
                pl.ds(pl.multiple_of(row * height, height), height),
                pl.ds(pl.multiple_of(col * width, width), width),
            ],
            sem,
        ).start()

    def each_block(counts, places):
        block = 0
        for i, count in enumerate(counts):
            for j in range(count):
                yield (i, j) + places[block]
                block += 1

    if parts > 1:
        width = att_hbm[0].shape[1]
        groups = parts // n_t
        for k in range(n_t):
            for g in range(groups):
                col = pl.multiple_of(((mine ^ order[k]) * groups + g) * width, width)
                pltpu.make_async_copy(
                    att_hbm[k * groups + g], att_own.at[:, pl.ds(col, width)], att_sem
                ).start()
    else:
        pltpu.make_async_copy(att_hbm[0], att_own, att_sem).start()
    for i, j, row, col in each_block(counts, places):
        fetch(first_hbm[i], j, wide, narrow, wo_t, row, col, wo_sem)
    for i, j, row, col in each_block(counts, places):
        fetch(first_hbm[i], j, 0, wide, w1, row, col, w1_sem.at[col])
    for i, j, row, col in each_block(counts2, places2):
        fetch(second_hbm[i], j, 0, wide, w2_t, row, col, w2_sem.at[col])

    pltpu.make_async_copy(att_own, att_own, att_sem).wait()
    pltpu.make_async_copy(wo_t, wo_t, wo_sem).wait()
    att = att_own[...]
    u_out = mm_nt(att, down_out[...]).astype(BF)
    first = x_ref[...].astype(F32) + mm_nt(att, wo_t[...]) + mm(u_out, up_out[...])
    normal, scale1 = normalize(first)
    normal1[...] = normal
    full = normal * gain1[...].astype(F32) + bias1[...].astype(F32)
    normed[...] = full
    low_rows[...] = full.astype(BF)
    u_fc1 = mm_nt(low_rows[...], down_fc1[...]).astype(BF)

    blocks = units // hidden_block
    per_cut = wide // hidden_block

    def before(i):
        cols = slice(i * hidden_block, (i + 1) * hidden_block)
        if i % per_cut == 0:
            b = i // per_cut
            for target, sem in ((w1, w1_sem), (w2_t, w2_sem)):
                view = target.at[:, b * wide : (b + 1) * wide]
                pltpu.make_async_copy(view, view, sem.at[b]).wait()
        return mm(low_rows[...], w1[:, cols]) + mm(u_fc1, up_fc1[:, cols])

    z = before(0)
    u_sum = None
    for i in range(blocks):
        cols = slice(i * hidden_block, (i + 1) * hidden_block)
        following = before(i + 1) if i + 1 < blocks else None
        phi_sum, phi = normal_parts(z)
        act = (z * phi_sum).astype(BF)
        hidden[:, cols] = act
        slope[:, cols] = phi_sum + z * phi
        part = mm_nt(act, w2_t[:, cols])
        total[...] = part if i == 0 else total[...] + part
        part = mm_nt(act, down_fc2[:, cols])
        u_sum = part if u_sum is None else u_sum + part
        z = following
    u_fc2 = u_sum.astype(BF)
    second = normed[...] + total[...] + mm(u_fc2, up_fc2[...])
    normal2, scale2 = normalize(second)
    gain = gain2[...].astype(F32)
    out_ref[...] = (normal2 * gain + bias2[...].astype(F32)).astype(BF)
    d_second = normalize_back(cot_ref[...].astype(F32) * gain, normal2, scale2)
    total[...] = d_second
    d_ffn = d_second.astype(BF)
    d_u2 = mm_nt(d_ffn, up_fc2[...]).astype(BF)
    d_u2_t = transpose_small(d_u2)
    g_up_fc2[...] = mm(transpose_small(u_fc2), d_ffn).astype(BF)
    u_fc1_t = transpose_small(u_fc1)

    def before_back(i):
        cols = slice(i * hidden_block, (i + 1) * hidden_block)
        return mm(d_ffn, w2_t[:, cols]) + mm(d_u2, down_fc2[:, cols])

    d_hidden = before_back(0)
    u_sum = None
    for i in range(blocks):
        cols = slice(i * hidden_block, (i + 1) * hidden_block)
        following = before_back(i + 1) if i + 1 < blocks else None
        d_pre = (d_hidden * slope[:, cols]).astype(BF)
        g_down_fc2[:, cols] = mm(d_u2_t, hidden[:, cols]).astype(BF)
        g_up_fc1[:, cols] = mm(u_fc1_t, d_pre).astype(BF)
        total[...] += mm_nt(d_pre, w1[:, cols])
        part = mm_nt(d_pre, up_fc1[:, cols])
        u_sum = part if u_sum is None else u_sum + part
        d_hidden = following
    d_u1 = u_sum.astype(BF)
    d_normed = total[...] + mm(d_u1, down_fc1[...])
    g_down_fc1[...] = mm(transpose_small(d_u1), low_rows[...]).astype(BF)
    d_first = normalize_back(d_normed * gain1[...].astype(F32), normal1[...], scale1)
    dy1_ref[...] = d_first
    d_a = d_first.astype(BF)
    d_uo = mm_nt(d_a, up_out[...]).astype(BF)
    g_up_out[...] = mm(transpose_small(u_out), d_a).astype(BF)
    g_down_out[...] = mm(transpose_small(d_uo), att).astype(BF)
    att_own[...] = (mm(d_a, wo_t[...]) + mm(d_uo, down_out[...])).astype(BF)
    width = model // cuts
    for k in range(cuts):
        col = pl.multiple_of((mine ^ order[k]) * width, width) if cuts > 1 else 0
        d_att_refs[k][...] = att_own[:, pl.ds(col, width)]


def cut_order(n_t):
    order = [0]
    bit = n_t // 2
    while bit:
        order = order + [k ^ bit for k in order]
        bit //= 2
    return order


def middle(atts, cuts, x, cot, adapters, norms, firsts, seconds, sizes):
    rows, model = x.shape
    rank, units = adapters[3].shape
    height, wide, narrow = sizes
    counts = [f.shape[0] // height for f in firsts]
    counts2 = [f.shape[0] // height for f in seconds]
    hidden_block = min(512, wide)
    cols = units // wide
    vmem = pl.BlockSpec(memory_space=pltpu.VMEM)
    anywhere = pl.BlockSpec(memory_space=pl.ANY)
    long = jax.ShapeDtypeStruct((rank, units), BF)
    short = jax.ShapeDtypeStruct((rank, model), BF)
    out_shape = (
        [jax.ShapeDtypeStruct((rows, model), BF), jax.ShapeDtypeStruct((rows, model), F32)]
        + [jax.ShapeDtypeStruct((rows, model // cuts), BF)] * cuts
        + [short, long, long, short, short, short]
    )
    return pl.pallas_call(
        functools.partial(
            middle_kernel, cuts, len(atts), counts, counts2, sizes, hidden_block
        ),
        in_specs=[vmem] * 12 + [anywhere] * (len(atts) + len(firsts) + len(seconds)),
        out_specs=[vmem] * len(out_shape),
        out_shape=out_shape,
        scratch_shapes=[
            pltpu.VMEM((rows, model), BF),
            pltpu.VMEM((model, model), BF),
            pltpu.VMEM((model, units), BF),
            pltpu.VMEM((model, units), BF),
            pltpu.VMEM((rows, units), BF),
            pltpu.VMEM((rows, units), F32),
            pltpu.VMEM((rows, model), F32),
            pltpu.VMEM((rows, model), F32),
            pltpu.VMEM((rows, model), BF),
            pltpu.VMEM((rows, model), F32),
            pltpu.SemaphoreType.DMA,
            pltpu.SemaphoreType.DMA,
            pltpu.SemaphoreType.DMA((cols,)),
            pltpu.SemaphoreType.DMA((cols,)),
        ],
        compiler_params=pltpu.CompilerParams(vmem_limit_bytes=VMEM_LIMIT),
        cost_estimate=BRIEF,
        name="middle",
    )(x, cot, *adapters, *norms, *atts, *firsts, *seconds)


class Spread:
    def __init__(self):
        self.n_dp, self.n_t = lax.axis_size("dp"), lax.axis_size("tensor")
        self.devices = [(d, t) for d in range(self.n_dp) for t in range(self.n_t)]

    def send(self, value, target):
        n_t = self.n_t
        pairs = []
        for d, t in self.devices:
            to_d, to_t = target(d, t)
            pairs.append((d * n_t + t, to_d * n_t + to_t))
        return lax.ppermute(value, ("dp", "tensor"), pairs)

    def along_z(self, value):
        count = self.n_dp // 2
        return [value] + [
            self.send(value, lambda d, t, j=j: ((d + 2 * j) % self.n_dp, t))
            for j in range(1, count)
        ]

    def cross(self, value, core):
        return self.send(value, lambda d, t: (d ^ 1, t) if t % 2 == core else (d, t ^ 2))

    def core(self, value):
        return self.send(value, lambda d, t: (d, t ^ 1))


def spread_places():
    n_dp = lax.axis_size("dp")
    d = lax.axis_index("dp")
    mine = lax.axis_index("tensor")
    found = []
    for t in (mine, mine ^ 1):
        even = (t % 2) == 0
        for to_d, to_t in (
            (d, t),
            (jnp.where(even, d ^ 1, d), jnp.where(even, t, t ^ 2)),
            (jnp.where(even, d, d ^ 1), jnp.where(even, t ^ 2, t)),
            (d ^ 1, t ^ 2),
        ):
            found += [((to_d + n_dp - 2 * j) % n_dp, to_t) for j in range(n_dp // 2)]
    return found


def shards(
    inputs, cotangent, lengths, adapter_index, w_qkv, w_out, w_fc1, w_fc2,
    ln1_gain, ln1_bias, ln2_gain, ln2_bias, down_qkv, up_qkv, down_out, up_out,
    down_fc1, up_fc1, down_fc2, up_fc2,
):
    n_dp = lax.axis_size("dp")
    n_t = lax.axis_size("tensor")
    every = ("dp", "tensor")
    mine = lax.axis_index("tensor")
    rows, model = inputs.shape
    length = rows * n_t
    n_set = down_qkv.shape[1]
    rank = down_qkv.shape[3]
    r_dp = rank // n_dp
    r_t = rank // n_t
    d_dp = model // n_dp
    c_t = model // n_t
    f_t = w_fc1.shape[1]
    f_all = f_t * n_t

    def swap(value, bit):
        return lax.ppermute(value, "tensor", [(i, i ^ bit) for i in range(n_t)])

    bits = []
    bit = n_t // 2
    while bit:
        bits.append(bit)
        bit //= 2
    order = cut_order(n_t)

    x_parts = [inputs]
    for bit in bits[:-1]:
        x_parts = x_parts + [swap(part, bit) for part in x_parts]

    w_local = w_qkv.transpose(1, 0, 2).reshape(d_dp, 3 * c_t)
    packed = jnp.concatenate([w_fc1, w_out.T], axis=1)
    packed_second = w_fc2.T
    mine_dp = lax.axis_index("dp")
    if (n_dp, n_t) == (8, 4):
        spread = Spread()
        w_parts = spread.along_z(w_local)
        w_height = d_dp
        block_sizes = (d_dp, f_t, c_t)
    else:
        w_parts = [lax.all_gather(w_local, "dp", axis=0, tiled=True)]
        w_height = model
        firsts = lax.all_gather(packed, every, axis=0).reshape(n_dp, n_t, d_dp, f_t + c_t)
        seconds = lax.all_gather(packed_second, every, axis=0).reshape(n_dp, n_t, d_dp, f_t)

        def whole(value):
            return value.transpose(0, 2, 1, 3).reshape(model, -1)

        firsts = [
            jnp.concatenate(
                [whole(firsts[..., :f_t]), whole(firsts[..., f_t:])], axis=1
            )
        ]
        seconds = [whole(seconds)]
        block_sizes = (model, f_all, model)

    index_all = lax.all_to_all(
        jnp.broadcast_to(adapter_index, (n_dp,)), "dp", 0, 0, tiled=True
    )
    onehot_all = (index_all[:, None] == jnp.arange(n_set, dtype=jnp.int32)[None, :]).astype(BF)
    down_t = down_qkv.transpose(1, 0, 3, 2).reshape(n_set, 3 * rank, d_dp)
    if n_dp * r_dp == rank and d_dp == 128 and c_t == 256:
        up_rows = up_qkv.transpose(1, 0, 2, 3).reshape(n_set, 6 * r_dp, 128)
        fill = jnp.zeros((n_set, -6 * r_dp % 16, 128), BF)
        table = jnp.concatenate([down_t, up_rows, fill], axis=1)
        sets = jnp.einsum("ns,srl->nrl", onehot_all, table, preferred_element_type=F32).astype(BF)
        w_parts, sets, packed = lax.optimization_barrier((w_parts, sets, packed))
        w_near = jnp.concatenate(w_parts, axis=0)
        w_parts = [w_near, lax.ppermute(w_near, "dp", [(i, i ^ 1) for i in range(n_dp)])]
        first = spread.along_z(packed)
        sets = lax.all_to_all(sets, "dp", 0, 0, tiled=True)
        w_parts, sets, x_parts = lax.optimization_barrier((w_parts, sets, x_parts))
        sel_down_qkv, sel_up_qkv = assemble(sets, rank, r_dp)
    else:
        table = jnp.concatenate(
            [down_t.reshape(n_set, -1), up_qkv.transpose(1, 0, 2, 3).reshape(n_set, -1)], axis=1
        )
        came = lax.all_to_all(mm(onehot_all, table).astype(BF), "dp", 0, 0, tiled=True)
        cut = 3 * rank * d_dp
        sel_down_qkv = (
            came[:, :cut].reshape(n_dp, 3 * rank, d_dp).transpose(1, 0, 2).reshape(3 * rank, model)
        )
        up_cols = came[:, cut:].reshape(n_dp, 3, r_dp, c_t).transpose(1, 0, 2, 3)
        same = jnp.eye(3, dtype=BF).reshape(3, 1, 3, 1)
        sel_up_qkv = (up_cols.reshape(3, rank, 1, c_t) * same).reshape(3 * rank, 3 * c_t)
    def part_of_rank(value, axis):
        return lax.dynamic_slice_in_dim(value, mine * r_t, r_t, axis)

    tables = [
        down_out.transpose(0, 2, 1),
        part_of_rank(up_out, 1),
        part_of_rank(down_fc1.transpose(0, 2, 1), 1),
        up_fc1,
        down_fc2.transpose(0, 2, 1),
        part_of_rank(up_fc2, 1),
    ]
    sizes = [t.size // n_set for t in tables]
    table = jnp.concatenate([t.reshape(n_set, -1) for t in tables], axis=1)
    chosen = mm(onehot_all, table).astype(BF)
    norm_part = jnp.stack([ln1_gain, ln1_bias, ln2_gain, ln2_bias]).reshape(1, -1)
    chosen = jnp.concatenate([chosen, jnp.broadcast_to(norm_part, (n_dp, norm_part.size))], axis=1)
    sent = jnp.broadcast_to(chosen[:, None, :], (n_dp, n_t, chosen.shape[1])).reshape(n_dp * n_t, -1)
    staged = n_dp == 8 and n_t == 4
    x_parts = x_parts + [swap(part, bits[-1]) for part in x_parts]
    if staged:
        x_parts, first, sent, packed_second = lax.optimization_barrier(
            (x_parts, first, sent, packed_second)
        )
        first = jnp.concatenate(first, axis=0)
        first_one = spread.cross(first, 0)
        first_two = spread.cross(first, 1)
        second = spread.along_z(packed_second)
    came = lax.all_to_all(sent, every, 0, 0, tiled=True)
    *qkv, u_in, w_cols = project(
        w_height, sel_down_qkv, sel_up_qkv, x_parts, w_parts
    )
    def make_adapters(came):
        came = came.reshape(n_dp, n_t, -1)
        pieces = []
        start = 0
        for size in sizes:
            pieces.append(came[:, :, start : start + size])
            start += size
        norms = came[:, 0, start:].reshape(n_dp, 4, d_dp).transpose(1, 0, 2).reshape(4, 1, model)

        def from_rank_parts(piece):
            return piece.reshape(n_dp, n_t, r_t, d_dp).transpose(1, 2, 0, 3).reshape(rank, model)

        def from_blocks(piece, width):
            return piece.reshape(n_dp, n_t, r_dp, width).transpose(0, 2, 1, 3).reshape(rank, n_t * width)

        adapters = [
            from_blocks(pieces[0], c_t),
            from_rank_parts(pieces[1]),
            from_rank_parts(pieces[2]),
            from_blocks(pieces[3], f_t),
            from_blocks(pieces[4], f_t),
            from_rank_parts(pieces[5]),
        ]
        return adapters, norms

    heads = c_t // HD
    group_heads = 2 if heads % 2 == 0 else 1
    groups = heads // group_heads
    kept = []
    att_parts = [[] for _ in range(n_t)]
    for g in range(groups):
        kept.append([])
        for part in range(2):
            if staged and (g, part) == (1, 0):
                qkv, kept, first_one, first_two, second, came = lax.optimization_barrier(
                    (qkv, kept, first_one, first_two, second, came)
                )
                first_both = spread.cross(first_one, 1)
                second = jnp.concatenate(second, axis=0)
                second_one = spread.cross(second, 0)
                second_two = spread.cross(second, 1)
            elif staged and (g, part) == (1, 1):
                qkv, kept, adapters, first_both = lax.optimization_barrier(
                    (qkv, kept, make_adapters(came), first_both)
                )
            att, e, row_sum, *cut_rows = attend_forward(
                *qkv, lengths, g, group_heads, rows, part, 2, kept[-1]
            )
            kept[-1] = [att, e, row_sum]
            for i, value in enumerate(cut_rows):
                k = part * len(cut_rows) + i
                att_parts[k].append(value if order[k] == 0 else swap(value, order[k]))
    atts = [part for parts in att_parts for part in parts]

    if staged:
        kept, second_one, second_two = lax.optimization_barrier((kept, second_one, second_two))
        seconds = [second, second_one, second_two, spread.cross(second_one, 1)]
        seconds += [spread.core(value) for value in seconds]
        firsts = [first, first_one, first_two, first_both]
        firsts += [spread.core(value) for value in firsts]
    else:
        adapters = make_adapters(came)
    adapters, norms = adapters
    blocks_fit = c_t % 128 == 0
    if not blocks_fit:
        by_cut = jnp.concatenate(atts, axis=1).reshape(rows, n_t, c_t)
        to_cut = jnp.array([order.index(k) for k in range(n_t)], jnp.int32)
        to_cut = to_cut[jnp.arange(n_t, dtype=jnp.int32) ^ mine]
        atts = [jnp.take(by_cut, to_cut, axis=1).reshape(rows, model)]
    cuts = n_t if blocks_fit else 1
    done = middle(
        atts, cuts, inputs, cotangent, adapters, list(norms), firsts, seconds, block_sizes
    )
    output, d_first = done[0:2]
    d_att_blocks = done[2 : 2 + cuts]
    if not blocks_fit:
        by_owner = d_att_blocks[0].reshape(rows, n_t, c_t)
        d_att_blocks = [
            lax.dynamic_index_in_dim(by_owner, mine ^ order[k], 1, keepdims=False)
            for k in range(n_t)
        ]
    g_up_fc2, g_down_fc2, g_up_fc1, g_down_fc1, g_up_out, g_down_out = done[2 + cuts :]

    def share_cols(value):
        lead = value.size // model
        return (
            value.reshape(lead, n_dp, n_t, model // (n_dp * n_t))
            .transpose(1, 2, 0, 3)
            .reshape(n_dp * n_t, -1)
        )

    def share_blocks(value):
        width = value.shape[1] // n_t
        return (
            value.reshape(n_dp, r_dp, n_t, width).transpose(0, 2, 1, 3).reshape(n_dp * n_t, -1)
        )

    def exchange(parts):
        widths = [p.shape[1] for p in parts]
        got = lax.all_to_all(jnp.concatenate(parts, axis=1), every, 0, 0, tiled=True)
        return got, widths

    early, early_widths = exchange(
        [
            share_blocks(g_down_out),
            share_cols(g_up_out),
            share_cols(g_down_fc1),
            share_blocks(g_up_fc1),
            share_blocks(g_down_fc2),
            share_cols(g_up_fc2),
        ]
    )

    d_att_all = [
        d_att_blocks[k] if order[k] == 0 else swap(d_att_blocks[k], order[k]) for k in range(n_t)
    ]
    grads = []
    for g in range(groups):
        if g == groups - 1:
            d_att_all, early = lax.optimization_barrier((d_att_all, early))
        grads.append(
            attend_backward(*qkv, kept[g][0], d_att_all, kept[g][1], kept[g][2], g, group_heads)
        )

    def partly(half, dtype):
        xs = x_parts[half * n_t // 2 : (half + 1) * n_t // 2]
        return unproject(grads, u_in, w_cols, sel_down_qkv, sel_up_qkv, xs, half, 2, dtype)

    other, g_up_other, g_down_other = partly(1, BF)
    parts, g_up_own, g_down_own = partly(0, F32)
    other = swap(other, bits[-1])
    span = length // 2
    for bit in reversed(bits[:-1]):
        half = span // 2
        sent = (parts[half:] + other[half:].astype(F32)).astype(BF)
        parts = parts[:half] + other[:half].astype(F32)
        other = swap(sent, bit)
        span = half
    grad_input = d_first + parts + other.astype(F32)

    g_down_qkv = (g_down_own + g_down_other).astype(BF)
    g_up_all = (g_up_own + g_up_other).astype(BF)
    g_up_qkv = jnp.stack(
        [
            g_up_all[j * rank : (j + 1) * rank, j * c_t : (j + 1) * c_t]
            for j in range(3)
        ]
    )
    up_share = (
        g_up_qkv.reshape(3, n_dp, r_dp, c_t).transpose(1, 0, 2, 3).reshape(n_dp, 1, -1)
    )
    up_share = jnp.broadcast_to(up_share, (n_dp, n_t, up_share.shape[2])).reshape(n_dp * n_t, -1)
    late, late_widths = exchange([share_cols(g_down_qkv), up_share])

    by_sender = jnp.broadcast_to(onehot_all[:, None, :], (n_dp, n_t, n_set)).reshape(-1, n_set)
    same_cols = (jnp.arange(n_dp * n_t, dtype=jnp.int32) % n_t == mine).astype(BF)

    tn = (((0,), (0,)), ((), ()))

    def total(got, weights):
        return lax.dot_general(weights, got, tn, preferred_element_type=F32)

    early_sum = total(early, by_sender)
    pieces = []
    start = 0
    for width in early_widths:
        pieces.append(early_sum[:, start : start + width])
        start += width
    d_all = model // (n_dp * n_t)
    sum_down_out = pieces[0].reshape(n_set, r_dp, c_t).transpose(0, 2, 1)
    sum_up_out = pieces[1].reshape(n_set, rank, d_all)
    sum_down_fc1 = pieces[2].reshape(n_set, rank, d_all).transpose(0, 2, 1)
    sum_up_fc1 = pieces[3].reshape(n_set, r_dp, f_t)
    sum_down_fc2 = pieces[4].reshape(n_set, r_dp, f_t).transpose(0, 2, 1)
    sum_up_fc2 = pieces[5].reshape(n_set, rank, d_all)
    sum_down_qkv = (
        total(late[:, : late_widths[0]], by_sender)
        .reshape(n_set, 3, rank, d_all)
        .transpose(1, 0, 3, 2)
    )
    sum_up_qkv = (
        total(late[:, late_widths[0] :], by_sender * same_cols[:, None])
        .reshape(n_set, 3, r_dp, c_t)
        .transpose(1, 0, 2, 3)
    )
    return (
        output,
        grad_input,
        sum_down_qkv,
        sum_up_qkv,
        sum_down_out,
        sum_up_out,
        sum_down_fc1,
        sum_up_fc1,
        sum_down_fc2,
        sum_up_fc2,
    )


def solution(mesh):
    both = ("dp", "tensor")
    in_specs = (
        P(both, None),
        P(both, None),
        P("dp", None),
        P("dp"),
        P(None, "dp", "tensor"),
        P("tensor", "dp"),
        P("dp", "tensor"),
        P("tensor", "dp"),
        P("dp"),
        P("dp"),
        P("dp"),
        P("dp"),
        P(None, None, "dp", None),
        P(None, None, "dp", "tensor"),
        P(None, "tensor", "dp"),
        P(None, None, "dp"),
        P(None, "dp", None),
        P(None, "dp", "tensor"),
        P(None, "tensor", "dp"),
        P(None, None, "dp"),
    )
    out_specs = (
        P(both, None),
        P(both, None),
        P(None, None, both, None),
        P(None, None, "dp", "tensor"),
        P(None, "tensor", "dp"),
        P(None, None, both),
        P(None, both, None),
        P(None, "dp", "tensor"),
        P(None, "tensor", "dp"),
        P(None, None, both),
    )
    return jax.shard_map(shards, mesh=mesh, in_specs=in_specs, out_specs=out_specs, check_vma=False)
```

time: 503 us -> 405 us (0.81)
  waiting for transfers between devices: 167 us -> 91.9 us
  matrix products: 56.4 us -> 2.17 us
  Pallas kernels: 131 us -> 173 us
  starting transfers between devices: 23.2 us -> 63.5 us
  between operations: 31.4 us -> 2.88 us
  blocking collectives: 13.3 us -> 0 us
  local copies, waits for them, and re-layouts: 56.3 us -> 48.4 us
    all_gather x4 -> x0, waiting for transfers between devices: 119 us -> none  [the longest x1 78.9 us: shards(): w2_all = lax.all_gather(w_fc2, every, axis=0)]
    pallas_call x1 -> x5, Pallas kernels: 45.5 us -> 75.5 us  [the longest x1 46 us: middle(): pl.pallas_call(functools.partial(middle_kernel, cuts, len(atts), counts,...]
    ppermute x0 -> x24, starting transfers between devices: none -> 28.9 us  [the longest x23 28.3 us: send(): return lax.ppermute(value, ('dp', 'tensor'), pairs)]
    dot_general x9 -> x1, matrix products: 28.3 us -> 0.87 us  [mm(): return jnp.dot(left, right, preferred_element_type=F32)]
    dot_general x14 -> x1, matrix products: 26.9 us -> 0.25 us  [shards(): jnp.einsum('ns,srl->nrl', onehot_all, table, preferred_element_type=F32)]
    ppermute x13 -> x14, waiting for transfers between devices: 45.9 us -> 66.3 us  [swap(): return lax.ppermute(value, 'tensor', [(i, i ^ bit) for i in range(n_t)])]
    ppermute x0 -> x24, waiting for transfers between devices: none -> 14.8 us  [the longest x23 14.8 us: send(): return lax.ppermute(value, ('dp', 'tensor'), pairs)]
    unnamed x1 -> x0, blocking collectives: 13.3 us -> none
  transfers between devices with their start and end apart: 20 -> 43, of which waited for: 9 -> 13; matrix products, arithmetic and copies ran while one was open for 18% -> 10% of each run, Pallas kernels for 8% -> 24%
where the time goes in v2:
time: 405 us; the launch traced here: 397 us
  Pallas kernels  173 us (43%)
  waiting for transfers between devices  91.9 us (23%)
  starting transfers between devices  63.5 us (16%)
  local copies, waits for them, and re-layouts  48.4 us (12%)
  other arithmetic  15.3 us (4%)
    ppermute x14, waiting for transfers between devices, swap(): return lax.ppermute(value, 'tensor', [(i, i ^ bit) for i in range(n_t)])  66.3 us
    pallas_call x4, Pallas kernels, attend_forward(): pl.pallas_call(functools.partial(attend_forward_kernel, heads, block, chu...  51.4 us
    pallas_call x1, Pallas kernels, middle(): pl.pallas_call(functools.partial(middle_kernel, cuts, len(atts), counts,...  46 us
    pallas_call x2, Pallas kernels, attend_backward(): pl.pallas_call(functools.partial(attend_backward_kernel, heads, block, ch...  45.7 us
    unnamed x144, local copies, waits for them, and re-layouts  28.3 us
    ppermute x23, starting transfers between devices, send(): return lax.ppermute(value, ('dp', 'tensor'), pairs)  28.3 us
    pallas_call x2, Pallas kernels, unproject(): pl.pallas_call(functools.partial(unproject_kernel, len(xs), len(grads) //...  15.1 us
    ppermute x23, waiting for transfers between devices, send(): return lax.ppermute(value, ('dp', 'tensor'), pairs)  14.8 us
  transfers between devices with their start and end apart: 43, of which 13 were waited for; matrix products, arithmetic and copies ran while one was open for 10% of the time, Pallas kernels for 24%

profile of v2, /device:TPU:0, one launch (start us, length us, event | category | flops | bytes accessed | tf_op | source)
XLA Modules:
  0.0 396.7 jit_solution(5959070461766716076)
XLA Ops:
  2.0 3.1 collective-permute-start
  5.1 2.6 collective-permute-start.1
  10.3 3.3 all-to-all-start
  13.6 1.6 collective-permute-start.4
  21.7 3.9 all-to-all-done
  30.8 3.8 all-to-all-start.1
  34.6 1.8 copy.186
  37.3 2.0 collective-permute-start.7
  39.3 2.4 collective-permute-start.8
  43.1 6.9 %all-to-all-done.1.sets = bf16[8,64,128]{2,1,0:T(8,128)(2,1)S(1)} async-done(((bf16[8,64,128]{2,1,0:T(8,128)(2,1)}), bf16[8,64,128]{2,1,0:T(8,128)(2,1)S(1)}, u32[]{:S(2)}, u32[]{:S(2)}) %all-to-all-start.1) | async-done | bytes 131104 | tf_op jit(solution)/shard_map/all_to_all | solution.py:807
  52.5 1.9 reshape.254
  54.4 8.2 %collective-permute-done.8 = bf16[128,1280]{1,0:T(8,128)(2,1)} collective-permute-done((bf16[128,1280]{1,0:T(8,128)(2,1)}, bf16[128,1280]{1,0:T(8,128)(2,1)}, u32[]{:S(2)}, u32[]{:S(2)}) %collective-permute-start.8) | collective-permute-done | bytes 327712 | tf_op jit(solution)/shard_map/ppermute | solution.py:700
  62.6 2.0 constant_dynamic-update-slice_fusion.9
  64.6 1.7 constant_dynamic-update-slice_fusion.8
  66.3 1.7 constant_dynamic-update-slice_fusion.7
  68.1 1.8 constant_dynamic-update-slice_fusion.6.rest_8_
  71.3 1.5 collective-permute-start.11
  75.0 8.6 %all-to-all-start.2 = ((bf16[32,2,3328]{2,1,0:T(2,128)(2,1)}), bf16[32,2,3328]{2,1,0:T(2,128)(2,1)S(1)}, u32[]{:S(2)}, u32[]{:S(2)}) async-start(bf16[32,2,3328]{2,1,0:T(2,128)(2,1)} %reshape.299), calls=%async_computation.2 | async-start | bytes 851968 | tf_op jit(solution)/shard_map/all_to_all | solution.py:849
  83.6 1.8 collective-permute-start.12
  85.5 2.4 collective-permute-start.13
  89.3 2.0 assemble.1
  91.3 12.4 %project.1 = (bf16[2048,256]{1,0:T(8,128)(2,1)}, bf16[2048,256]{1,0:T(8,128)(2,1)}, bf16[2048,256]{1,0:T(8,128)(2,1)}, bf16[2048,48]{1,0:T(8,128)(2,1)}, bf16[1024,768]{1,0:T(8,128)(2,1)}) custom-call(bf16[48,1024]{1,0:T(8,128)(2,1)} %get-tuple-element.131.down_ref, bf16[48,768]{1,0:T(8,128)(2,1)} %get-tuple-element.132.up_ref, bf16[512,1024]{1,0:T(8,128)(2,1)} %rest_0_.1, ...), custom_call_target="tpu_custom_call" | custom-call | flops 1 | bytes 1 | tf_op jit(solution)/shard_map/project/pallas_call | solution.py:404
  103.7 13.0 %attend_forward.4 = (bf16[2048,128]{1,0:T(8,128)(2,1)}, bf16[2,4,2048,512]{3,2,1,0:T(8,128)(2,1)}, f32[2,4,8,512]{3,2,1,0:T(8,128)}, bf16[512,128]{1,0:T(8,128)(2,1)}, bf16[512,128]{1,0:T(8,128)(2,1)}) custom-call(s32[1,8]{1,0:T(1,128)} %lengths_ref.7, bf16[2048,256]{1,0:T(8,128)(2,1)} %get-tuple-element.180.q_ref, ...), custom_call_target="tpu_custom_call" | custom-call | flops 1 | bytes 1 | tf_op jit(solution)/shard_map/attend_forward/pallas_call | solution.py:136
  116.7 12.5 %attend_forward.5 = (bf16[2048,128]{1,0:T(8,128)(2,1)}, bf16[2,4,2048,512]{3,2,1,0:T(8,128)(2,1)}, f32[2,4,8,512]{3,2,1,0:T(8,128)}, bf16[512,128]{1,0:T(8,128)(2,1)}, bf16[512,128]{1,0:T(8,128)(2,1)}) custom-call(s32[1,8]{1,0:T(1,128)} %lengths_ref.7, ...), custom_call_target="tpu_custom_call", output_to_operand_aliasing={{0}: (4, {}), {1}: (5, {}), {2}: (6, {})} | custom-call | flops 1 | bytes 1 | tf_op jit(solution)/shard_map/attend_forward/pallas_call | solution.py:136
  134.1 1.5 collective-permute-start.26
  136.9 12.7 %attend_forward.6 = (bf16[2048,128]{1,0:T(8,128)(2,1)}, bf16[2,4,2048,512]{3,2,1,0:T(8,128)(2,1)}, f32[2,4,8,512]{3,2,1,0:T(8,128)}, bf16[512,128]{1,0:T(8,128)(2,1)}, bf16[512,128]{1,0:T(8,128)(2,1)}) custom-call(s32[1,8]{1,0:T(1,128)} %lengths_ref.7, bf16[2048,256]{1,0:T(8,128)(2,1)} %get-tuple-element.180.q_ref, ...), custom_call_target="tpu_custom_call" | custom-call | flops 1 | bytes 1 | tf_op jit(solution)/shard_map/attend_forward/pallas_call | solution.py:136
  153.0 6.6 %collective-permute-done.15.rest_11_ = bf16[512,1280]{1,0:T(8,128)(2,1)S(1)} collective-permute-done((bf16[512,1280]{1,0:T(8,128)(2,1)}, bf16[512,1280]{1,0:T(8,128)(2,1)S(1)}, u32[]{:S(2)}, u32[]{:S(2)}) %collective-permute-start.15) | collective-permute-done | bytes 1310752 | tf_op jit(solution)/shard_map/ppermute | solution.py:700
  159.7 13.2 %attend_forward.7 = (bf16[2048,128]{1,0:T(8,128)(2,1)}, bf16[2,4,2048,512]{3,2,1,0:T(8,128)(2,1)}, f32[2,4,8,512]{3,2,1,0:T(8,128)}, bf16[512,128]{1,0:T(8,128)(2,1)}, bf16[512,128]{1,0:T(8,128)(2,1)}) custom-call(s32[1,8]{1,0:T(1,128)} %lengths_ref.7, ...), custom_call_target="tpu_custom_call", output_to_operand_aliasing={{0}: (4, {}), {1}: (5, {}), {2}: (6, {})} | custom-call | flops 1 | bytes 1 | tf_op jit(solution)/shard_map/attend_forward/pallas_call | solution.py:136
  172.9 1.5 collective-permute-start.28
  175.0 15.8 %collective-permute-done.16.rest_2_ = bf16[512,128]{1,0:T(8,128)(2,1)S(1)} collective-permute-done((bf16[512,128]{1,0:T(8,128)(2,1)S(1)}, bf16[512,128]{1,0:T(8,128)(2,1)S(1)}, u32[]{:S(2)}, u32[]{:S(2)}) %collective-permute-start.16) | collective-permute-done | bytes 131104 | tf_op jit(solution)/shard_map/ppermute | solution.py:754
  193.4 4.2 %collective-permute-done.20.rest_6_ = bf16[512,128]{1,0:T(8,128)(2,1)S(1)} collective-permute-done((bf16[512,128]{1,0:T(8,128)(2,1)S(1)}, bf16[512,128]{1,0:T(8,128)(2,1)S(1)}, u32[]{:S(2)}, u32[]{:S(2)}) %collective-permute-start.20) | collective-permute-done | bytes 131104 | tf_op jit(solution)/shard_map/ppermute | solution.py:754
  199.3 4.5 %collective-permute-done.17.rest_3_ = bf16[512,128]{1,0:T(8,128)(2,1)S(1)} collective-permute-done((bf16[512,128]{1,0:T(8,128)(2,1)}, bf16[512,128]{1,0:T(8,128)(2,1)S(1)}, u32[]{:S(2)}, u32[]{:S(2)}) %collective-permute-start.17) | collective-permute-done | bytes 131104 | tf_op jit(solution)/shard_map/ppermute | solution.py:754
  204.9 3.8 collective-permute-done.19.rest_5_
  210.6 3.8 collective-permute-done.21.rest_7_
  216.8 46.0 %middle.1 = (bf16[512,1024]{1,0:T(8,128)(2,1)}, f32[512,1024]{1,0:T(8,128)}, bf16[512,256]{1,0:T(8,128)(2,1)}, bf16[512,256]{1,0:T(8,128)(2,1)}, bf16[512,256]{1...) custom-call(bf16[512,1024]{1,0:T(8,128)(2,1)} %rest_0_.1, ...), custom_call_target="tpu_custom_call" | custom-call | flops 1 | bytes 1 | tf_op jit(solution)/shard_map/middle/pallas_call | solution.py:660
  269.8 2.8 all-to-all-start.3
  272.7 1.8 collective-permute-start.33
  274.9 10.9 %collective-permute-done.33.rest_1_ = bf16[512,256]{1,0:T(8,128)(2,1)S(1)} collective-permute-done((bf16[512,256]{1,0:T(8,128)(2,1)S(1)}, bf16[512,256]{1,0:T(8,128)(2,1)S(1)}, u32[]{:S(2)}, u32[]{:S(2)}) %collective-permute-start.33) | collective-permute-done | bytes 262176 | tf_op jit(solution)/shard_map/ppermute | solution.py:754
  285.8 4.5 %collective-permute-done.35.rest_3_ = bf16[512,256]{1,0:T(8,128)(2,1)S(1)} collective-permute-done((bf16[512,256]{1,0:T(8,128)(2,1)S(1)}, bf16[512,256]{1,0:T(8,128)(2,1)S(1)}, u32[]{:S(2)}, u32[]{:S(2)}) %collective-permute-start.35) | collective-permute-done | bytes 262176 | tf_op jit(solution)/shard_map/ppermute | solution.py:754
  290.9 22.7 %attend_backward.2 = (bf16[2048,128]{1,0:T(8,128)(2,1)}, bf16[2048,128]{1,0:T(8,128)(2,1)}, bf16[2048,128]{1,0:T(8,128)(2,1)}) custom-call(bf16[2048,256]{1,0:T(8,128)(2,1)} %get-tuple-element.180.q_ref, bf16[2048,256]{1,0:T(8,128)(2,1)} %get-tuple-element.181.k_ref, bf16[2048,256]{1,0:T(8,128)(2,1)} %get-tuple-element.182.v_ref, ...), custom_call_target="tpu_custom_call" | custom-call | flops 1 | bytes 1 | tf_op jit(solution)/shard_map/attend_backward/pallas_call | solution.py:247
  314.3 22.9 %attend_backward.3 = (bf16[2048,128]{1,0:T(8,128)(2,1)}, bf16[2048,128]{1,0:T(8,128)(2,1)}, bf16[2048,128]{1,0:T(8,128)(2,1)}) custom-call(bf16[2048,256]{1,0:T(8,128)(2,1)} %get-tuple-element.180.q_ref, bf16[2048,256]{1,0:T(8,128)(2,1)} %get-tuple-element.181.k_ref, bf16[2048,256]{1,0:T(8,128)(2,1)} %get-tuple-element.182.v_ref, ...), custom_call_target="tpu_custom_call" | custom-call | flops 1 | bytes 1 | tf_op jit(solution)/shard_map/attend_backward/pallas_call | solution.py:247
  337.2 7.2 %unproject.3 = (bf16[1024,1024]{1,0:T(8,128)(2,1)}, f32[48,768]{1,0:T(8,128)}, f32[48,1024]{1,0:T(8,128)}) custom-call(bf16[2048,48]{1,0:T(8,128)(2,1)} %get-tuple-element.205.u_ref, bf16[1024,768]{1,0:T(8,128)(2,1)} %get-tuple-element.206.w_ref, bf16[48,1024]{1,0:T(8,128)(2,1)} %get-tuple-element.131.down_ref, bf16[48,768]{1,0:T(8,128)(2,1)} %get-tuple-element.132.up_ref, ...), custom_call_target="tpu_custom_call" | custom-call | flops 1 | bytes 1 | tf_op jit(solution)/shard_map/unproject/pallas_call | solution.py:472
  345.0 7.9 %unproject.2 = (f32[1024,1024]{1,0:T(8,128)}, f32[48,768]{1,0:T(8,128)}, f32[48,1024]{1,0:T(8,128)}) custom-call(bf16[2048,48]{1,0:T(8,128)(2,1)} %get-tuple-element.205.u_ref, bf16[1024,768]{1,0:T(8,128)(2,1)} %get-tuple-element.206.w_ref, bf16[48,1024]{1,0:T(8,128)(2,1)} %get-tuple-element.131.down_ref, bf16[48,768]{1,0:T(8,128)(2,1)} %get-tuple-element.132.up_ref, ...), custom_call_target="tpu_custom_call" | custom-call | flops 1 | bytes 1 | tf_op jit(solution)/shard_map/unproject/pallas_call | solution.py:472
  357.2 4.8 %all-to-all-start.4 = ((bf16[32,2,1536]{2,1,0:T(2,128)(2,1)}), bf16[32,2,1536]{2,1,0:T(2,128)(2,1)S(1)}, u32[]{:S(2)}, u32[]{:S(2)}) async-start(bf16[32,2,1536]{2,1,0:T(2,128)(2,1)} %reshape.303), calls=%async_computation.4 | async-start | bytes 393216 | tf_op jit(solution)/shard_map/all_to_all | solution.py:952
  362.3 3.7 add_convert_fusion
  366.0 1.8 collective-permute-start.37
  374.6 17.5 %collective-permute-done.37 = bf16[512,1024]{1,0:T(8,128)(2,1)} collective-permute-done((bf16[512,1024]{1,0:T(8,128)(2,1)}, bf16[512,1024]{1,0:T(8,128)(2,1)}, u32[]{:S(2)}, u32[]{:S(2)}) %collective-permute-start.37) | collective-permute-done | bytes 1048608 | tf_op jit(solution)/shard_map/ppermute | solution.py:754
  392.1 4.2 %convert_add_fusion = f32[512,1024]{1,0:T(8,128)} fusion(bf16[512,1024]{1,0:T(8,128)(2,1)} %collective-permute-done.37, f32[512,1024]{1,0:T(8,128)S(1)} %copy-done.6, f32[1024,1024]{1,0:T(8,128)} %get-tuple-element.233, bf16[1024,1024]{1,0:T(8,128)(2,1)} %copy-done.7), kind=kLoop, calls=%fused_computation.1 | loop fusion | flops 2621440 | bytes 8388608 | tf_op jit(solution)/shard_map/add | solution.py:991
  (285 shorter events, 64.5 us)
Async XLA Ops:
  2.0 24.8 %collective-permute-start = (bf16[128,768]{1,0:T(8,128)(2,1)S(1)}, bf16[128,768]{1,0:T(8,128)(2,1)S(1)}, u32[]{:S(2)}, u32[]{:S(2)}) collective-permute-start(bf16[128,768]{1,0:T(8,128)(2,1)S(1)} %copy.175), channel_id=1, source_target_pairs={{0,8},{1,9},{2,10},{3,11},{4,12},{5,13},{6,14},{7,15},{8,16},{9,17... | collective-permute-start | bytes 589832 | tf_op jit(solution)/shard_map/ppermute | solution.py:700
  5.1 21.7 %collective-permute-start.1 = (bf16[128,768]{1,0:T(8,128)(2,1)S(1)}, bf16[128,768]{1,0:T(8,128)(2,1)S(1)}, u32[]{:S(2)}, u32[]{:S(2)}) collective-permute-start(bf16[128,768]{1,0:T(8,128)(2,1)S(1)} %copy.175), channel_id=1, source_target_pairs={{0,16},{1,17},{2,18},{3,19},{4,20},{5,21},{6,22},{7,23},{8,24},{9,... | collective-permute-start | bytes 589832 | tf_op jit(solution)/shard_map/ppermute | solution.py:700
  7.7 19.2 %collective-permute-start.2 = (bf16[128,768]{1,0:T(8,128)(2,1)S(1)}, bf16[128,768]{1,0:T(8,128)(2,1)S(1)}, u32[]{:S(2)}, u32[]{:S(2)}) collective-permute-start(bf16[128,768]{1,0:T(8,128)(2,1)S(1)} %copy.175), channel_id=1, source_target_pairs={{0,24},{1,25},{2,26},{3,27},{4,28},{5,29},{6,30},{7,31},{8,0},{9,1... | collective-permute-start | bytes 589832 | tf_op jit(solution)/shard_map/ppermute | solution.py:700
  10.3 15.3 %all-to-all-start = ((s32[8,1,1]{2,1,0:T(1,128)}), s32[8,1,1]{2,1,0:T(1,128)S(1)}, u32[]{:S(2)}, u32[]{:S(2)}) async-start(s32[8,1,1]{2,1,0:T(1,128)} %broadcast_in_dim.19), calls=%async_computation | async-start | bytes 8192 | tf_op jit(solution)/shard_map/all_to_all | solution.py:793
  13.6 36.5 %collective-permute-start.4 = (bf16[512,1024]{1,0:T(8,128)(2,1)}, bf16[512,1024]{1,0:T(8,128)(2,1)S(1)}, u32[]{:S(2)}, u32[]{:S(2)}) collective-permute-start(bf16[512,1024]{1,0:T(8,128)(2,1)} %rest_0_.1), channel_id=1, source_target_pairs={{0,2},{1,3},{2,0},{3,1},{4,6},{5,7},{6,4},{7,5},{8,10},{9,11},{10,... | collective-permute-start | bytes 3145736 | tf_op jit(solution)/shard_map/ppermute | solution.py:754
  29.4 20.6 %collective-permute-start.3 = (bf16[512,768]{1,0:T(8,128)(2,1)S(1)}, bf16[512,768]{1,0:T(8,128)(2,1)}, u32[]{:S(2)}, u32[]{:S(2)}) collective-permute-start(bf16[512,768]{1,0:T(8,128)(2,1)S(1)} %pad_maximum_fusion.rest_4_), channel_id=1, source_target_pairs={{0,4},{4,0},{8,12},{12,8},{16,20},{20,16},{24,28},{28,24},{1,5},{5... | collective-permute-start | bytes 2359304 | tf_op jit(solution)/shard_map/ppermute | solution.py:805
  30.8 19.2 %all-to-all-start.1 = ((bf16[8,64,128]{2,1,0:T(8,128)(2,1)}), bf16[8,64,128]{2,1,0:T(8,128)(2,1)S(1)}, u32[]{:S(2)}, u32[]{:S(2)}) async-start(bf16[8,64,128]{2,1,0:T(8,128)(2,1)} %copy.270), calls=%async_computation.1 | async-start | bytes 262144 | tf_op jit(solution)/shard_map/all_to_all | solution.py:807
  37.3 17.1 %collective-permute-start.7 = (bf16[128,1280]{1,0:T(8,128)(2,1)}, bf16[128,1280]{1,0:T(8,128)(2,1)}, u32[]{:S(2)}, u32[]{:S(2)}) collective-permute-start(bf16[128,1280]{1,0:T(8,128)(2,1)} %pad_maximum_fusion.1), channel_id=1, source_target_pairs={{0,8},{1,9},{2,10},{3,11},{4,12},{5,13},{6,14},{7,15},{8,16},{9,17... | collective-permute-start | bytes 983048 | tf_op jit(solution)/shard_map/ppermute | solution.py:700
  39.3 23.3 %collective-permute-start.8 = (bf16[128,1280]{1,0:T(8,128)(2,1)}, bf16[128,1280]{1,0:T(8,128)(2,1)}, u32[]{:S(2)}, u32[]{:S(2)}) collective-permute-start(bf16[128,1280]{1,0:T(8,128)(2,1)} %pad_maximum_fusion.1), channel_id=1, source_target_pairs={{0,16},{1,17},{2,18},{3,19},{4,20},{5,21},{6,22},{7,23},{8,24},{9,... | collective-permute-start | bytes 983048 | tf_op jit(solution)/shard_map/ppermute | solution.py:700
  41.7 20.9 %collective-permute-start.9 = (bf16[128,1280]{1,0:T(8,128)(2,1)}, bf16[128,1280]{1,0:T(8,128)(2,1)}, u32[]{:S(2)}, u32[]{:S(2)}) collective-permute-start(bf16[128,1280]{1,0:T(8,128)(2,1)} %pad_maximum_fusion.1), channel_id=1, source_target_pairs={{0,24},{1,25},{2,26},{3,27},{4,28},{5,29},{6,30},{7,31},{8,0},{9,1... | collective-permute-start | bytes 983048 | tf_op jit(solution)/shard_map/ppermute | solution.py:700
  50.1 12.5 %collective-permute-start.5 = (bf16[512,1024]{1,0:T(8,128)(2,1)S(1)}, bf16[512,1024]{1,0:T(8,128)(2,1)S(1)}, u32[]{:S(2)}, u32[]{:S(2)}) collective-permute-start(bf16[512,1024]{1,0:T(8,128)(2,1)S(1)} %copy-done.2), channel_id=1, source_target_pairs={{0,1},{1,0},{2,3},{3,2},{4,5},{5,4},{6,7},{7,6},{8,9},{9,8},{10,11... | collective-permute-start | bytes 3145736 | tf_op jit(solution)/shard_map/ppermute | solution.py:754
  50.2 12.4 %collective-permute-start.6 = (bf16[512,1024]{1,0:T(8,128)(2,1)S(1)}, bf16[512,1024]{1,0:T(8,128)(2,1)}, u32[]{:S(2)}, u32[]{:S(2)}) collective-permute-start(bf16[512,1024]{1,0:T(8,128)(2,1)S(1)} %collective-permute-done.4.rest_1_), channel_id=1, source_target_pairs={{0,1},{1,0},{2,3},{3,2},{4,5},{5,4},{6,7},{7,6},{8,9},{9,8},{10,11... | collective-permute-start | bytes 3145736 | tf_op jit(solution)/shard_map/ppermute | solution.py:754
  69.8 59.9 %collective-permute-start.10 = (bf16[512,1280]{1,0:T(8,128)(2,1)}, bf16[512,1280]{1,0:T(8,128)(2,1)}, u32[]{:S(2)}, u32[]{:S(2)}) collective-permute-start(bf16[512,1280]{1,0:T(8,128)(2,1)} %constant_dynamic-update-slice_fusion.6.rest_8_), channel_id=1, source_target_pairs={{0,4},{1,3},{2,6},{3,1},{4,0},{5,7},{6,2},{7,5},{8,12},{9,11},{10,... | collective-permute-start | bytes 3932168 | tf_op jit(solution)/shard_map/ppermute | solution.py:700
  71.3 58.4 %collective-permute-start.11 = (bf16[512,1280]{1,0:T(8,128)(2,1)}, bf16[512,1280]{1,0:T(8,128)(2,1)}, u32[]{:S(2)}, u32[]{:S(2)}) collective-permute-start(bf16[512,1280]{1,0:T(8,128)(2,1)} %constant_dynamic-update-slice_fusion.6.rest_8_), channel_id=1, source_target_pairs={{0,2},{1,5},{2,0},{3,7},{4,6},{5,1},{6,4},{7,3},{8,10},{9,13},{10,... | collective-permute-start | bytes 3932168 | tf_op jit(solution)/shard_map/ppermute | solution.py:700
  75.0 54.2 %all-to-all-start.2 = ((bf16[32,2,3328]{2,1,0:T(2,128)(2,1)}), bf16[32,2,3328]{2,1,0:T(2,128)(2,1)S(1)}, u32[]{:S(2)}, u32[]{:S(2)}) async-start(bf16[32,2,3328]{2,1,0:T(2,128)(2,1)} %reshape.299), calls=%async_computation.2 | async-start | bytes 851968 | tf_op jit(solution)/shard_map/all_to_all | solution.py:849
  83.6 46.0 %collective-permute-start.12 = (bf16[128,1024]{1,0:T(8,128)(2,1)S(1)}, bf16[128,1024]{1,0:T(8,128)(2,1)S(1)}, u32[]{:S(2)}, u32[]{:S(2)}) collective-permute-start(bf16[128,1024]{1,0:T(8,128)(2,1)S(1)} %bitcast.179), channel_id=1, source_target_pairs={{0,8},{1,9},{2,10},{3,11},{4,12},{5,13},{6,14},{7,15},{8,16},{9,17... | collective-permute-start | bytes 786440 | tf_op jit(solution)/shard_map/ppermute | solution.py:700
  85.5 44.2 %collective-permute-start.13 = (bf16[128,1024]{1,0:T(8,128)(2,1)S(1)}, bf16[128,1024]{1,0:T(8,128)(2,1)S(1)}, u32[]{:S(2)}, u32[]{:S(2)}) collective-permute-start(bf16[128,1024]{1,0:T(8,128)(2,1)S(1)} %bitcast.180), channel_id=1, source_target_pairs={{0,16},{1,17},{2,18},{3,19},{4,20},{5,21},{6,22},{7,23},{8,24},{9,... | collective-permute-start | bytes 786440 | tf_op jit(solution)/shard_map/ppermute | solution.py:700
  87.9 41.8 %collective-permute-start.14 = (bf16[128,1024]{1,0:T(8,128)(2,1)S(1)}, bf16[128,1024]{1,0:T(8,128)(2,1)S(1)}, u32[]{:S(2)}, u32[]{:S(2)}) collective-permute-start(bf16[128,1024]{1,0:T(8,128)(2,1)S(1)} %bitcast.181), channel_id=1, source_target_pairs={{0,24},{1,25},{2,26},{3,27},{4,28},{5,29},{6,30},{7,31},{8,0},{9,1... | collective-permute-start | bytes 786440 | tf_op jit(solution)/shard_map/ppermute | solution.py:700
  130.6 29.1 %collective-permute-start.15 = (bf16[512,1280]{1,0:T(8,128)(2,1)}, bf16[512,1280]{1,0:T(8,128)(2,1)S(1)}, u32[]{:S(2)}, u32[]{:S(2)}) collective-permute-start(bf16[512,1280]{1,0:T(8,128)(2,1)} %collective-permute-done.10.rest_9_), channel_id=1, source_target_pairs={{0,2},{1,5},{2,0},{3,7},{4,6},{5,1},{6,4},{7,3},{8,10},{9,13},{10,... | collective-permute-start | bytes 3932168 | tf_op jit(solution)/shard_map/ppermute | solution.py:700
  134.0 25.6 %copy-start.9 = (bf16[512,1024]{1,0:T(8,128)(2,1)}, bf16[512,1024]{1,0:T(8,128)(2,1)S(1)}, u32[]{:S(2)}) copy-start(bf16[512,1024]{1,0:T(8,128)(2,1)S(1)} %constant_dynamic-update-slice_fusion.10.rest_16_) | copy-start | bytes 3145732
  134.1 38.8 %collective-permute-start.26 = (bf16[512,1024]{1,0:T(8,128)(2,1)S(1)}, bf16[512,1024]{1,0:T(8,128)(2,1)}, u32[]{:S(2)}, u32[]{:S(2)}) collective-permute-start(bf16[512,1024]{1,0:T(8,128)(2,1)S(1)} %constant_dynamic-update-slice_fusion.10.rest_16_), channel_id=1, source_target_pairs={{0,4},{1,3},{2,6},{3,1},{4,0},{5,7},{6,2},{7,5},{8,12},{9,11},{10,... | collective-permute-start | bytes 3145736 | tf_op jit(solution)/shard_map/ppermute | solution.py:700
  135.6 37.3 %collective-permute-start.27 = (bf16[512,1024]{1,0:T(8,128)(2,1)S(1)}, bf16[512,1024]{1,0:T(8,128)(2,1)}, u32[]{:S(2)}, u32[]{:S(2)}) collective-permute-start(bf16[512,1024]{1,0:T(8,128)(2,1)S(1)} %constant_dynamic-update-slice_fusion.10.rest_16_), channel_id=1, source_target_pairs={{0,2},{1,5},{2,0},{3,7},{4,6},{5,1},{6,4},{7,3},{8,10},{9,13},{10,... | collective-permute-start | bytes 3145736 | tf_op jit(solution)/shard_map/ppermute | solution.py:700
  136.1 61.6 %collective-permute-start.22 = (bf16[512,1280]{1,0:T(8,128)(2,1)}, bf16[512,1280]{1,0:T(8,128)(2,1)}, u32[]{:S(2)}, u32[]{:S(2)}) collective-permute-start(bf16[512,1280]{1,0:T(8,128)(2,1)} %constant_dynamic-update-slice_fusion.6.rest_8_), channel_id=1, source_target_pairs={{0,1},{1,0},{2,3},{3,2},{4,5},{5,4},{6,7},{7,6},{8,9},{9,8},{10,11... | collective-permute-start | bytes 3932168 | tf_op jit(solution)/shard_map/ppermute | solution.py:700
  136.1 68.1 %collective-permute-start.23 = (bf16[512,1280]{1,0:T(8,128)(2,1)}, bf16[512,1280]{1,0:T(8,128)(2,1)}, u32[]{:S(2)}, u32[]{:S(2)}) collective-permute-start(bf16[512,1280]{1,0:T(8,128)(2,1)} %collective-permute-done.10.rest_9_), channel_id=1, source_target_pairs={{0,1},{1,0},{2,3},{3,2},{4,5},{5,4},{6,7},{7,6},{8,9},{9,8},{10,11... | collective-permute-start | bytes 3932168 | tf_op jit(solution)/shard_map/ppermute | solution.py:700
  159.6 44.1 %copy-start.10 = (bf16[512,1280]{1,0:T(8,128)(2,1)}, bf16[512,1280]{1,0:T(8,128)(2,1)S(1)}, u32[]{:S(2)}) copy-start(bf16[512,1280]{1,0:T(8,128)(2,1)S(1)} %collective-permute-done.15.rest_11_) | copy-start | bytes 3932164
  159.6 44.1 %collective-permute-start.29 = (bf16[512,1024]{1,0:T(8,128)(2,1)S(1)}, bf16[512,1024]{1,0:T(8,128)(2,1)}, u32[]{:S(2)}, u32[]{:S(2)}) collective-permute-start(bf16[512,1024]{1,0:T(8,128)(2,1)S(1)} %constant_dynamic-update-slice_fusion.10.rest_16_), channel_id=1, source_target_pairs={{0,1},{1,0},{2,3},{3,2},{4,5},{5,4},{6,7},{7,6},{8,9},{9,8},{10,11... | collective-permute-start | bytes 3145736 | tf_op jit(solution)/shard_map/ppermute | solution.py:700
  159.6 31.1 %copy-start.49 = (bf16[512,128]{1,0:T(8,128)(2,1)S(1)}, bf16[512,128]{1,0:T(8,128)(2,1)}, u32[]{:S(2)}) copy-start(bf16[512,128]{1,0:T(8,128)(2,1)} %get-tuple-element.179) | copy-start | bytes 393220
  159.6 32.5 %copy-start.48 = (bf16[512,128]{1,0:T(8,128)(2,1)S(1)}, bf16[512,128]{1,0:T(8,128)(2,1)}, u32[]{:S(2)}) copy-start(bf16[512,128]{1,0:T(8,128)(2,1)} %get-tuple-element.187) | copy-start | bytes 393220
  172.9 31.4 %collective-permute-start.28 = (bf16[512,1024]{1,0:T(8,128)(2,1)}, bf16[512,1024]{1,0:T(8,128)(2,1)S(1)}, u32[]{:S(2)}, u32[]{:S(2)}) collective-permute-start(bf16[512,1024]{1,0:T(8,128)(2,1)} %collective-permute-done.26.rest_17_), channel_id=1, source_target_pairs={{0,2},{1,5},{2,0},{3,7},{4,6},{5,1},{6,4},{7,3},{8,10},{9,13},{10,... | collective-permute-start | bytes 3145736 | tf_op jit(solution)/shard_map/ppermute | solution.py:700
  174.5 16.3 %collective-permute-start.16 = (bf16[512,128]{1,0:T(8,128)(2,1)S(1)}, bf16[512,128]{1,0:T(8,128)(2,1)S(1)}, u32[]{:S(2)}, u32[]{:S(2)}) collective-permute-start(bf16[512,128]{1,0:T(8,128)(2,1)S(1)} %copy-done.50), channel_id=1, source_target_pairs={{0,2},{1,3},{2,0},{3,1},{4,6},{5,7},{6,4},{7,5},{8,10},{9,11},{10,... | collective-permute-start | bytes 393224 | tf_op jit(solution)/shard_map/ppermute | solution.py:754
  190.8 26.1 %copy-start.32 = (bf16[512,128]{1,0:T(8,128)(2,1)}, bf16[512,128]{1,0:T(8,128)(2,1)S(1)}, u32[]{:S(2)}) copy-start(bf16[512,128]{1,0:T(8,128)(2,1)S(1)} %collective-permute-done.16.rest_2_) | copy-start | bytes 393220
  190.8 1.3 collective-permute-start.18
  192.1 5.5 %collective-permute-start.20 = (bf16[512,128]{1,0:T(8,128)(2,1)S(1)}, bf16[512,128]{1,0:T(8,128)(2,1)S(1)}, u32[]{:S(2)}, u32[]{:S(2)}) collective-permute-start(bf16[512,128]{1,0:T(8,128)(2,1)S(1)} %copy-done.48), channel_id=1, source_target_pairs={{0,3},{1,2},{2,1},{3,0},{4,7},{5,6},{6,5},{7,4},{8,11},{9,10},{10,... | collective-permute-start | bytes 393224 | tf_op jit(solution)/shard_map/ppermute | solution.py:754
  197.6 7.2 %collective-permute-start.24 = (bf16[512,1280]{1,0:T(8,128)(2,1)}, bf16[512,1280]{1,0:T(8,128)(2,1)S(1)}, u32[]{:S(2)}, u32[]{:S(2)}) collective-permute-start(bf16[512,1280]{1,0:T(8,128)(2,1)} %collective-permute-done.11.rest_10_), channel_id=1, source_target_pairs={{0,1},{1,0},{2,3},{3,2},{4,5},{5,4},{6,7},{7,6},{8,9},{9,8},{10,11... | collective-permute-start | bytes 3932168 | tf_op jit(solution)/shard_map/ppermute | solution.py:700
  197.8 6.0 %collective-permute-start.17 = (bf16[512,128]{1,0:T(8,128)(2,1)}, bf16[512,128]{1,0:T(8,128)(2,1)S(1)}, u32[]{:S(2)}, u32[]{:S(2)}) collective-permute-start(bf16[512,128]{1,0:T(8,128)(2,1)} %get-tuple-element.178), channel_id=1, source_target_pairs={{0,2},{1,3},{2,0},{3,1},{4,6},{5,7},{6,4},{7,5},{8,10},{9,11},{10,... | collective-permute-start | bytes 393224 | tf_op jit(solution)/shard_map/ppermute | solution.py:754
  203.7 10.7 %collective-permute-start.25 = (bf16[512,1280]{1,0:T(8,128)(2,1)S(1)}, bf16[512,1280]{1,0:T(8,128)(2,1)S(1)}, u32[]{:S(2)}, u32[]{:S(2)}) collective-permute-start(bf16[512,1280]{1,0:T(8,128)(2,1)S(1)} %collective-permute-done.15.rest_11_), channel_id=1, source_target_pairs={{0,1},{1,0},{2,3},{3,2},{4,5},{5,4},{6,7},{7,6},{8,9},{9,8},{10,11... | collective-permute-start | bytes 3932168 | tf_op jit(solution)/shard_map/ppermute | solution.py:700
  203.8 10.7 %collective-permute-start.30 = (bf16[512,1024]{1,0:T(8,128)(2,1)}, bf16[512,1024]{1,0:T(8,128)(2,1)S(1)}, u32[]{:S(2)}, u32[]{:S(2)}) collective-permute-start(bf16[512,1024]{1,0:T(8,128)(2,1)} %collective-permute-done.26.rest_17_), channel_id=1, source_target_pairs={{0,1},{1,0},{2,3},{3,2},{4,5},{5,4},{6,7},{7,6},{8,9},{9,8},{10,11... | collective-permute-start | bytes 3145736 | tf_op jit(solution)/shard_map/ppermute | solution.py:700
  204.3 10.2 %collective-permute-start.31 = (bf16[512,1024]{1,0:T(8,128)(2,1)}, bf16[512,1024]{1,0:T(8,128)(2,1)S(1)}, u32[]{:S(2)}, u32[]{:S(2)}) collective-permute-start(bf16[512,1024]{1,0:T(8,128)(2,1)} %collective-permute-done.27.rest_18_), channel_id=1, source_target_pairs={{0,1},{1,0},{2,3},{3,2},{4,5},{5,4},{6,7},{7,6},{8,9},{9,8},{10,11... | collective-permute-start | bytes 3145736 | tf_op jit(solution)/shard_map/ppermute | solution.py:700
  204.3 11.5 %collective-permute-start.32 = (bf16[512,1024]{1,0:T(8,128)(2,1)S(1)}, bf16[512,1024]{1,0:T(8,128)(2,1)S(1)}, u32[]{:S(2)}, u32[]{:S(2)}) collective-permute-start(bf16[512,1024]{1,0:T(8,128)(2,1)S(1)} %collective-permute-done.28.rest_19_), channel_id=1, source_target_pairs={{0,1},{1,0},{2,3},{3,2},{4,5},{5,4},{6,7},{7,6},{8,9},{9,8},{10,11... | collective-permute-start | bytes 3145736 | tf_op jit(solution)/shard_map/ppermute | solution.py:700
  204.8 4.0 collective-permute-start.19
  208.7 5.7 %collective-permute-start.21 = (bf16[512,128]{1,0:T(8,128)(2,1)}, bf16[512,128]{1,0:T(8,128)(2,1)S(1)}, u32[]{:S(2)}, u32[]{:S(2)}) collective-permute-start(bf16[512,128]{1,0:T(8,128)(2,1)} %get-tuple-element.188), channel_id=1, source_target_pairs={{0,3},{1,2},{2,1},{3,0},{4,7},{5,6},{6,5},{7,4},{8,11},{9,10},{10,... | collective-permute-start | bytes 393224 | tf_op jit(solution)/shard_map/ppermute | solution.py:754
  269.8 43.8 %all-to-all-start.3 = ((bf16[32,2,3072]{2,1,0:T(2,128)(2,1)}), bf16[32,2,3072]{2,1,0:T(2,128)(2,1)S(1)}, u32[]{:S(2)}, u32[]{:S(2)}) async-start(bf16[32,2,3072]{2,1,0:T(2,128)(2,1)} %reshape.301), calls=%async_computation.3 | async-start | bytes 786432 | tf_op jit(solution)/shard_map/all_to_all | solution.py:952
  272.7 13.1 %collective-permute-start.33 = (bf16[512,256]{1,0:T(8,128)(2,1)S(1)}, bf16[512,256]{1,0:T(8,128)(2,1)S(1)}, u32[]{:S(2)}, u32[]{:S(2)}) collective-permute-start(bf16[512,256]{1,0:T(8,128)(2,1)S(1)} %copy-done.47), channel_id=1, source_target_pairs={{0,2},{1,3},{2,0},{3,1},{4,6},{5,7},{6,4},{7,5},{8,10},{9,11},{10,... | collective-permute-start | bytes 786440 | tf_op jit(solution)/shard_map/ppermute | solution.py:754
  274.5 11.3 %collective-permute-start.34 = (bf16[512,256]{1,0:T(8,128)(2,1)S(1)}, bf16[512,256]{1,0:T(8,128)(2,1)S(1)}, u32[]{:S(2)}, u32[]{:S(2)}) collective-permute-start(bf16[512,256]{1,0:T(8,128)(2,1)S(1)} %copy-done.46), channel_id=1, source_target_pairs={{0,1},{1,0},{2,3},{3,2},{4,5},{5,4},{6,7},{7,6},{8,9},{9,8},{10,11... | collective-permute-start | bytes 786440 | tf_op jit(solution)/shard_map/ppermute | solution.py:754
  274.5 15.7 %collective-permute-start.35 = (bf16[512,256]{1,0:T(8,128)(2,1)S(1)}, bf16[512,256]{1,0:T(8,128)(2,1)S(1)}, u32[]{:S(2)}, u32[]{:S(2)}) collective-permute-start(bf16[512,256]{1,0:T(8,128)(2,1)S(1)} %copy-done.45), channel_id=1, source_target_pairs={{0,3},{1,2},{2,1},{3,0},{4,7},{5,6},{6,5},{7,4},{8,11},{9,10},{10,... | collective-permute-start | bytes 786440 | tf_op jit(solution)/shard_map/ppermute | solution.py:754
  344.4 17.9 %collective-permute-start.36 = (bf16[1024,1024]{1,0:T(8,128)(2,1)}, bf16[1024,1024]{1,0:T(8,128)(2,1)S(1)}, u32[]{:S(2)}, u32[]{:S(2)}) collective-permute-start(bf16[1024,1024]{1,0:T(8,128)(2,1)} %get-tuple-element.234), channel_id=1, source_target_pairs={{0,1},{1,0},{2,3},{3,2},{4,5},{5,4},{6,7},{7,6},{8,9},{9,8},{10,11... | collective-permute-start | bytes 6291464 | tf_op jit(solution)/shard_map/ppermute | solution.py:754
  357.2 14.7 %all-to-all-start.4 = ((bf16[32,2,1536]{2,1,0:T(2,128)(2,1)}), bf16[32,2,1536]{2,1,0:T(2,128)(2,1)S(1)}, u32[]{:S(2)}, u32[]{:S(2)}) async-start(bf16[32,2,1536]{2,1,0:T(2,128)(2,1)} %reshape.303), calls=%async_computation.4 | async-start | bytes 393216 | tf_op jit(solution)/shard_map/all_to_all | solution.py:952
  366.0 26.1 %collective-permute-start.37 = (bf16[512,1024]{1,0:T(8,128)(2,1)}, bf16[512,1024]{1,0:T(8,128)(2,1)}, u32[]{:S(2)}, u32[]{:S(2)}) collective-permute-start(bf16[512,1024]{1,0:T(8,128)(2,1)} %add_convert_fusion), channel_id=1, source_target_pairs={{0,2},{1,3},{2,0},{3,1},{4,6},{5,7},{6,4},{7,5},{8,10},{9,11},{10,... | collective-permute-start | bytes 3145736 | tf_op jit(solution)/shard_map/ppermute | solution.py:754
  (46 other events, 418.3 us)
